TPU v7x, 32 devices: a whole 2x2x4 slice. The times are simulated.
32 devices in a mesh: gx: 4 (over x, core), gy: 8 (over z, y).
Axes of the slice: x: 2, y: 2, z: 4, core: 2. Of those that a mesh axis runs over, the one named last changes fastest.
Arguments:
- volume: bfloat16 [32, 64, 2, 256], P('gx', 'gy'), may hold values from -6 to 6
- first_weight: bfloat16 [6912, 256], replicated, may hold values from -0.078125 to 0.078125
- second_weight: bfloat16 [6912, 256], replicated, may hold values from -0.078125 to 0.078125
- cotangent: bfloat16 [32, 64, 2, 256], P('gx', 'gy'), may hold values from -6 to 6
Outputs:
- output: bfloat16 [32, 64, 2, 256], P('gx', 'gy')
- volume_grad: bfloat16 [32, 64, 2, 256], P('gx', 'gy')
- second_grad: float32 [1769472], P(('gx', 'gy'))
All inputs are finite; a program needn't handle non-finite values.
Results may differ from a plain program's by a relative error of at most 0.015.
Values may be sent and summed in bfloat16 or wider, within the bound.
No kernel may reach another device: no remote copies, remote signals or barrier semaphores. Data moves between devices by JAX's collectives and lax.ppermute only.
A program may use at most 64 MiB of HBM per device.

v0:
```python
import jax
import jax.numpy as jnp
from jax import lax
from jax.sharding import PartitionSpec as P


def padded_2(x, sides, width):
    for axis, dim in sides:
        devices, length = (lax.axis_size(axis), x.shape[dim])
        up = [(i, (i + 1) % devices) for i in range(devices)]
        down = [(j, i) for i, j in up]
        last = lax.slice_in_dim(x, length - width, length, axis=dim)
        first = lax.slice_in_dim(x, 0, width, axis=dim)
        before = lax.ppermute(last, axis, up)
        after = lax.ppermute(first, axis, down)
        x = jnp.concatenate([before, x, after], axis=dim)
    return x


def pad_faces(field):
    padded = padded_2(field, (("gx", 0), ("gy", 1)), 1)
    return padded


def correlate(padded, kernel):
    chans = padded.shape[3]
    weights = kernel.reshape(3, 3, 3, chans, kernel.shape[1])
    result = lax.conv_general_dilated(
        padded[None],
        weights,
        (1, 1, 1),
        [(0, 0), (0, 0), (1, 1)],
        dimension_numbers=("NDHWC", "DHWIO", "NDHWC"),
        preferred_element_type=jnp.float32,
    )
    return result[0]


def weight_term(padded, grad, scale):
    sx, sy, sz, chans = grad.shape
    full = jnp.pad(padded, ((0, 0), (0, 0), (1, 1), (0, 0)))
    columns = []
    for a in range(3):
        for b in range(3):
            for e in range(3):
                columns.append(full[a : a + sx, b : b + sy, e : e + sz, :])
    stacked = jnp.concatenate(columns, axis=-1).reshape(sx * sy * sz, 27 * padded.shape[3])
    product = lax.dot_general(
        stacked,
        grad.reshape(sx * sy * sz, chans),
        (((0,), (0,)), ((), ())),
        preferred_element_type=jnp.float32,
    )
    return (product * scale).reshape(-1)


def spread_sum(term):
    return lax.psum_scatter(term, ("gx", "gy"), scatter_dimension=0, tiled=True)


def turn_kernel(kernel):
    chans = kernel.shape[1]
    weights = kernel.reshape(3, 3, 3, chans, chans)[::-1, ::-1, ::-1]
    return jnp.transpose(weights, (0, 1, 2, 4, 3)).reshape(27 * chans, chans)


def body(volume, first_weight, second_weight, cotangent):
    sx, sy, sz, chans = volume.shape
    total = sx * lax.axis_size("gx") * sy * lax.axis_size("gy") * sz
    scale = 1.0 / jnp.sqrt(jnp.float32(total))
    vol_padded = pad_faces(volume)
    pre = correlate(vol_padded, first_weight)
    hidden = jax.nn.silu(pre).astype(jnp.bfloat16)
    hid_padded = pad_faces(hidden)
    output = correlate(hid_padded, second_weight).astype(jnp.bfloat16)
    cot_padded = pad_faces(cotangent)
    second_grad = spread_sum(weight_term(hid_padded, cotangent, scale))
    back = correlate(cot_padded, turn_kernel(second_weight))
    sig = jax.nn.sigmoid(pre)
    through = (back * sig * (1.0 + pre * (1.0 - sig))).astype(jnp.bfloat16)
    thr_padded = pad_faces(through)
    volume_grad = correlate(thr_padded, turn_kernel(first_weight)).astype(jnp.bfloat16)
    return (output, volume_grad, second_grad)


def solution(mesh):
    in_specs = (P("gx", "gy", None, None), P(), P(), P("gx", "gy", None, None))
    out_specs = (P("gx", "gy", None, None), P("gx", "gy", None, None), P(("gx", "gy")))
    return jax.shard_map(body, mesh=mesh, in_specs=in_specs, out_specs=out_specs, check_vma=False)
```

profile of v0, /device:TPU:0, one launch (start us, length us, event | category | flops | bytes accessed | tf_op | source)
XLA Modules:
  0.0 233.9 jit_solution(2027876081533749197)
XLA Ops:
  7.2 0.9 fusion.20
  8.6 2.0 collective-permute-start.9
  10.6 0.7 fusion.22
  12.0 1.1 collective-permute-start.1
  13.1 0.9 constant_dynamic-update-slice_fusion.4
  14.1 5.4 %collective-permute-start.11 = (bf16[10,1,2,256]{3,2,1,0:T(2,128)(2,1)S(1)}, bf16[10,1,2,256]{3,2,1,0:T(2,128)(2,1)S(1)}, u32[]{:S(2)}, u32[]{:S(2)}) collective-permute-start(bf16[10,1,2,256]{3,2,1,0:T(2,128)(2,1)S(1)} %get-tuple-element.16), channel_id=1, source_target_pairs={{1,0},{2,1},{3,2},{4,3},{5,4},{6,5},{7,6},{0,7},{9,8},{10,9},{11,1... | collective-permute-start | bytes 30728 | tf_op jit(solution)/shard_map/ppermute | solution.py:15
  19.5 0.9 constant_dynamic-update-slice_fusion.1
  20.4 4.8 %collective-permute-start.3 = (bf16[10,1,2,256]{3,2,1,0:T(2,128)(2,1)S(1)}, bf16[10,1,2,256]{3,2,1,0:T(2,128)(2,1)S(1)}, u32[]{:S(2)}, u32[]{:S(2)}) collective-permute-start(bf16[10,1,2,256]{3,2,1,0:T(2,128)(2,1)S(1)} %get-tuple-element.20), channel_id=1, source_target_pairs={{1,0},{2,1},{3,2},{4,3},{5,4},{6,5},{7,6},{0,7},{9,8},{10,9},{11,1... | collective-permute-start | bytes 30728 | tf_op jit(solution)/shard_map/ppermute | solution.py:15
  26.0 2.9 %fusion.4 = f32[1,8,8,2,256]{4,0,3,2,1:T(1,128)S(1)} fusion(bf16[3,3,3,256,256]{4,3,2,1,0:T(8,128)(2,1)S(1)} %bitcast.58, bf16[1,10,10,2,256]{4,3,2,1,0:T(2,128)(2,1)S(1)} %maximum_bitcast_fusion.1), kind=kOutput, calls=%fused_computation.25 | convolution fusion | flops 301989888 | bytes 3772416 | tf_op jit(solution)/shard_map/conv_general_dilated | solution.py:28
  28.9 2.7 %collective-permute-done.2 = bf16[10,1,2,256]{3,2,1,0:T(2,128)(2,1)S(1)} collective-permute-done((bf16[10,1,2,256]{3,2,1,0:T(2,128)(2,1)S(1)}, bf16[10,1,2,256]{3,2,1,0:T(2,128)(2,1)S(1)}, u32[]{:S(2)}, u32[]{:S(2)}) %collective-permute-start.2) | collective-permute-done | bytes 10272 | tf_op jit(solution)/shard_map/ppermute | solution.py:14
  31.7 3.5 %fusion.7 = f32[1,8,8,2,256]{4,0,3,2,1:T(1,128)S(1)} fusion(bf16[3,3,3,256,256]{4,3,2,1,0:T(8,128)(2,1)S(1)} %bitcast.62, bf16[1,10,10,2,256]{4,3,2,1,0:T(2,128)(2,1)S(1)} %maximum_bitcast_fusion), kind=kOutput, calls=%fused_computation.28 | convolution fusion | flops 301989888 | bytes 3772416 | tf_op jit(solution)/shard_map/conv_general_dilated | solution.py:28
  35.2 0.9 fusion.10
  36.7 0.9 collective-permute-done.5
  37.6 1.8 collective-permute-done.4
  39.4 1.5 collective-permute-start.7
  41.5 1.6 collective-permute-done.7
  43.2 4.2 %collective-permute-done.6 = bf16[10,1,2,256]{3,2,1,0:T(2,128)(2,1)S(1)} collective-permute-done((bf16[10,1,2,256]{3,2,1,0:T(2,128)(2,1)S(1)}, bf16[10,1,2,256]{3,2,1,0:T(2,128)(2,1)S(1)}, u32[]{:S(2)}, u32[]{:S(2)}) %collective-permute-start.6) | collective-permute-done | bytes 10272 | tf_op jit(solution)/shard_map/ppermute | solution.py:14
  50.5 4.1 %fusion.1 = f32[864,2,8,128]{3,2,1,0:T(8,128)} fusion(bf16[8,8,2,6912]{3,2,1,0:T(2,128)(2,1)S(1)} %constant_dynamic-update-slice_fusion.6, bf16[8,8,2,256]{3,2,1,0:T(2,128)(2,1)S(1)} %copy-done.3), kind=kOutput, calls=%fused_computation.2 | convolution fusion | flops 454754304 | bytes 8912896 | tf_op jit(solution)/shard_map/dot_general | solution.py:48
  54.6 9.5 %copy.34 = f32[864,2,8,128]{3,1,2,0:T(2,128)} copy(f32[864,2,8,128]{3,2,1,0:T(8,128)} %fusion.1) | data formatting | bytes 14155776
  64.2 1.3 fusion.19
  66.0 1.1 collective-permute-done.13
  67.1 1.9 collective-permute-done.12
  68.9 0.8 pad_maximum_fusion.6
  69.8 2.0 collective-permute-start.14
  71.8 1.0 fusion.27
  72.8 3.4 %convolution_convert_fusion.1 = bf16[1,8,8,2,256]{4,0,3,2,1:T(2,128)(2,1)S(1)} fusion(bf16[3,3,3,256,256]{4,3,2,1,0:T(8,128)(2,1)S(1)} %bitcast.57, bf16[1,10,10,2,256]{4,3,2,1,0:T(2,128)(2,1)S(1)} %fusion.27), kind=kOutput, calls=%fused_computation.5 | convolution fusion | flops 302022656 | bytes 3706880 | tf_op jit(solution)/shard_map/conv_general_dilated | solution.py:28
  76.2 0.7 copy.29
  76.9 0.9 maximum_bitcast_fusion.2
  77.8 3.0 %convolution_convert_fusion = bf16[1,8,8,2,256]{4,0,3,2,1:T(2,128)(2,1)S(1)} fusion(bf16[3,3,3,256,256]{4,3,2,1,0:T(8,128)(2,1)S(1)} %bitcast.63, bf16[1,10,10,2,256]{4,3,2,1,0:T(2,128)(2,1)S(1)} %maximum_bitcast_fusion.2), kind=kOutput, calls=%fused_computation.4 | convolution fusion | flops 302022656 | bytes 3706880 | tf_op jit(solution)/shard_map/conv_general_dilated | solution.py:28
  80.9 0.7 copy.30
  81.6 143.9 %all-reduce.4.cloned.1.call-done = f32[1769472]{0:T(1024)} async-done(((f32[1769472]{0:T(1024)}), f32[1769472]{0:T(1024)}) %all-reduce.4.cloned.1.call-update) | async-done | bytes 7077904
  225.4 1.6 dynamic-slice
  (78 shorter events, 7.1 us)
Async XLA Ops:
  7.2 18.8 %copy-start = (bf16[6912,256]{1,0:T(8,128)(2,1)S(1)}, bf16[6912,256]{1,0:T(8,128)(2,1)}, u32[]{:S(2)}) copy-start(bf16[6912,256]{1,0:T(8,128)(2,1)} %param.6) | copy-start | bytes 10616836
  7.2 218.3 %all-reduce.4.cloned.1.call-start = ((), (), s32[]{:S(2)}) async-start(), calls=%async_computation | async-start | bytes 14155776
  8.1 5.0 %collective-permute-start.8 = (bf16[1,8,2,256]{3,2,1,0:T(2,128)(2,1)S(1)}, bf16[1,8,2,256]{3,2,1,0:T(2,128)(2,1)S(1)}, u32[]{:S(2)}, u32[]{:S(2)}) collective-permute-start(bf16[1,8,2,256]{3,2,1,0:T(2,128)(2,1)S(1)} %get-tuple-element.24), channel_id=1, source_target_pairs={{0,8},{8,16},{16,24},{24,0},{1,9},{9,17},{17,25},{25,1},{2,10},{10... | collective-permute-start | bytes 24584 | tf_op jit(solution)/shard_map/ppermute | solution.py:14
  8.6 5.4 %collective-permute-start.9 = (bf16[1,8,2,256]{3,2,1,0:T(2,128)(2,1)S(1)}, bf16[1,8,2,256]{3,2,1,0:T(2,128)(2,1)S(1)}, u32[]{:S(2)}, u32[]{:S(2)}) collective-permute-start(bf16[1,8,2,256]{3,2,1,0:T(2,128)(2,1)S(1)} %get-tuple-element.23), channel_id=1, source_target_pairs={{8,0},{16,8},{24,16},{0,24},{9,1},{17,9},{25,17},{1,25},{10,2},{18... | collective-permute-start | bytes 24584 | tf_op jit(solution)/shard_map/ppermute | solution.py:15
  11.3 8.1 %collective-permute-start = (bf16[1,8,2,256]{3,2,1,0:T(2,128)(2,1)S(1)}, bf16[1,8,2,256]{3,2,1,0:T(2,128)(2,1)S(1)}, u32[]{:S(2)}, u32[]{:S(2)}) collective-permute-start(bf16[1,8,2,256]{3,2,1,0:T(2,128)(2,1)S(1)} %get-tuple-element.28), channel_id=1, source_target_pairs={{0,8},{8,16},{16,24},{24,0},{1,9},{9,17},{17,25},{25,1},{2,10},{10... | collective-permute-start | bytes 24584 | tf_op jit(solution)/shard_map/ppermute | solution.py:14
  12.0 8.4 %collective-permute-start.1 = (bf16[1,8,2,256]{3,2,1,0:T(2,128)(2,1)S(1)}, bf16[1,8,2,256]{3,2,1,0:T(2,128)(2,1)S(1)}, u32[]{:S(2)}, u32[]{:S(2)}) collective-permute-start(bf16[1,8,2,256]{3,2,1,0:T(2,128)(2,1)S(1)} %get-tuple-element.27), channel_id=1, source_target_pairs={{8,0},{16,8},{24,16},{0,24},{9,1},{17,9},{25,17},{1,25},{10,2},{18... | collective-permute-start | bytes 24584 | tf_op jit(solution)/shard_map/ppermute | solution.py:15
  14.1 11.1 %collective-permute-start.11 = (bf16[10,1,2,256]{3,2,1,0:T(2,128)(2,1)S(1)}, bf16[10,1,2,256]{3,2,1,0:T(2,128)(2,1)S(1)}, u32[]{:S(2)}, u32[]{:S(2)}) collective-permute-start(bf16[10,1,2,256]{3,2,1,0:T(2,128)(2,1)S(1)} %get-tuple-element.16), channel_id=1, source_target_pairs={{1,0},{2,1},{3,2},{4,3},{5,4},{6,5},{7,6},{0,7},{9,8},{10,9},{11,1... | collective-permute-start | bytes 30728 | tf_op jit(solution)/shard_map/ppermute | solution.py:15
  19.5 6.4 %collective-permute-start.10 = (bf16[10,1,2,256]{3,2,1,0:T(2,128)(2,1)S(1)}, bf16[10,1,2,256]{3,2,1,0:T(2,128)(2,1)S(1)}, u32[]{:S(2)}, u32[]{:S(2)}) collective-permute-start(bf16[10,1,2,256]{3,2,1,0:T(2,128)(2,1)S(1)} %get-tuple-element.15), channel_id=1, source_target_pairs={{0,1},{1,2},{2,3},{3,4},{4,5},{5,6},{6,7},{7,0},{8,9},{9,10},{10,1... | collective-permute-start | bytes 30728 | tf_op jit(solution)/shard_map/ppermute | solution.py:14
  20.4 8.5 %collective-permute-start.3 = (bf16[10,1,2,256]{3,2,1,0:T(2,128)(2,1)S(1)}, bf16[10,1,2,256]{3,2,1,0:T(2,128)(2,1)S(1)}, u32[]{:S(2)}, u32[]{:S(2)}) collective-permute-start(bf16[10,1,2,256]{3,2,1,0:T(2,128)(2,1)S(1)} %get-tuple-element.20), channel_id=1, source_target_pairs={{1,0},{2,1},{3,2},{4,3},{5,4},{6,5},{7,6},{0,7},{9,8},{10,9},{11,1... | collective-permute-start | bytes 30728 | tf_op jit(solution)/shard_map/ppermute | solution.py:15
  25.2 6.4 %collective-permute-start.2 = (bf16[10,1,2,256]{3,2,1,0:T(2,128)(2,1)S(1)}, bf16[10,1,2,256]{3,2,1,0:T(2,128)(2,1)S(1)}, u32[]{:S(2)}, u32[]{:S(2)}) collective-permute-start(bf16[10,1,2,256]{3,2,1,0:T(2,128)(2,1)S(1)} %get-tuple-element.19), channel_id=1, source_target_pairs={{0,1},{1,2},{2,3},{3,4},{4,5},{5,6},{6,7},{7,0},{8,9},{9,10},{10,1... | collective-permute-start | bytes 30728 | tf_op jit(solution)/shard_map/ppermute | solution.py:14
  26.0 5.7 %copy-start.6 = (bf16[6912,256]{1,0:T(8,128)(2,1)S(1)}, bf16[6912,256]{1,0:T(8,128)(2,1)}, u32[]{:S(2)}) copy-start(bf16[6912,256]{1,0:T(8,128)(2,1)} %param.5) | copy-start | bytes 10616836
  36.1 13.9 %copy-start.1 = (bf16[8,8,2,256]{3,2,1,0:T(2,128)(2,1)}, bf16[8,8,2,256]{3,2,1,0:T(2,128)(2,1)S(1)}, u32[]{:S(2)}) copy-start(bf16[8,8,2,256]{3,2,1,0:T(2,128)(2,1)S(1)} %get-tuple-element.10) | copy-start | bytes 196612
  36.1 1.4 collective-permute-start.5
  36.2 3.2 %collective-permute-start.4 = (bf16[1,8,2,256]{3,2,1,0:T(2,128)(2,1)S(1)}, bf16[1,8,2,256]{3,2,1,0:T(2,128)(2,1)S(1)}, u32[]{:S(2)}, u32[]{:S(2)}) collective-permute-start(bf16[1,8,2,256]{3,2,1,0:T(2,128)(2,1)S(1)} %get-tuple-element.25), channel_id=1, source_target_pairs={{0,8},{8,16},{16,24},{24,0},{1,9},{9,17},{17,25},{25,1},{2,10},{10... | collective-permute-start | bytes 24584 | tf_op jit(solution)/shard_map/ppermute | solution.py:14
  39.4 3.7 %collective-permute-start.7 = (bf16[10,1,2,256]{3,2,1,0:T(2,128)(2,1)S(1)}, bf16[10,1,2,256]{3,2,1,0:T(2,128)(2,1)S(1)}, u32[]{:S(2)}, u32[]{:S(2)}) collective-permute-start(bf16[10,1,2,256]{3,2,1,0:T(2,128)(2,1)S(1)} %get-tuple-element.18), channel_id=1, source_target_pairs={{1,0},{2,1},{3,2},{4,3},{5,4},{6,5},{7,6},{0,7},{9,8},{10,9},{11,1... | collective-permute-start | bytes 30728 | tf_op jit(solution)/shard_map/ppermute | solution.py:15
  41.0 6.4 %collective-permute-start.6 = (bf16[10,1,2,256]{3,2,1,0:T(2,128)(2,1)S(1)}, bf16[10,1,2,256]{3,2,1,0:T(2,128)(2,1)S(1)}, u32[]{:S(2)}, u32[]{:S(2)}) collective-permute-start(bf16[10,1,2,256]{3,2,1,0:T(2,128)(2,1)S(1)} %get-tuple-element.17), channel_id=1, source_target_pairs={{0,1},{1,2},{2,3},{3,4},{4,5},{5,6},{6,7},{7,0},{8,9},{9,10},{10,1... | collective-permute-start | bytes 30728 | tf_op jit(solution)/shard_map/ppermute | solution.py:14
  43.2 6.6 %copy-start.4 = (bf16[10,1,2,256]{3,2,1,0:T(2,128)(2,1)}, bf16[10,1,2,256]{3,2,1,0:T(2,128)(2,1)S(1)}, u32[]{:S(2)}) copy-start(bf16[10,1,2,256]{3,2,1,0:T(2,128)(2,1)S(1)} %collective-permute-done.7) | copy-start | bytes 30724
  47.3 2.4 %copy-start.5 = (bf16[10,1,2,256]{3,2,1,0:T(2,128)(2,1)}, bf16[10,1,2,256]{3,2,1,0:T(2,128)(2,1)S(1)}, u32[]{:S(2)}) copy-start(bf16[10,1,2,256]{3,2,1,0:T(2,128)(2,1)S(1)} %collective-permute-done.6) | copy-start | bytes 30724
  48.1 2.4 %copy-start.3 = (bf16[8,8,2,256]{3,2,1,0:T(2,128)(2,1)S(1)}, bf16[8,8,2,256]{3,2,1,0:T(2,128)(2,1)}, u32[]{:S(2)}) copy-start(bf16[8,8,2,256]{3,2,1,0:T(2,128)(2,1)} %param.7) | copy-start | bytes 196612
  65.5 1.6 collective-permute-start.13
  65.5 3.5 %collective-permute-start.12 = (bf16[1,8,2,256]{3,2,1,0:T(2,128)(2,1)}, bf16[1,8,2,256]{3,2,1,0:T(2,128)(2,1)}, u32[]{:S(2)}, u32[]{:S(2)}) collective-permute-start(bf16[1,8,2,256]{3,2,1,0:T(2,128)(2,1)} %get-tuple-element.21), channel_id=1, source_target_pairs={{0,8},{8,16},{16,24},{24,0},{1,9},{9,17},{17,25},{25,1},{2,10},{10... | collective-permute-start | bytes 24584 | tf_op jit(solution)/shard_map/ppermute | solution.py:14
  69.7 7.2 %collective-permute-start.15 = (bf16[10,1,2,256]{3,2,1,0:T(2,128)(2,1)S(1)}, bf16[10,1,2,256]{3,2,1,0:T(2,128)(2,1)S(1)}, u32[]{:S(2)}, u32[]{:S(2)}) collective-permute-start(bf16[10,1,2,256]{3,2,1,0:T(2,128)(2,1)S(1)} %get-tuple-element.14), channel_id=1, source_target_pairs={{1,0},{2,1},{3,2},{4,3},{5,4},{6,5},{7,6},{0,7},{9,8},{10,9},{11,1... | collective-permute-start | bytes 30728 | tf_op jit(solution)/shard_map/ppermute | solution.py:15
  69.8 7.2 %collective-permute-start.14 = (bf16[10,1,2,256]{3,2,1,0:T(2,128)(2,1)S(1)}, bf16[10,1,2,256]{3,2,1,0:T(2,128)(2,1)S(1)}, u32[]{:S(2)}, u32[]{:S(2)}) collective-permute-start(bf16[10,1,2,256]{3,2,1,0:T(2,128)(2,1)S(1)} %get-tuple-element.13), channel_id=1, source_target_pairs={{0,1},{1,2},{2,3},{3,4},{4,5},{5,6},{6,7},{7,0},{8,9},{9,10},{10,1... | collective-permute-start | bytes 30728 | tf_op jit(solution)/shard_map/ppermute | solution.py:14
  72.8 4.1 %copy-start.2 = (bf16[8,8,2,256]{3,2,1,0:T(2,128)(2,1)S(1)}, bf16[8,8,2,256]{3,2,1,0:T(2,128)(2,1)}, u32[]{:S(2)}) copy-start(bf16[8,8,2,256]{3,2,1,0:T(2,128)(2,1)} %get-tuple-element.9) | copy-start | bytes 196612
  72.8 5.0 %copy-start.7 = (bf16[6912,256]{1,0:T(8,128)(2,1)S(1)}, bf16[6912,256]{1,0:T(8,128)(2,1)}, u32[]{:S(2)}) copy-start(bf16[6912,256]{1,0:T(8,128)(2,1)} %param.5) | copy-start | bytes 10616836
Sparse Core Ops, SparseCore 0:
  64.3 161.1 all-reduce.3
where the time goes:
time: 235 us; the launch traced here: 234 us
  waiting for transfers between devices  159 us (68%)
  local copies, waits for them, and re-layouts  19.9 us (8%)
  starting transfers between devices  19.7 us (8%)
  matrix products  16.9 us (7%)
  between operations  14.4 us (6%)
  other arithmetic  4.42 us (2%)
    unnamed x2, waiting for transfers between devices  144 us
    unnamed x48, local copies, waits for them, and re-layouts  16.8 us
    ppermute x8, starting transfers between devices, padded_2(): after = lax.ppermute(first, axis, down)  14.9 us
    conv_general_dilated x4, matrix products, correlate(): lax.conv_general_dilated(padded[None], weights, (1, 1, 1), [(0, 0), (0, 0...  12.8 us
    ppermute x8, waiting for transfers between devices, padded_2(): before = lax.ppermute(last, axis, up)  11.2 us
    ppermute x8, starting transfers between devices, padded_2(): before = lax.ppermute(last, axis, up)  4.76 us
  transfers between devices with their start and end apart: 17, of which 9 were waited for; matrix products, arithmetic and copies ran while one was open for 7% of the time, Pallas kernels for 0%

commit v1 on v0

v1 whole, which is shorter than its diff:
```python
import functools

import jax
import jax.numpy as jnp
from jax import lax
from jax.experimental import pallas as pl
from jax.experimental.pallas import tpu as pltpu
from jax.sharding import PartitionSpec as P

AX = ("gx", "gy")
F32 = jnp.float32
BF16 = jnp.bfloat16
CH = 256
ROWS = 27 * CH


def permutation(n_gx, n_gy, move):
    pairs = []
    for i in range(n_gx):
        for j in range(n_gy):
            x, c, z, y = move(i // 2, i % 2, j // 2, j % 2)
            x, z = x % (n_gx // 2), z % (n_gy // 2)
            pairs.append((i * n_gy + j, (x * 2 + c) * n_gy + z * 2 + y))
    return pairs


def dot(a, b):
    return lax.dot_general(a, b, (((1,), (0,)), ((), ())), preferred_element_type=F32)


def dot_t(a, b):
    return lax.dot_general(a, b, (((1,), (1,)), ((), ())), preferred_element_type=F32)


def shifted(v, by):
    if by == 0:
        return v
    axis, n = v.ndim - 2, v.shape[-2]
    if by > 0:
        parts = [lax.slice_in_dim(v, by, n, axis=axis), lax.slice_in_dim(v, 0, by, axis=axis)]
    else:
        parts = [lax.slice_in_dim(v, n + by, n, axis=axis), lax.slice_in_dim(v, 0, n + by, axis=axis)]
    return jnp.concatenate(parts, axis=axis)


def window(v, core):
    n = v.shape[-2]
    first = jnp.concatenate([v[..., n - 4 :, :], v[..., :12, :]], axis=-2)
    return jnp.where(core == 0, first, v[..., 4:20, :])


def gradient_kernel(n_x, n_z, n_taps, strip, block, scale, *refs):
    same, other = refs[: 2 * n_x], refs[2 * n_x : 4 * n_x]
    w_hbm = refs[4 * n_x]
    pre_out, cot_out, own_out = refs[4 * n_x + 1 : 4 * n_x + 4]
    sends = refs[4 * n_x + 4 : 4 * n_x + 3 + n_z]
    w_ref, vol, cot, acc0, acc1, hid, grad, sems = refs[4 * n_x + 3 + n_z :]
    gx, gy = lax.axis_index("gx"), lax.axis_index("gy")
    core, side, z = lax.rem(gx, 2), lax.rem(gy, 2), lax.div(gy, 2)
    full = 16 * n_x

    def weight(k):
        rows = pl.ds(k * 768, 768)
        return pltpu.make_async_copy(w_hbm.at[rows], w_ref.at[rows], sems.at[k])

    for k in range(9):
        weight(k).start()

    for dy in range(2):
        at = side if dy == 0 else 1 - side
        for which in range(2):
            for pair in range(5):
                rows = pl.ds(which * 80 + pair * 16, 16)
                parts = []
                for dx in range(n_x):
                    a = same[dx * 2 + dy][rows, :].astype(F32).reshape(2, 8, 512)
                    b = other[dx * 2 + dy][rows, :].astype(F32).reshape(2, 8, 512)
                    parts += [jnp.where(core == 0, a, b), jnp.where(core == 0, b, a)]
                line = jnp.concatenate(parts, axis=1)
                row = 2 + 8 * at + 2 * pair if pair < 4 else 18 * at
                for s in range(3):
                    if which == 0:
                        vol[s, pl.ds(row, 2)] = shifted(line, s - 1).astype(BF16)
                    else:
                        turned = shifted(line, 1 - s).astype(BF16)
                        cot[s, 0, pl.ds(row, 2)] = turned[..., :CH]
                        cot[s, 1, pl.ds(row, 2)] = turned[..., CH:]
    cot[:, 2] = jnp.zeros_like(cot[:, 2])

    acc0[...] = jnp.zeros_like(acc0)
    acc1[...] = jnp.zeros_like(acc1)

    def tap(k, carry):
        weight(k).wait()
        left = vol[lax.div(k, 3), pl.ds(lax.rem(k, 3), 18)].reshape(18 * full, 512)
        base = pl.multiple_of(k * 768, 256)
        acc0[...] += dot(left, w_ref[pl.ds(base + 256, 512), :])
        acc1[...] += dot(left, w_ref[pl.ds(base, 512), :])
        return carry

    lax.fori_loop(0, 9, tap, 0)

    for half, acc in enumerate((acc0, acc1)):
        pre = acc[pl.ds(full, 16 * full), :]
        hid[:, half * 16 * full : (half + 1) * 16 * full] = (pre * jax.nn.sigmoid(pre)).T.astype(BF16)

    first = lax.div(gx * strip, CH)

    def piece(k, carry):
        t = jnp.minimum(first + k, 26)
        a, b, e = lax.div(t, 9), lax.rem(lax.div(t, 3), 3), lax.rem(t, 3)
        z0 = jnp.where(e == 1, 0, jnp.where(e == 0, 1, 2))
        z1 = jnp.where(e == 1, 1, jnp.where(e == 0, 2, 0))
        rows = pl.ds(3 - b, 16)
        total = dot(hid[:, : 16 * full], cot[a, z0, rows].reshape(16 * full, CH))
        total += dot(hid[:, 16 * full :], cot[a, z1, rows].reshape(16 * full, CH))
        grad[pl.ds(pl.multiple_of(k * CH, CH), CH), :] = total * scale
        return carry

    lax.fori_loop(0, n_taps, piece, 0)

    for k in range(n_z):
        start = gx * strip + (2 * lax.rem(z + k, n_z) + side) * block - first * CH
        if block % 8 == 0:
            value = grad[pl.ds(pl.multiple_of(start, 8), block), :]
        else:
            over = lax.rem(start, 8)
            rows = (block + 7 + 7) // 8 * 8
            value = grad[pl.ds(pl.multiple_of(start - over, 8), rows), :]
            value = pltpu.roll(value, lax.rem(rows - over, rows), 0)[:block]
        if k == 0:
            own_out[...] = value
        else:
            sends[k - 1][...] = value.astype(BF16)

    for half, acc in enumerate((acc0, acc1)):
        rows = acc[pl.ds(pl.multiple_of(side * 8 * full, full), 10 * full), :].reshape(10, full, CH)
        pre_out[:, :, half * CH : (half + 1) * CH] = window(rows, core)
        rows = cot[1, half, pl.ds(side * 8, 12)].astype(F32)
        cot_out[:, :, half * CH : (half + 1) * CH] = window(rows, core).astype(BF16)


def local_kernel(pre_ref, cot_ref, w1_hbm, w2_hbm, out_ref, vgrad_ref, w1, w2, hid, cot, thr, acc, sems):
    def weight(which, k):
        rows = pl.ds(k * 768, 768)
        src, dst = ((w1_hbm, w1), (w2_hbm, w2))[which]
        return pltpu.make_async_copy(src.at[rows], dst.at[rows], sems.at[which, k])

    for which in (1, 0):
        for k in range(9):
            weight(which, k).start()

    pre = pre_ref[...]
    sig = jax.nn.sigmoid(pre)
    for s in range(3):
        hid[s] = shifted(pre * sig, s - 1).astype(BF16)
        cot[s] = shifted(cot_ref[...].astype(F32), s - 1).astype(BF16)

    def back(k, carry):
        left = cot[lax.div(k, 3), pl.ds(lax.rem(k, 3), 10)].reshape(160, 512)
        base = pl.multiple_of((8 - k) * 768, 256)
        w = w2[pl.ds(base, 768), :]
        acc[:, :CH] += dot_t(left[:, :CH], w[256:512]) + dot_t(left[:, CH:], w[:256])
        acc[:, CH:] += dot_t(left[:, :CH], w[512:]) + dot_t(left[:, CH:], w[256:512])
        return carry

    def forward(k, carry):
        left = hid[lax.div(k, 3), pl.ds(lax.rem(k, 3), 8)].reshape(128, 512)
        base = pl.multiple_of(k * 768, 256)
        acc[:128, :CH] += dot(left, w2[pl.ds(base + 256, 512), :])
        acc[:128, CH:] += dot(left, w2[pl.ds(base, 512), :])
        return carry

    def last(k, carry):
        left = thr[lax.div(k, 3), pl.ds(lax.rem(k, 3), 8)].reshape(128, 512)
        base = pl.multiple_of((8 - k) * 768, 256)
        w = w1[pl.ds(base, 768), :]
        acc[:128, :CH] += dot_t(left[:, :CH], w[256:512]) + dot_t(left[:, CH:], w[:256])
        acc[:128, CH:] += dot_t(left[:, :CH], w[512:]) + dot_t(left[:, CH:], w[256:512])
        return carry

    for k in range(9):
        weight(1, k).wait()
    acc[...] = jnp.zeros_like(acc)
    lax.fori_loop(0, 9, back, 0)
    through = acc[...].reshape(10, 16, 512) * sig * (1.0 + pre * (1.0 - sig))
    for s in range(3):
        thr[s] = shifted(through, s - 1).astype(BF16)

    acc[...] = jnp.zeros_like(acc)
    lax.fori_loop(0, 9, forward, 0)
    out_ref[...] = acc[:128].reshape(8, 16, 512)[:, 4:12].astype(BF16)

    for k in range(9):
        weight(0, k).wait()
    acc[...] = jnp.zeros_like(acc)
    lax.fori_loop(0, 9, last, 0)
    vgrad_ref[...] = acc[:128].reshape(8, 16, 512)[:, 4:12].astype(BF16)


def body(volume, first_weight, second_weight, cotangent):
    sx, sy, sz, chans = volume.shape
    n_gx, n_gy = lax.axis_size("gx"), lax.axis_size("gy")
    n_x, n_z = n_gx // 2, n_gy // 2
    scale = 1.0 / float(sx * n_gx * sy * n_gy * sz) ** 0.5
    strip = ROWS // n_gx
    block = strip // n_gy
    n_taps = max(-(-(i + 1) * strip // CH) - i * strip // CH for i in range(n_gx))
    full = sx * n_gx
    side = lax.rem(lax.axis_index("gy"), 2)
    perm = functools.partial(permutation, n_gx, n_gy)

    def lines(v):
        return jnp.transpose(v, (1, 0, 2, 3)).reshape(sy, sx, sz * chans)

    own = jnp.stack([lines(volume), lines(cotangent)])
    edge = lax.dynamic_slice_in_dim(own, side * (sy - 2), 2, axis=1)
    edge = lax.ppermute(edge, AX, perm(lambda x, c, z, y: (x, c, z - 1 + 2 * y, 1 - y)))
    own = jnp.concatenate([own, edge], axis=1).reshape(2 * (sy + 2) * sx, sz * chans)

    same = []
    for dx in range(n_x):
        for dy in range(2):
            if dx == 0 and dy == 0:
                same.append(own)
            else:
                same.append(lax.ppermute(own, AX, perm(lambda x, c, z, y, dx=dx, dy=dy: (x - dx, c, z, y ^ dy))))
    other = [lax.ppermute(v, AX, perm(lambda x, c, z, y: (x, 1 - c, z, y))) for v in same]

    vmem = pl.BlockSpec(memory_space=pltpu.VMEM)
    hbm = pl.BlockSpec(memory_space=pl.ANY)
    results = pl.pallas_call(
        functools.partial(gradient_kernel, n_x, n_z, n_taps, strip, block, scale),
        out_shape=[
            jax.ShapeDtypeStruct((10, 16, 512), F32),
            jax.ShapeDtypeStruct((12, 16, 512), BF16),
            jax.ShapeDtypeStruct((block, CH), F32),
        ]
        + [jax.ShapeDtypeStruct((block, CH), BF16)] * (n_z - 1),
        in_specs=[vmem] * (4 * n_x) + [hbm],
        out_specs=[vmem] * (2 + n_z),
        scratch_shapes=[
            pltpu.VMEM((ROWS, CH), BF16),
            pltpu.VMEM((3, 20, full, 512), BF16),
            pltpu.VMEM((3, 3, 20, full, CH), BF16),
            pltpu.VMEM((18 * full, CH), F32),
            pltpu.VMEM((18 * full, CH), F32),
            pltpu.VMEM((CH, 32 * full), BF16),
            pltpu.VMEM((n_taps * CH + (0 if block % 8 == 0 else 16), CH), F32),
            pltpu.SemaphoreType.DMA((9,)),
        ],
        compiler_params=pltpu.CompilerParams(vmem_limit_bytes=48 * 1024 * 1024),
        cost_estimate=pl.CostEstimate(flops=4 * 10**9, bytes_accessed=6 * 10**6, transcendentals=0),
        name="group_gradient",
    )(*same, *other, first_weight)
    pre, cot, mine, sends = results[0], results[1], results[2], results[3:]

    received = [
        lax.ppermute(v, AX, perm(lambda x, c, z, y, k=k: (x, c, z + k + 1, y))) for k, v in enumerate(sends)
    ]

    output, volume_grad = pl.pallas_call(
        local_kernel,
        out_shape=[jax.ShapeDtypeStruct((sy, sx, 512), BF16)] * 2,
        in_specs=[vmem, vmem, hbm, hbm],
        out_specs=[vmem, vmem],
        scratch_shapes=[
            pltpu.VMEM((ROWS, CH), BF16),
            pltpu.VMEM((ROWS, CH), BF16),
            pltpu.VMEM((3, 10, 16, 512), BF16),
            pltpu.VMEM((3, 12, 16, 512), BF16),
            pltpu.VMEM((3, 10, 16, 512), BF16),
            pltpu.VMEM((160, 512), F32),
            pltpu.SemaphoreType.DMA((2, 9)),
        ],
        compiler_params=pltpu.CompilerParams(vmem_limit_bytes=32 * 1024 * 1024),
        cost_estimate=pl.CostEstimate(flops=4 * 10**9, bytes_accessed=8 * 10**6, transcendentals=0),
        name="local_convolutions",
    )(pre, cot, first_weight, second_weight)

    def cells(v):
        return jnp.transpose(v.reshape(sy, sx, sz, chans), (1, 0, 2, 3))

    total = mine
    for v in received:
        total = total + v.astype(F32)
    return cells(output), cells(volume_grad), total.reshape(-1)


def solution(mesh):
    in_specs = (P("gx", "gy", None, None), P(), P(), P("gx", "gy", None, None))
    out_specs = (P("gx", "gy", None, None), P("gx", "gy", None, None), P(("gx", "gy")))
    return jax.shard_map(body, mesh=mesh, in_specs=in_specs, out_specs=out_specs, check_vma=False)
```

time: 235 us -> 51.2 us (0.22)
  waiting for transfers between devices: 159 us -> 9.27 us
  Pallas kernels: 0 us -> 21.5 us
  matrix products: 16.9 us -> 0 us
  local copies, waits for them, and re-layouts: 19.9 us -> 5.4 us
  between operations: 14.4 us -> 0.72 us
  starting transfers between devices: 19.7 us -> 14 us
  other arithmetic: 4.42 us -> 0.07 us
    unnamed x2 -> x0, waiting for transfers between devices: 144 us -> none
    pallas_call x0 -> x2, Pallas kernels: none -> 21.5 us  [the longest x1 11.7 us: body(): pl.pallas_call(local_kernel, out_shape=[jax.ShapeDtypeStruct((sy, sx, 512...]
    unnamed x48 -> x6, local copies, waits for them, and re-layouts: 16.8 us -> 2.83 us
    conv_general_dilated x4 -> x0, matrix products: 12.8 us -> none  [correlate(): lax.conv_general_dilated(padded[None], weights, (1, 1, 1), [(0, 0), (0, 0...]
    ppermute x16 -> x11, starting transfers between devices: 19.6 us -> 14 us  [the longest x1 6.07 us: body(): lax.ppermute(edge, AX, perm(lambda x, c, z, y: (x, c, z - 1 + 2 * y, 1 -...]
    ppermute x16 -> x11, waiting for transfers between devices: 14.7 us -> 9.27 us  [the longest x3 5.98 us: body(): lax.ppermute(own, AX, perm(lambda x, c, z, y, dx=dx, dy=dy: (x - dx, c, z...]
    dot_general x1 -> x0, matrix products: 4.07 us -> none  [weight_term(): lax.dot_general(stacked, grad.reshape(sx * sy * sz, chans), (((0,), (0,))...]
    slice x6 -> x0, local copies, waits for them, and re-layouts: 2.98 us -> none  [the longest x2 1.61 us: padded_2(): first = lax.slice_in_dim(x, 0, width, axis=dim)]
  transfers between devices with their start and end apart: 17 -> 11, of which waited for: 9 -> 6; matrix products, arithmetic and copies ran while one was open for 7% -> 1% of each run, Pallas kernels for 0% -> 23%
where the time goes in v1:
time: 51.2 us; the launch traced here: 51 us
  Pallas kernels  21.5 us (42%)
  starting transfers between devices  14 us (27%)
  waiting for transfers between devices  9.27 us (18%)
  local copies, waits for them, and re-layouts  5.4 us (11%)
  between operations  0.72 us (1%)
    pallas_call x1, Pallas kernels, body(): pl.pallas_call(local_kernel, out_shape=[jax.ShapeDtypeStruct((sy, sx, 512...  11.7 us
    pallas_call x1, Pallas kernels, body(): pl.pallas_call(functools.partial(gradient_kernel, n_x, n_z, n_taps, strip...  9.79 us
    ppermute x1, starting transfers between devices, body(): lax.ppermute(edge, AX, perm(lambda x, c, z, y: (x, c, z - 1 + 2 * y, 1 -...  6.07 us
    ppermute x3, waiting for transfers between devices, body(): lax.ppermute(own, AX, perm(lambda x, c, z, y, dx=dx, dy=dy: (x - dx, c, z...  5.98 us
    ppermute x3, starting transfers between devices, body(): lax.ppermute(v, AX, perm(lambda x, c, z, y, k=k: (x, c, z + k + 1, y)))  4.38 us
    ppermute x3, starting transfers between devices, body(): lax.ppermute(own, AX, perm(lambda x, c, z, y, dx=dx, dy=dy: (x - dx, c, z...  3.55 us
    unnamed x6, local copies, waits for them, and re-layouts  2.83 us
    ppermute x1, waiting for transfers between devices, body(): lax.ppermute(edge, AX, perm(lambda x, c, z, y: (x, c, z - 1 + 2 * y, 1 -...  1.89 us
  transfers between devices with their start and end apart: 11, of which 6 were waited for; matrix products, arithmetic and copies ran while one was open for 1% of the time, Pallas kernels for 23%

profile of v1, /device:TPU:0, one launch (start us, length us, event | category | flops | bytes accessed | tf_op | source)
XLA Modules:
  0.0 51.0 jit_solution(17433405986644586988)
XLA Ops:
  0.6 0.9 %stack_reshape.6 = bf16[1,8,8,512]{3,1,2,0:T(8,128)(2,1)S(1)} reshape(bf16[8,8,2,256]{3,2,0,1:T(2,128)(2,1)} %bitcast.24) | data formatting | bytes 131072 | tf_op jit(solution)/shard_map/stack;reshape | solution.py:216
  1.6 0.9 %stack_reshape.7 = bf16[1,8,8,512]{3,1,2,0:T(8,128)(2,1)S(1)} reshape(bf16[8,8,2,256]{3,2,0,1:T(2,128)(2,1)} %bitcast.25) | data formatting | bytes 131072 | tf_op jit(solution)/shard_map/stack;reshape | solution.py:216
  2.5 6.1 %collective-permute-start = (bf16[2,2,8,512]{3,2,1,0:T(8,128)(2,1)S(1)}, bf16[2,2,8,512]{3,2,1,0:T(8,128)(2,1)S(1)}, u32[]{:S(2)}, u32[]{:S(2)}) collective-permute-start(bf16[2,2,8,512]{3,2,1,0:T(8,128)(2,1)S(1)} %constant_dynamic-slice_fusion), channel_id=1, source_target_pairs={{0,7},{1,2},{2,1},{3,4},{4,3},{5,6},{6,5},{7,0},{8,15},{9,10},{10,... | collective-permute-start | bytes 98312 | tf_op jit(solution)/shard_map/ppermute | solution.py:218
  8.6 1.9 %collective-permute-done = bf16[2,2,8,512]{3,2,1,0:T(8,128)(2,1)S(1)} collective-permute-done((bf16[2,2,8,512]{3,2,1,0:T(8,128)(2,1)S(1)}, bf16[2,2,8,512]{3,2,1,0:T(8,128)(2,1)S(1)}, u32[]{:S(2)}, u32[]{:S(2)}) %collective-permute-start) | collective-permute-done | bytes 32800 | tf_op jit(solution)/shard_map/ppermute | solution.py:218
  10.5 0.9 %collective-permute-start.3 = (bf16[160,512]{1,0:T(8,128)(2,1)S(1)}, bf16[160,512]{1,0:T(8,128)(2,1)S(1)}, u32[]{:S(2)}, u32[]{:S(2)}) collective-permute-start(bf16[160,512]{1,0:T(8,128)(2,1)S(1)} %bitcast.16), channel_id=1, source_target_pairs={{0,17},{1,16},{2,19},{3,18},{4,21},{5,20},{6,23},{7,22},{8,25},{9,... | collective-permute-start | bytes 491528 | tf_op jit(solution)/shard_map/ppermute | solution.py:227
  11.4 0.9 %collective-permute-start.2 = (bf16[160,512]{1,0:T(8,128)(2,1)S(1)}, bf16[160,512]{1,0:T(8,128)(2,1)S(1)}, u32[]{:S(2)}, u32[]{:S(2)}) collective-permute-start(bf16[160,512]{1,0:T(8,128)(2,1)S(1)} %bitcast.17), channel_id=1, source_target_pairs={{0,16},{1,17},{2,18},{3,19},{4,20},{5,21},{6,22},{7,23},{8,24},{9,... | collective-permute-start | bytes 491528 | tf_op jit(solution)/shard_map/ppermute | solution.py:227
  12.3 1.8 %collective-permute-start.1 = (bf16[160,512]{1,0:T(8,128)(2,1)S(1)}, bf16[160,512]{1,0:T(8,128)(2,1)S(1)}, u32[]{:S(2)}, u32[]{:S(2)}) collective-permute-start(bf16[160,512]{1,0:T(8,128)(2,1)S(1)} %bitcast.18), channel_id=1, source_target_pairs={{0,1},{1,0},{2,3},{3,2},{4,5},{5,4},{6,7},{7,6},{8,9},{9,8},{10,11... | collective-permute-start | bytes 491528 | tf_op jit(solution)/shard_map/ppermute | solution.py:227
  14.0 0.0 collective-permute-start.4
  14.1 4.3 %collective-permute-done.3.refs_3_ = bf16[160,512]{1,0:T(8,128)(2,1)S(1)} collective-permute-done((bf16[160,512]{1,0:T(8,128)(2,1)S(1)}, bf16[160,512]{1,0:T(8,128)(2,1)S(1)}, u32[]{:S(2)}, u32[]{:S(2)}) %collective-permute-start.3) | collective-permute-done | bytes 163872 | tf_op jit(solution)/shard_map/ppermute | solution.py:227
  18.3 0.0 collective-permute-start.7
  18.3 0.6 %collective-permute-done.2.refs_2_ = bf16[160,512]{1,0:T(8,128)(2,1)S(1)} collective-permute-done((bf16[160,512]{1,0:T(8,128)(2,1)S(1)}, bf16[160,512]{1,0:T(8,128)(2,1)S(1)}, u32[]{:S(2)}, u32[]{:S(2)}) %collective-permute-start.2) | collective-permute-done | bytes 163872 | tf_op jit(solution)/shard_map/ppermute | solution.py:227
  18.9 0.0 collective-permute-start.6
  18.9 1.1 %collective-permute-done.1.refs_1_ = bf16[160,512]{1,0:T(8,128)(2,1)S(1)} collective-permute-done((bf16[160,512]{1,0:T(8,128)(2,1)S(1)}, bf16[160,512]{1,0:T(8,128)(2,1)S(1)}, u32[]{:S(2)}, u32[]{:S(2)}) %collective-permute-start.1) | collective-permute-done | bytes 163872 | tf_op jit(solution)/shard_map/ppermute | solution.py:227
  20.0 0.0 collective-permute-start.5
  20.0 0.0 collective-permute-done.4.refs_4_
  20.0 0.0 collective-permute-done.7.refs_7_
  20.1 0.2 collective-permute-done.6.refs_6_
  20.3 1.1 %collective-permute-done.5.refs_5_ = bf16[160,512]{1,0:T(8,128)(2,1)S(1)} collective-permute-done((bf16[160,512]{1,0:T(8,128)(2,1)S(1)}, bf16[160,512]{1,0:T(8,128)(2,1)S(1)}, u32[]{:S(2)}, u32[]{:S(2)}) %collective-permute-start.5) | collective-permute-done | bytes 163872 | tf_op jit(solution)/shard_map/ppermute | solution.py:228
  21.4 0.0 copy-start
  21.4 2.0 %copy-done = bf16[6912,256]{1,0:T(8,128)(2,1)S(1)} copy-done((bf16[6912,256]{1,0:T(8,128)(2,1)S(1)}, bf16[6912,256]{1,0:T(8,128)(2,1)}, u32[]{:S(2)}) %copy-start) | copy-done | bytes 3538968
  23.4 9.8 %group_gradient.1 = (f32[10,16,512]{2,1,0:T(8,128)S(1)}, bf16[12,16,512]{2,1,0:T(8,128)(2,1)S(1)}, f32[216,256]{1,0:T(8,128)S(1)}, bf16[216,256]{1,0:T(8,128)(2,...) custom-call(bf16[160,512]{1,0:T(8,128)(2,1)S(1)} %bitcast.20, ...), custom_call_target="tpu_custom_call" | custom-call | flops 4000000000 | bytes 6000000 | tf_op jit(solution)/shard_map/group_gradient/pallas_call | solution.py:232
  33.2 0.1 collective-permute-start.8
  33.3 4.3 %collective-permute-start.9 = (bf16[216,256]{1,0:T(8,128)(2,1)S(1)}, bf16[216,256]{1,0:T(8,128)(2,1)S(1)}, u32[]{:S(2)}, u32[]{:S(2)}) collective-permute-start(bf16[216,256]{1,0:T(8,128)(2,1)S(1)} %get-tuple-element.17), channel_id=1, source_target_pairs={{0,4},{1,5},{2,6},{3,7},{4,0},{5,1},{6,2},{7,3},{8,12},{9,13},{10,... | collective-permute-start | bytes 331784 | tf_op jit(solution)/shard_map/ppermute | solution.py:259
  37.6 0.0 collective-permute-start.10
  37.6 0.0 copy-done.1
  37.6 11.7 %local_convolutions.1 = (bf16[8,8,512]{2,1,0:T(8,128)(2,1)S(1)}, bf16[8,8,512]{2,1,0:T(8,128)(2,1)S(1)}) custom-call(f32[10,16,512]{2,1,0:T(8,128)S(1)} %get-tuple-element.11.pre_ref, bf16[12,16,512]{2,1,0:T(8,128)(2,1)S(1)} %get-tuple-element.12.cot_ref, bf16[6912,256]{1,0:T(8,128)(2,1)S(1)} %copy-done, bf16[6912,256]{1,0:T(8,128)(2,1)S(1)} %copy-done.1), custom_call_target="tpu_custom_call" | custom-call | flops 4000000000 | bytes 8000000 | tf_op jit(solution)/shard_map/local_convolutions/pallas_call | solution.py:262
  49.4 0.8 %copy_bitcast_fusion = (bf16[8,8,2,256]{3,2,1,0:T(2,128)(2,1)}, bf16[8,8,2,256]{3,2,1,0:T(2,128)(2,1)}) fusion(bf16[8,8,2,256]{3,1,2,0:T(8,128)(2,1)S(1)} %bitcast.22, bf16[8,8,2,256]{3,1,2,0:T(8,128)(2,1)S(1)} %bitcast.21), kind=kLoop, calls=%fused_computation.2 | loop fusion | bytes 262144 | tf_op jit(solution)/shard_map/transpose | solution.py:282
  50.1 0.0 collective-permute-done.8
  50.1 0.0 collective-permute-done.9
  50.1 0.0 collective-permute-done.10
  50.1 0.1 add_bitcast_fusion
  50.2 0.8 %copy.11 = f32[27,2,8,128]{3,1,2,0:T(2,128)} copy(f32[27,2,8,128]{3,2,1,0:T(8,128)S(1)} %add_bitcast_fusion) | data formatting | bytes 442368
  (5 shorter events, 0.1 us)
Async XLA Ops:
  2.5 8.0 %collective-permute-start = (bf16[2,2,8,512]{3,2,1,0:T(8,128)(2,1)S(1)}, bf16[2,2,8,512]{3,2,1,0:T(8,128)(2,1)S(1)}, u32[]{:S(2)}, u32[]{:S(2)}) collective-permute-start(bf16[2,2,8,512]{3,2,1,0:T(8,128)(2,1)S(1)} %constant_dynamic-slice_fusion), channel_id=1, source_target_pairs={{0,7},{1,2},{2,1},{3,4},{4,3},{5,6},{6,5},{7,0},{8,15},{9,10},{10,... | collective-permute-start | bytes 98312 | tf_op jit(solution)/shard_map/ppermute | solution.py:218
  10.5 7.8 %collective-permute-start.3 = (bf16[160,512]{1,0:T(8,128)(2,1)S(1)}, bf16[160,512]{1,0:T(8,128)(2,1)S(1)}, u32[]{:S(2)}, u32[]{:S(2)}) collective-permute-start(bf16[160,512]{1,0:T(8,128)(2,1)S(1)} %bitcast.16), channel_id=1, source_target_pairs={{0,17},{1,16},{2,19},{3,18},{4,21},{5,20},{6,23},{7,22},{8,25},{9,... | collective-permute-start | bytes 491528 | tf_op jit(solution)/shard_map/ppermute | solution.py:227
  11.4 7.5 %collective-permute-start.2 = (bf16[160,512]{1,0:T(8,128)(2,1)S(1)}, bf16[160,512]{1,0:T(8,128)(2,1)S(1)}, u32[]{:S(2)}, u32[]{:S(2)}) collective-permute-start(bf16[160,512]{1,0:T(8,128)(2,1)S(1)} %bitcast.17), channel_id=1, source_target_pairs={{0,16},{1,17},{2,18},{3,19},{4,20},{5,21},{6,22},{7,23},{8,24},{9,... | collective-permute-start | bytes 491528 | tf_op jit(solution)/shard_map/ppermute | solution.py:227
  12.3 7.8 %collective-permute-start.1 = (bf16[160,512]{1,0:T(8,128)(2,1)S(1)}, bf16[160,512]{1,0:T(8,128)(2,1)S(1)}, u32[]{:S(2)}, u32[]{:S(2)}) collective-permute-start(bf16[160,512]{1,0:T(8,128)(2,1)S(1)} %bitcast.18), channel_id=1, source_target_pairs={{0,1},{1,0},{2,3},{3,2},{4,5},{5,4},{6,7},{7,6},{8,9},{9,8},{10,11... | collective-permute-start | bytes 491528 | tf_op jit(solution)/shard_map/ppermute | solution.py:227
  14.0 6.0 %collective-permute-start.4 = (bf16[160,512]{1,0:T(8,128)(2,1)S(1)}, bf16[160,512]{1,0:T(8,128)(2,1)S(1)}, u32[]{:S(2)}, u32[]{:S(2)}) collective-permute-start(bf16[160,512]{1,0:T(8,128)(2,1)S(1)} %bitcast.19), channel_id=1, source_target_pairs={{0,8},{1,9},{2,10},{3,11},{4,12},{5,13},{6,14},{7,15},{8,0},{9,1},... | collective-permute-start | bytes 491528 | tf_op jit(solution)/shard_map/ppermute | solution.py:228
  18.3 1.7 %collective-permute-start.7 = (bf16[160,512]{1,0:T(8,128)(2,1)S(1)}, bf16[160,512]{1,0:T(8,128)(2,1)S(1)}, u32[]{:S(2)}, u32[]{:S(2)}) collective-permute-start(bf16[160,512]{1,0:T(8,128)(2,1)S(1)} %collective-permute-done.3.refs_3_), channel_id=1, source_target_pairs={{0,8},{1,9},{2,10},{3,11},{4,12},{5,13},{6,14},{7,15},{8,0},{9,1},... | collective-permute-start | bytes 491528 | tf_op jit(solution)/shard_map/ppermute | solution.py:228
  18.9 1.4 %collective-permute-start.6 = (bf16[160,512]{1,0:T(8,128)(2,1)S(1)}, bf16[160,512]{1,0:T(8,128)(2,1)S(1)}, u32[]{:S(2)}, u32[]{:S(2)}) collective-permute-start(bf16[160,512]{1,0:T(8,128)(2,1)S(1)} %collective-permute-done.2.refs_2_), channel_id=1, source_target_pairs={{0,8},{1,9},{2,10},{3,11},{4,12},{5,13},{6,14},{7,15},{8,0},{9,1},... | collective-permute-start | bytes 491528 | tf_op jit(solution)/shard_map/ppermute | solution.py:228
  20.0 1.4 %collective-permute-start.5 = (bf16[160,512]{1,0:T(8,128)(2,1)S(1)}, bf16[160,512]{1,0:T(8,128)(2,1)S(1)}, u32[]{:S(2)}, u32[]{:S(2)}) collective-permute-start(bf16[160,512]{1,0:T(8,128)(2,1)S(1)} %collective-permute-done.1.refs_1_), channel_id=1, source_target_pairs={{0,8},{1,9},{2,10},{3,11},{4,12},{5,13},{6,14},{7,15},{8,0},{9,1},... | collective-permute-start | bytes 491528 | tf_op jit(solution)/shard_map/ppermute | solution.py:228
  21.4 2.0 %copy-start = (bf16[6912,256]{1,0:T(8,128)(2,1)S(1)}, bf16[6912,256]{1,0:T(8,128)(2,1)}, u32[]{:S(2)}) copy-start(bf16[6912,256]{1,0:T(8,128)(2,1)} %w1_hbm.1) | copy-start | bytes 10616836
  23.4 14.2 %copy-start.1 = (bf16[6912,256]{1,0:T(8,128)(2,1)S(1)}, bf16[6912,256]{1,0:T(8,128)(2,1)}, u32[]{:S(2)}) copy-start(bf16[6912,256]{1,0:T(8,128)(2,1)} %w2_hbm.1) | copy-start | bytes 10616836
  33.2 16.9 %collective-permute-start.8 = (bf16[216,256]{1,0:T(8,128)(2,1)S(1)}, bf16[216,256]{1,0:T(8,128)(2,1)S(1)}, u32[]{:S(2)}, u32[]{:S(2)}) collective-permute-start(bf16[216,256]{1,0:T(8,128)(2,1)S(1)} %get-tuple-element.16), channel_id=1, source_target_pairs={{0,2},{1,3},{2,4},{3,5},{4,6},{5,7},{6,0},{7,1},{8,10},{9,11},{10,... | collective-permute-start | bytes 331784 | tf_op jit(solution)/shard_map/ppermute | solution.py:259
  33.3 16.8 %collective-permute-start.9 = (bf16[216,256]{1,0:T(8,128)(2,1)S(1)}, bf16[216,256]{1,0:T(8,128)(2,1)S(1)}, u32[]{:S(2)}, u32[]{:S(2)}) collective-permute-start(bf16[216,256]{1,0:T(8,128)(2,1)S(1)} %get-tuple-element.17), channel_id=1, source_target_pairs={{0,4},{1,5},{2,6},{3,7},{4,0},{5,1},{6,2},{7,3},{8,12},{9,13},{10,... | collective-permute-start | bytes 331784 | tf_op jit(solution)/shard_map/ppermute | solution.py:259
  37.6 12.5 %collective-permute-start.10 = (bf16[216,256]{1,0:T(8,128)(2,1)S(1)}, bf16[216,256]{1,0:T(8,128)(2,1)S(1)}, u32[]{:S(2)}, u32[]{:S(2)}) collective-permute-start(bf16[216,256]{1,0:T(8,128)(2,1)S(1)} %get-tuple-element.18), channel_id=1, source_target_pairs={{0,6},{1,7},{2,0},{3,1},{4,2},{5,3},{6,4},{7,5},{8,14},{9,15},{10,... | collective-permute-start | bytes 331784 | tf_op jit(solution)/shard_map/ppermute | solution.py:259

commit v2 on v1

v2 whole, which is shorter than its diff:
```python
import functools

import jax
import jax.numpy as jnp
from jax import lax
from jax.experimental import pallas as pl
from jax.experimental.pallas import tpu as pltpu
from jax.sharding import PartitionSpec as P

AX = ("gx", "gy")
F32 = jnp.float32
BF16 = jnp.bfloat16
CH = 256
ROWS = 27 * CH


def permutation(n_gx, n_gy, move):
    pairs = []
    for i in range(n_gx):
        for j in range(n_gy):
            x, c, z, y = move(i // 2, i % 2, j // 2, j % 2)
            x, z = x % (n_gx // 2), z % (n_gy // 2)
            pairs.append((i * n_gy + j, (x * 2 + c) * n_gy + z * 2 + y))
    return pairs


def dot(a, b):
    return lax.dot_general(a, b, (((1,), (0,)), ((), ())), preferred_element_type=F32)


def dot_t(a, b):
    return lax.dot_general(a, b, (((1,), (1,)), ((), ())), preferred_element_type=F32)


def shifted(v, by):
    if by == 0:
        return v
    axis, n = v.ndim - 2, v.shape[-2]
    if by > 0:
        parts = [lax.slice_in_dim(v, by, n, axis=axis), lax.slice_in_dim(v, 0, by, axis=axis)]
    else:
        parts = [lax.slice_in_dim(v, n + by, n, axis=axis), lax.slice_in_dim(v, 0, n + by, axis=axis)]
    return jnp.concatenate(parts, axis=axis)


def window(v, core):
    n = v.shape[-2]
    first = jnp.concatenate([v[..., n - 4 :, :], v[..., :12, :]], axis=-2)
    return jnp.where(core == 0, first, v[..., 4:20, :])


def assemble(same, other, core, side, put):
    n_x = len(same) // 2
    for dy in range(2):
        at = side if dy == 0 else 1 - side
        for pair in range(5):
            rows = slice(pair * 16, pair * 16 + 16)
            parts = []
            for dx in range(n_x):
                a = same[dx * 2 + dy][rows, :].astype(F32).reshape(2, 8, 512)
                b = other[dx * 2 + dy][rows, :].astype(F32).reshape(2, 8, 512)
                parts += [jnp.where(core == 0, a, b), jnp.where(core == 0, b, a)]
            put(2 + 8 * at + 2 * pair if pair < 4 else 18 * at, jnp.concatenate(parts, axis=1))


def both(w):
    return jnp.concatenate([w[CH:], w[: 2 * CH]], axis=1)


def place():
    gx, gy = lax.axis_index("gx"), lax.axis_index("gy")
    return gx, lax.rem(gx, 2), lax.div(gy, 2), lax.rem(gy, 2)


def hidden_kernel(n_x, *refs):
    same, other = refs[: 2 * n_x], refs[2 * n_x : 4 * n_x]
    w_ref, pre, hid, vol = refs[4 * n_x :]
    _, core, _, side = place()
    full = 16 * n_x

    def put(row, line):
        for s in range(3):
            vol[s, pl.ds(row, 2)] = shifted(line, s - 1).astype(BF16)

    assemble(same, other, core, side, put)
    for k in range(9):
        left = vol[k // 3, k % 3 : k % 3 + 18].reshape(18 * full, 512)
        term = dot(left, both(w_ref[k * 768 : k * 768 + 768, :]))
        pre[...] = term if k == 0 else pre[...] + term
    inner = pre[full : 17 * full, :]
    hid[...] = (inner * jax.nn.sigmoid(inner)).T.astype(BF16)


def gradient_kernel(n_x, n_z, groups, strip, block, scale, *refs):
    same, other = refs[: 2 * n_x], refs[2 * n_x : 4 * n_x]
    hid, cot, own_out = refs[4 * n_x : 4 * n_x + 3]
    sends = refs[4 * n_x + 3 : 4 * n_x + 2 + n_z]
    grad = refs[-1]
    gx, core, z, side = place()
    full = 16 * n_x

    def put(row, line):
        for s in range(3):
            cot[s, pl.ds(row, 2)] = shifted(line, 1 - s).astype(BF16)

    assemble(same, other, core, side, put)
    first = lax.div(gx * strip, 3 * CH)
    for k in range(groups):
        ab = jnp.minimum(first + k, 8)
        right = cot[lax.div(ab, 3), pl.ds(3 - lax.rem(ab, 3), 16)].reshape(16 * full, 512)
        product = dot(hid[...], right) * scale
        at = k * 3 * CH
        grad[at : at + CH, :] = product[:CH, CH:]
        grad[at + CH : at + 2 * CH, :] = product[:CH, :CH] + product[CH:, CH:]
        grad[at + 2 * CH : at + 3 * CH, :] = product[CH:, :CH]

    for k in range(n_z):
        start = gx * strip + (2 * lax.rem(z + k, n_z) + side) * block - first * 3 * CH
        if block % 8 == 0:
            value = grad[pl.ds(pl.multiple_of(start, 8), block), :]
        else:
            over = lax.rem(start, 8)
            rows = (block + 7 + 7) // 8 * 8
            value = grad[pl.ds(pl.multiple_of(start - over, 8), rows), :]
            value = pltpu.roll(value, lax.rem(rows - over, rows), 0)[:block]
        if k == 0:
            own_out[...] = value
        else:
            sends[k - 1][...] = value.astype(BF16)


def local_kernel(pre_ref, cot_ref, w1, w2, out_ref, vgrad_ref, hid, cot, thr, acc):
    _, core, _, side = place()
    full = cot_ref.shape[2]
    pre = pre_ref[pl.ds(pl.multiple_of(side * 8 * full, full), 10 * full), :]
    pre = window(pre.reshape(10, full, 512), core)
    sig = jax.nn.sigmoid(pre)
    turned = window(cot_ref[1, pl.ds(side * 8, 12)].astype(F32), core)
    for s in range(3):
        hid[s] = shifted(pre * sig, s - 1).astype(BF16)
        cot[s] = shifted(turned, s - 1).astype(BF16)

    for k in range(9):
        left = cot[k // 3, k % 3 : k % 3 + 10].reshape(160, 512)
        term = dot_t(left, both(w2[(8 - k) * 768 : (8 - k) * 768 + 768, :]))
        acc[...] = term if k == 0 else acc[...] + term
    through = acc[...].reshape(10, 16, 512) * sig * (1.0 + pre * (1.0 - sig))
    for s in range(3):
        thr[s] = shifted(through, s - 1).astype(BF16)

    for k in range(9):
        left = hid[k // 3, k % 3 : k % 3 + 8].reshape(128, 512)
        term = dot(left, both(w2[k * 768 : k * 768 + 768, :]))
        acc[:128] = term if k == 0 else acc[:128] + term
    out_ref[...] = acc[:128].reshape(8, 16, 512)[:, 4:12].astype(BF16)

    for k in range(9):
        left = thr[k // 3, k % 3 : k % 3 + 8].reshape(128, 512)
        term = dot_t(left, both(w1[(8 - k) * 768 : (8 - k) * 768 + 768, :]))
        acc[:128] = term if k == 0 else acc[:128] + term
    vgrad_ref[...] = acc[:128].reshape(8, 16, 512)[:, 4:12].astype(BF16)


def extend_kernel(vol, cot, edge, vol_out, cot_out):
    for k, (ref, out) in enumerate(((vol, vol_out), (cot, cot_out))):
        out[:64, :] = ref[...]
        out[64:, :] = edge[k * 16 : k * 16 + 16, :]


def params(mib):
    return pltpu.CompilerParams(vmem_limit_bytes=mib * 1024 * 1024)


def cost(us):
    return pl.CostEstimate(flops=us * 10**9, bytes_accessed=us * 3 * 10**6, transcendentals=0)


def body(volume, first_weight, second_weight, cotangent):
    sx, sy, sz, chans = volume.shape
    n_gx, n_gy = lax.axis_size("gx"), lax.axis_size("gy")
    n_x, n_z = n_gx // 2, n_gy // 2
    scale = 1.0 / float(sx * n_gx * sy * n_gy * sz) ** 0.5
    strip = ROWS // n_gx
    block = strip // n_gy
    groups = max(-(-(i + 1) * strip // (3 * CH)) - i * strip // (3 * CH) for i in range(n_gx))
    full = sx * n_gx
    side = lax.rem(lax.axis_index("gy"), 2)
    perm = functools.partial(permutation, n_gx, n_gy)
    vmem = pl.BlockSpec(memory_space=pltpu.VMEM)

    def lines(v):
        return jnp.transpose(v, (1, 0, 2, 3)).reshape(-1, sz * chans)

    def ends(v):
        return lines(lax.dynamic_slice_in_dim(v, side * (sy - 2), 2, axis=1))

    edge = jnp.concatenate([ends(volume), ends(cotangent)])
    edge = lax.ppermute(edge, AX, perm(lambda x, c, z, y: (x, c, z - 1 + 2 * y, 1 - y)))
    pieces = pl.pallas_call(
        extend_kernel,
        out_shape=[jax.ShapeDtypeStruct((80, 512), BF16)] * 2,
        in_specs=[vmem] * 3,
        out_specs=[vmem] * 2,
        compiler_params=params(4),
        cost_estimate=cost(4),
        name="extend",
    )(lines(volume), lines(cotangent), edge)

    gathered = []
    for piece in pieces:
        same = []
        for dx in range(n_x):
            for dy in range(2):
                if dx == 0 and dy == 0:
                    same.append(piece)
                else:
                    same.append(lax.ppermute(piece, AX, perm(lambda x, c, z, y, dx=dx, dy=dy: (x - dx, c, z, y ^ dy))))
        gathered.append(same + [lax.ppermute(v, AX, perm(lambda x, c, z, y: (x, 1 - c, z, y))) for v in same])

    pre, hid = pl.pallas_call(
        functools.partial(hidden_kernel, n_x),
        out_shape=[
            jax.ShapeDtypeStruct((18 * full, 512), F32),
            jax.ShapeDtypeStruct((512, 16 * full), BF16),
        ],
        in_specs=[vmem] * (4 * n_x + 1),
        out_specs=[vmem] * 2,
        scratch_shapes=[pltpu.VMEM((3, 20, full, 512), BF16)],
        compiler_params=params(24),
        cost_estimate=cost(5),
        name="group_hidden",
    )(*gathered[0], first_weight)

    cot, mine, *sends = pl.pallas_call(
        functools.partial(gradient_kernel, n_x, n_z, groups, strip, block, scale),
        out_shape=[
            jax.ShapeDtypeStruct((3, 20, full, 512), BF16),
            jax.ShapeDtypeStruct((block, CH), F32),
        ]
        + [jax.ShapeDtypeStruct((block, CH), BF16)] * (n_z - 1),
        in_specs=[vmem] * (4 * n_x + 1),
        out_specs=[vmem] * (1 + n_z),
        scratch_shapes=[pltpu.VMEM((groups * 3 * CH + (0 if block % 8 == 0 else 16), CH), F32)],
        compiler_params=params(24),
        cost_estimate=cost(2),
        name="group_gradient",
    )(*gathered[1], hid)

    received = [
        lax.ppermute(v, AX, perm(lambda x, c, z, y, k=k: (x, c, z + k + 1, y))) for k, v in enumerate(sends)
    ]

    output, volume_grad = pl.pallas_call(
        local_kernel,
        out_shape=[jax.ShapeDtypeStruct((sy, sx, 512), BF16)] * 2,
        in_specs=[vmem] * 4,
        out_specs=[vmem] * 2,
        scratch_shapes=[
            pltpu.VMEM((3, 10, 16, 512), BF16),
            pltpu.VMEM((3, 12, 16, 512), BF16),
            pltpu.VMEM((3, 10, 16, 512), BF16),
            pltpu.VMEM((160, 512), F32),
        ],
        compiler_params=params(24),
        cost_estimate=cost(7),
        name="local_convolutions",
    )(pre, cot, first_weight, second_weight)

    def cells(v):
        return jnp.transpose(v.reshape(sy, sx, sz, chans), (1, 0, 2, 3))

    total = mine
    for v in received:
        total = total + v.astype(F32)
    return cells(output), cells(volume_grad), total.reshape(-1)


def solution(mesh):
    in_specs = (P("gx", "gy", None, None), P(), P(), P("gx", "gy", None, None))
    out_specs = (P("gx", "gy", None, None), P("gx", "gy", None, None), P(("gx", "gy")))
    return jax.shard_map(body, mesh=mesh, in_specs=in_specs, out_specs=out_specs, check_vma=False)
```

time: 51.2 us -> 39.4 us (0.77)
  Pallas kernels: 21.5 us -> 8.59 us
  starting transfers between devices: 14 us -> 18.1 us
  waiting for transfers between devices: 9.27 us -> 6.95 us
  local copies, waits for them, and re-layouts: 5.4 us -> 4.68 us
    pallas_call x1, Pallas kernels: 11.7 us -> 3.92 us  [body(): pl.pallas_call(local_kernel, out_shape=[jax.ShapeDtypeStruct((sy, sx, 512...]
    pallas_call x1 -> x3, Pallas kernels: 9.79 us -> 4.67 us  [the longest x1 3.27 us: body(): pl.pallas_call(functools.partial(hidden_kernel, n_x), out_shape=[jax.Shap...]
    ppermute x3 -> x6, starting transfers between devices: 3.55 us -> 6.17 us  [body(): lax.ppermute(piece, AX, perm(lambda x, c, z, y, dx=dx, dy=dy: (x - dx, c,...]
    ppermute x3, waiting for transfers between devices: 0.01 us -> 2.26 us  [body(): lax.ppermute(v, AX, perm(lambda x, c, z, y, k=k: (x, c, z + k + 1, y)))]
    unnamed x6 -> x5, local copies, waits for them, and re-layouts: 2.83 us -> 0.81 us
    another operation x3 -> x0, local copies, waits for them, and re-layouts: 1.8 us -> none  [body(): own = jnp.stack([lines(volume), lines(cotangent)])]
    transpose x1 -> x5, local copies, waits for them, and re-layouts: 0.75 us -> 2.51 us  [lines(): return jnp.transpose(v, (1, 0, 2, 3)).reshape(-1, sz * chans)]
    ppermute x1, waiting for transfers between devices: 1.89 us -> 0.16 us  [body(): lax.ppermute(edge, AX, perm(lambda x, c, z, y: (x, c, z - 1 + 2 * y, 1 -...]
  transfers between devices with their start and end apart: 11 -> 18, of which waited for: 6 -> 7; matrix products, arithmetic and copies ran while one was open for 1% -> 8% of each run, Pallas kernels for 23% -> 18%
where the time goes in v2:
time: 39.4 us; the launch traced here: 39.2 us
  starting transfers between devices  18.1 us (46%)
  Pallas kernels  8.59 us (22%)
  waiting for transfers between devices  6.95 us (18%)
  local copies, waits for them, and re-layouts  4.68 us (12%)
  between operations  0.77 us (2%)
    ppermute x6, starting transfers between devices, body(): lax.ppermute(piece, AX, perm(lambda x, c, z, y, dx=dx, dy=dy: (x - dx, c,...  6.17 us
    ppermute x1, starting transfers between devices, body(): lax.ppermute(edge, AX, perm(lambda x, c, z, y: (x, c, z - 1 + 2 * y, 1 -...  6.07 us
    ppermute x3, starting transfers between devices, body(): lax.ppermute(v, AX, perm(lambda x, c, z, y, k=k: (x, c, z + k + 1, y)))  4.88 us
    ppermute x6, waiting for transfers between devices, body(): lax.ppermute(piece, AX, perm(lambda x, c, z, y, dx=dx, dy=dy: (x - dx, c,...  4.51 us
    pallas_call x1, Pallas kernels, body(): pl.pallas_call(local_kernel, out_shape=[jax.ShapeDtypeStruct((sy, sx, 512...  3.92 us
    pallas_call x1, Pallas kernels, body(): pl.pallas_call(functools.partial(hidden_kernel, n_x), out_shape=[jax.Shap...  3.27 us
    transpose x5, local copies, waits for them, and re-layouts, lines(): return jnp.transpose(v, (1, 0, 2, 3)).reshape(-1, sz * chans)  2.51 us
    ppermute x3, waiting for transfers between devices, body(): lax.ppermute(v, AX, perm(lambda x, c, z, y, k=k: (x, c, z + k + 1, y)))  2.26 us
  transfers between devices with their start and end apart: 18, of which 7 were waited for; matrix products, arithmetic and copies ran while one was open for 8% of the time, Pallas kernels for 18%

profile of v2, /device:TPU:0, one launch (start us, length us, event | category | flops | bytes accessed | tf_op | source)
XLA Modules:
  0.0 39.2 jit_solution(16302734264525336818)
XLA Ops:
  0.6 0.8 %dynamic-slice_bitcast_fusion = (bf16[2,8,2,256]{3,2,0,1:T(2,128)(2,1)S(1)}, bf16[2,8,2,256]{3,2,0,1:T(2,128)(2,1)S(1)}) fusion(bf16[8,8,2,256]{3,2,1,0:T(2,128)(2,1)} %param.7, s32[]{:T(128)S(6)} %select_n.4, bf16[8,8,2,256]{3,2,1,0:T(2,128)(2,1)} %param.4), kind=kLoop, calls=%fused_computation.4 | loop fusion | bytes 65540 | tf_op jit(solution)/shard_map/transpose | solution.py:192
  1.4 6.1 %collective-permute-start = (bf16[32,512]{1,0:T(8,128)(2,1)S(1)}, bf16[32,512]{1,0:T(8,128)(2,1)S(1)}, u32[]{:S(2)}, u32[]{:S(2)}) collective-permute-start(bf16[32,512]{1,0:T(8,128)(2,1)S(1)} %pad_maximum_fusion), channel_id=1, source_target_pairs={{0,7},{1,2},{2,1},{3,4},{4,3},{5,6},{6,5},{7,0},{8,15},{9,10},{10,... | collective-permute-start | bytes 98312 | tf_op jit(solution)/shard_map/ppermute | solution.py:198
  7.5 0.9 %copy.8 = bf16[8,8,2,256]{3,1,2,0:T(8,128)(2,1)S(1)} copy(bf16[8,8,2,256]{3,2,0,1:T(2,128)(2,1)} %bitcast.26) | data formatting | bytes 131072 | tf_op jit(solution)/shard_map/transpose | solution.py:192
  8.4 0.9 %copy.7 = bf16[8,8,2,256]{3,1,2,0:T(8,128)(2,1)S(1)} copy(bf16[8,8,2,256]{3,2,0,1:T(2,128)(2,1)} %bitcast.27) | data formatting | bytes 131072 | tf_op jit(solution)/shard_map/transpose | solution.py:192
  9.2 0.2 collective-permute-done.edge
  9.4 0.1 collective-permute-start.4
  9.5 0.9 %collective-permute-start.3 = (bf16[80,512]{1,0:T(8,128)(2,1)S(1)}, bf16[80,512]{1,0:T(8,128)(2,1)S(1)}, u32[]{:S(2)}, u32[]{:S(2)}) collective-permute-start(bf16[80,512]{1,0:T(8,128)(2,1)S(1)} %get-tuple-element.14.refs_0_), channel_id=1, source_target_pairs={{0,17},{1,16},{2,19},{3,18},{4,21},{5,20},{6,23},{7,22},{8,25},{9,... | collective-permute-start | bytes 245768 | tf_op jit(solution)/shard_map/ppermute | solution.py:217
  10.4 0.9 %collective-permute-start.2 = (bf16[80,512]{1,0:T(8,128)(2,1)S(1)}, bf16[80,512]{1,0:T(8,128)(2,1)S(1)}, u32[]{:S(2)}, u32[]{:S(2)}) collective-permute-start(bf16[80,512]{1,0:T(8,128)(2,1)S(1)} %get-tuple-element.14.refs_0_), channel_id=1, source_target_pairs={{0,16},{1,17},{2,18},{3,19},{4,20},{5,21},{6,22},{7,23},{8,24},{9,... | collective-permute-start | bytes 245768 | tf_op jit(solution)/shard_map/ppermute | solution.py:217
  11.3 1.8 %collective-permute-start.1 = (bf16[80,512]{1,0:T(8,128)(2,1)S(1)}, bf16[80,512]{1,0:T(8,128)(2,1)S(1)}, u32[]{:S(2)}, u32[]{:S(2)}) collective-permute-start(bf16[80,512]{1,0:T(8,128)(2,1)S(1)} %get-tuple-element.14.refs_0_), channel_id=1, source_target_pairs={{0,1},{1,0},{2,3},{3,2},{4,5},{5,4},{6,7},{7,6},{8,9},{9,8},{10,11... | collective-permute-start | bytes 245768 | tf_op jit(solution)/shard_map/ppermute | solution.py:217
  13.1 1.1 %collective-permute-start.10 = (bf16[80,512]{1,0:T(8,128)(2,1)S(1)}, bf16[80,512]{1,0:T(8,128)(2,1)S(1)}, u32[]{:S(2)}, u32[]{:S(2)}) collective-permute-start(bf16[80,512]{1,0:T(8,128)(2,1)S(1)} %get-tuple-element.16.refs_0_), channel_id=1, source_target_pairs={{0,17},{1,16},{2,19},{3,18},{4,21},{5,20},{6,23},{7,22},{8,25},{9,... | collective-permute-start | bytes 245768 | tf_op jit(solution)/shard_map/ppermute | solution.py:217
  14.2 0.0 collective-permute-done.4.refs_4_
  14.2 0.6 %collective-permute-start.9 = (bf16[80,512]{1,0:T(8,128)(2,1)S(1)}, bf16[80,512]{1,0:T(8,128)(2,1)S(1)}, u32[]{:S(2)}, u32[]{:S(2)}) collective-permute-start(bf16[80,512]{1,0:T(8,128)(2,1)S(1)} %get-tuple-element.16.refs_0_), channel_id=1, source_target_pairs={{0,16},{1,17},{2,18},{3,19},{4,20},{5,21},{6,22},{7,23},{8,24},{9,... | collective-permute-start | bytes 245768 | tf_op jit(solution)/shard_map/ppermute | solution.py:217
  14.8 0.9 %collective-permute-done.3.refs_3_ = bf16[80,512]{1,0:T(8,128)(2,1)S(1)} collective-permute-done((bf16[80,512]{1,0:T(8,128)(2,1)S(1)}, bf16[80,512]{1,0:T(8,128)(2,1)S(1)}, u32[]{:S(2)}, u32[]{:S(2)}) %collective-permute-start.3) | collective-permute-done | bytes 81952 | tf_op jit(solution)/shard_map/ppermute | solution.py:217
  15.7 0.9 %collective-permute-start.8 = (bf16[80,512]{1,0:T(8,128)(2,1)S(1)}, bf16[80,512]{1,0:T(8,128)(2,1)S(1)}, u32[]{:S(2)}, u32[]{:S(2)}) collective-permute-start(bf16[80,512]{1,0:T(8,128)(2,1)S(1)} %get-tuple-element.16.refs_0_), channel_id=1, source_target_pairs={{0,1},{1,0},{2,3},{3,2},{4,5},{5,4},{6,7},{7,6},{8,9},{9,8},{10,11... | collective-permute-start | bytes 245768 | tf_op jit(solution)/shard_map/ppermute | solution.py:217
  16.6 0.8 %collective-permute-done.1.refs_1_ = bf16[80,512]{1,0:T(8,128)(2,1)S(1)} collective-permute-done((bf16[80,512]{1,0:T(8,128)(2,1)S(1)}, bf16[80,512]{1,0:T(8,128)(2,1)S(1)}, u32[]{:S(2)}, u32[]{:S(2)}) %collective-permute-start.1) | collective-permute-done | bytes 81952 | tf_op jit(solution)/shard_map/ppermute | solution.py:217
  17.4 1.9 %collective-permute-done.10.refs_3_ = bf16[80,512]{1,0:T(8,128)(2,1)S(1)} collective-permute-done((bf16[80,512]{1,0:T(8,128)(2,1)S(1)}, bf16[80,512]{1,0:T(8,128)(2,1)S(1)}, u32[]{:S(2)}, u32[]{:S(2)}) %collective-permute-start.10) | collective-permute-done | bytes 81952 | tf_op jit(solution)/shard_map/ppermute | solution.py:217
  19.3 0.2 collective-permute-done.9.refs_2_
  19.5 0.3 collective-permute-start.11
  19.9 0.7 %collective-permute-done.8.refs_1_ = bf16[80,512]{1,0:T(8,128)(2,1)S(1)} collective-permute-done((bf16[80,512]{1,0:T(8,128)(2,1)S(1)}, bf16[80,512]{1,0:T(8,128)(2,1)S(1)}, u32[]{:S(2)}, u32[]{:S(2)}) %collective-permute-start.8) | collective-permute-done | bytes 81952 | tf_op jit(solution)/shard_map/ppermute | solution.py:217
  20.5 0.5 %collective-permute-start.13 = (bf16[80,512]{1,0:T(8,128)(2,1)S(1)}, bf16[80,512]{1,0:T(8,128)(2,1)S(1)}, u32[]{:S(2)}, u32[]{:S(2)}) collective-permute-start(bf16[80,512]{1,0:T(8,128)(2,1)S(1)} %collective-permute-done.9.refs_2_), channel_id=1, source_target_pairs={{0,8},{1,9},{2,10},{3,11},{4,12},{5,13},{6,14},{7,15},{8,0},{9,1},... | collective-permute-start | bytes 245768 | tf_op jit(solution)/shard_map/ppermute | solution.py:218
  21.1 0.1 collective-permute-start.12
  21.1 3.3 %group_hidden.1 = (f32[576,512]{1,0:T(8,128)S(1)}, bf16[512,512]{1,0:T(8,128)(2,1)S(1)}) custom-call(bf16[80,512]{1,0:T(8,128)(2,1)S(1)} %get-tuple-element.14.refs_0_, bf16[80,512]{1,0:T(8,128)(2,1)S(1)} %collective-permute-done.1.refs_1_, bf16[80,512]{1,0:T(8,128)(2,1)S(1)} %collective-permute-done.2.refs_2_, ...), custom_call_target="tpu_custom_call" | custom-call | flops 5000000000 | bytes 15000000 | tf_op jit(solution)/shard_map/group_hidden/pallas_call | solution.py:220
  24.5 0.0 copy-start.1
  24.5 1.4 %group_gradient.1 = (bf16[3,20,32,512]{3,2,1,0:T(8,128)(2,1)S(1)}, f32[216,256]{1,0:T(8,128)S(1)}, bf16[216,256]{1,0:T(8,128)(2,1)S(1)}, bf16[216,256]{1,0:T(8,128)(2,1)S(1)}, bf16[216,256]{1,0:T(8,128)(2,1)S(1)}) custom-call(bf16[80,512]{1,0:T(8,128)(2,1)S(1)} %get-tuple-element.16.refs_0_, bf16[80,512]{1,0:T(8,128)(2,1)S(1)} %collective-permute-done.8.refs_1_, ...), custom_call_target="tpu_custom_call" | custom-call | flops 2000000000 | bytes 6000000 | tf_op jit(solution)/shard_map/group_gradient/pallas_call | solution.py:234
  25.9 0.5 %collective-permute-start.15 = (bf16[216,256]{1,0:T(8,128)(2,1)S(1)}, bf16[216,256]{1,0:T(8,128)(2,1)S(1)}, u32[]{:S(2)}, u32[]{:S(2)}) collective-permute-start(bf16[216,256]{1,0:T(8,128)(2,1)S(1)} %get-tuple-element.22), channel_id=1, source_target_pairs={{0,2},{1,3},{2,4},{3,5},{4,6},{5,7},{6,0},{7,1},{8,10},{9,11},{10,... | collective-permute-start | bytes 331784 | tf_op jit(solution)/shard_map/ppermute | solution.py:250
  26.4 4.4 %collective-permute-start.16 = (bf16[216,256]{1,0:T(8,128)(2,1)S(1)}, bf16[216,256]{1,0:T(8,128)(2,1)S(1)}, u32[]{:S(2)}, u32[]{:S(2)}) collective-permute-start(bf16[216,256]{1,0:T(8,128)(2,1)S(1)} %get-tuple-element.23), channel_id=1, source_target_pairs={{0,4},{1,5},{2,6},{3,7},{4,0},{5,1},{6,2},{7,3},{8,12},{9,13},{10,... | collective-permute-start | bytes 331784 | tf_op jit(solution)/shard_map/ppermute | solution.py:250
  30.7 3.9 %local_convolutions.1 = (bf16[8,8,512]{2,1,0:T(8,128)(2,1)S(1)}, bf16[8,8,512]{2,1,0:T(8,128)(2,1)S(1)}) custom-call(f32[576,512]{1,0:T(8,128)S(1)} %get-tuple-element.15.pre_ref, bf16[3,20,32,512]{3,2,1,0:T(8,128)(2,1)S(1)} %get-tuple-element.18.cot_ref, bf16[6912,256]{1,0:T(8,128)(2,1)S(1)} %copy-done, bf16[6912,256]{1,0:T(8,128)(2,1)S(1)} %copy-done.1), custom_call_target="tpu_custom_call" | custom-call | flops 7000000000 | bytes 21000000 | tf_op jit(solution)/shard_map/local_convolutions/pallas_call | solution.py:253
  34.7 0.7 %copy.17 = bf16[8,8,2,256]{3,2,0,1:T(2,128)(2,1)} copy(bf16[8,8,2,256]{3,1,2,0:T(8,128)(2,1)S(1)} %bitcast.24) | data formatting | bytes 131072 | tf_op jit(solution)/shard_map/reshape | solution.py:270
  35.4 0.7 %copy.16 = bf16[8,8,2,256]{3,2,0,1:T(2,128)(2,1)} copy(bf16[8,8,2,256]{3,1,2,0:T(8,128)(2,1)S(1)} %bitcast.23) | data formatting | bytes 131072 | tf_op jit(solution)/shard_map/reshape | solution.py:270
  36.0 2.3 %collective-permute-done.16 = bf16[216,256]{1,0:T(8,128)(2,1)S(1)} collective-permute-done((bf16[216,256]{1,0:T(8,128)(2,1)S(1)}, bf16[216,256]{1,0:T(8,128)(2,1)S(1)}, u32[]{:S(2)}, u32[]{:S(2)}) %collective-permute-start.16) | collective-permute-done | bytes 110624 | tf_op jit(solution)/shard_map/ppermute | solution.py:250
  38.3 0.1 add_bitcast_fusion
  38.4 0.8 %copy.13 = f32[27,2,8,128]{3,1,2,0:T(2,128)} copy(f32[27,2,8,128]{3,2,1,0:T(8,128)S(1)} %add_bitcast_fusion) | data formatting | bytes 442368
  (22 shorter events, 0.1 us)
Async XLA Ops:
  1.4 8.0 %collective-permute-start = (bf16[32,512]{1,0:T(8,128)(2,1)S(1)}, bf16[32,512]{1,0:T(8,128)(2,1)S(1)}, u32[]{:S(2)}, u32[]{:S(2)}) collective-permute-start(bf16[32,512]{1,0:T(8,128)(2,1)S(1)} %pad_maximum_fusion), channel_id=1, source_target_pairs={{0,7},{1,2},{2,1},{3,4},{4,3},{5,6},{6,5},{7,0},{8,15},{9,10},{10,... | collective-permute-start | bytes 98312 | tf_op jit(solution)/shard_map/ppermute | solution.py:198
  9.4 11.7 %copy-start = (bf16[6912,256]{1,0:T(8,128)(2,1)S(1)}, bf16[6912,256]{1,0:T(8,128)(2,1)}, u32[]{:S(2)}) copy-start(bf16[6912,256]{1,0:T(8,128)(2,1)} %w1.1) | copy-start | bytes 10616836
  9.4 4.7 %collective-permute-start.4 = (bf16[80,512]{1,0:T(8,128)(2,1)S(1)}, bf16[80,512]{1,0:T(8,128)(2,1)S(1)}, u32[]{:S(2)}, u32[]{:S(2)}) collective-permute-start(bf16[80,512]{1,0:T(8,128)(2,1)S(1)} %get-tuple-element.14.refs_0_), channel_id=1, source_target_pairs={{0,8},{1,9},{2,10},{3,11},{4,12},{5,13},{6,14},{7,15},{8,0},{9,1},... | collective-permute-start | bytes 245768 | tf_op jit(solution)/shard_map/ppermute | solution.py:218
  9.5 6.2 %collective-permute-start.3 = (bf16[80,512]{1,0:T(8,128)(2,1)S(1)}, bf16[80,512]{1,0:T(8,128)(2,1)S(1)}, u32[]{:S(2)}, u32[]{:S(2)}) collective-permute-start(bf16[80,512]{1,0:T(8,128)(2,1)S(1)} %get-tuple-element.14.refs_0_), channel_id=1, source_target_pairs={{0,17},{1,16},{2,19},{3,18},{4,21},{5,20},{6,23},{7,22},{8,25},{9,... | collective-permute-start | bytes 245768 | tf_op jit(solution)/shard_map/ppermute | solution.py:217
  10.4 6.2 %collective-permute-start.2 = (bf16[80,512]{1,0:T(8,128)(2,1)S(1)}, bf16[80,512]{1,0:T(8,128)(2,1)S(1)}, u32[]{:S(2)}, u32[]{:S(2)}) collective-permute-start(bf16[80,512]{1,0:T(8,128)(2,1)S(1)} %get-tuple-element.14.refs_0_), channel_id=1, source_target_pairs={{0,16},{1,17},{2,18},{3,19},{4,20},{5,21},{6,22},{7,23},{8,24},{9,... | collective-permute-start | bytes 245768 | tf_op jit(solution)/shard_map/ppermute | solution.py:217
  11.3 6.1 %collective-permute-start.1 = (bf16[80,512]{1,0:T(8,128)(2,1)S(1)}, bf16[80,512]{1,0:T(8,128)(2,1)S(1)}, u32[]{:S(2)}, u32[]{:S(2)}) collective-permute-start(bf16[80,512]{1,0:T(8,128)(2,1)S(1)} %get-tuple-element.14.refs_0_), channel_id=1, source_target_pairs={{0,1},{1,0},{2,3},{3,2},{4,5},{5,4},{6,7},{7,6},{8,9},{9,8},{10,11... | collective-permute-start | bytes 245768 | tf_op jit(solution)/shard_map/ppermute | solution.py:217
  13.1 6.3 %collective-permute-start.10 = (bf16[80,512]{1,0:T(8,128)(2,1)S(1)}, bf16[80,512]{1,0:T(8,128)(2,1)S(1)}, u32[]{:S(2)}, u32[]{:S(2)}) collective-permute-start(bf16[80,512]{1,0:T(8,128)(2,1)S(1)} %get-tuple-element.16.refs_0_), channel_id=1, source_target_pairs={{0,17},{1,16},{2,19},{3,18},{4,21},{5,20},{6,23},{7,22},{8,25},{9,... | collective-permute-start | bytes 245768 | tf_op jit(solution)/shard_map/ppermute | solution.py:217
  14.2 5.4 %collective-permute-start.9 = (bf16[80,512]{1,0:T(8,128)(2,1)S(1)}, bf16[80,512]{1,0:T(8,128)(2,1)S(1)}, u32[]{:S(2)}, u32[]{:S(2)}) collective-permute-start(bf16[80,512]{1,0:T(8,128)(2,1)S(1)} %get-tuple-element.16.refs_0_), channel_id=1, source_target_pairs={{0,16},{1,17},{2,18},{3,19},{4,20},{5,21},{6,22},{7,23},{8,24},{9,... | collective-permute-start | bytes 245768 | tf_op jit(solution)/shard_map/ppermute | solution.py:217
  15.7 4.9 %collective-permute-start.8 = (bf16[80,512]{1,0:T(8,128)(2,1)S(1)}, bf16[80,512]{1,0:T(8,128)(2,1)S(1)}, u32[]{:S(2)}, u32[]{:S(2)}) collective-permute-start(bf16[80,512]{1,0:T(8,128)(2,1)S(1)} %get-tuple-element.16.refs_0_), channel_id=1, source_target_pairs={{0,1},{1,0},{2,3},{3,2},{4,5},{5,4},{6,7},{7,6},{8,9},{9,8},{10,11... | collective-permute-start | bytes 245768 | tf_op jit(solution)/shard_map/ppermute | solution.py:217
  16.6 4.0 %collective-permute-start.7 = (bf16[80,512]{1,0:T(8,128)(2,1)S(1)}, bf16[80,512]{1,0:T(8,128)(2,1)S(1)}, u32[]{:S(2)}, u32[]{:S(2)}) collective-permute-start(bf16[80,512]{1,0:T(8,128)(2,1)S(1)} %collective-permute-done.3.refs_3_), channel_id=1, source_target_pairs={{0,8},{1,9},{2,10},{3,11},{4,12},{5,13},{6,14},{7,15},{8,0},{9,1},... | collective-permute-start | bytes 245768 | tf_op jit(solution)/shard_map/ppermute | solution.py:218
  17.4 3.6 %collective-permute-start.6 = (bf16[80,512]{1,0:T(8,128)(2,1)S(1)}, bf16[80,512]{1,0:T(8,128)(2,1)S(1)}, u32[]{:S(2)}, u32[]{:S(2)}) collective-permute-start(bf16[80,512]{1,0:T(8,128)(2,1)S(1)} %collective-permute-done.2.refs_2_), channel_id=1, source_target_pairs={{0,8},{1,9},{2,10},{3,11},{4,12},{5,13},{6,14},{7,15},{8,0},{9,1},... | collective-permute-start | bytes 245768 | tf_op jit(solution)/shard_map/ppermute | solution.py:218
  19.3 1.8 %collective-permute-start.5 = (bf16[80,512]{1,0:T(8,128)(2,1)S(1)}, bf16[80,512]{1,0:T(8,128)(2,1)S(1)}, u32[]{:S(2)}, u32[]{:S(2)}) collective-permute-start(bf16[80,512]{1,0:T(8,128)(2,1)S(1)} %collective-permute-done.1.refs_1_), channel_id=1, source_target_pairs={{0,8},{1,9},{2,10},{3,11},{4,12},{5,13},{6,14},{7,15},{8,0},{9,1},... | collective-permute-start | bytes 245768 | tf_op jit(solution)/shard_map/ppermute | solution.py:218
  19.5 4.9 %collective-permute-start.11 = (bf16[80,512]{1,0:T(8,128)(2,1)S(1)}, bf16[80,512]{1,0:T(8,128)(2,1)S(1)}, u32[]{:S(2)}, u32[]{:S(2)}) collective-permute-start(bf16[80,512]{1,0:T(8,128)(2,1)S(1)} %get-tuple-element.16.refs_0_), channel_id=1, source_target_pairs={{0,8},{1,9},{2,10},{3,11},{4,12},{5,13},{6,14},{7,15},{8,0},{9,1},... | collective-permute-start | bytes 245768 | tf_op jit(solution)/shard_map/ppermute | solution.py:218
  20.5 3.9 %collective-permute-start.14 = (bf16[80,512]{1,0:T(8,128)(2,1)S(1)}, bf16[80,512]{1,0:T(8,128)(2,1)S(1)}, u32[]{:S(2)}, u32[]{:S(2)}) collective-permute-start(bf16[80,512]{1,0:T(8,128)(2,1)S(1)} %collective-permute-done.10.refs_3_), channel_id=1, source_target_pairs={{0,8},{1,9},{2,10},{3,11},{4,12},{5,13},{6,14},{7,15},{8,0},{9,1},... | collective-permute-start | bytes 245768 | tf_op jit(solution)/shard_map/ppermute | solution.py:218
  20.5 3.9 %collective-permute-start.13 = (bf16[80,512]{1,0:T(8,128)(2,1)S(1)}, bf16[80,512]{1,0:T(8,128)(2,1)S(1)}, u32[]{:S(2)}, u32[]{:S(2)}) collective-permute-start(bf16[80,512]{1,0:T(8,128)(2,1)S(1)} %collective-permute-done.9.refs_2_), channel_id=1, source_target_pairs={{0,8},{1,9},{2,10},{3,11},{4,12},{5,13},{6,14},{7,15},{8,0},{9,1},... | collective-permute-start | bytes 245768 | tf_op jit(solution)/shard_map/ppermute | solution.py:218
  21.1 3.4 %collective-permute-start.12 = (bf16[80,512]{1,0:T(8,128)(2,1)S(1)}, bf16[80,512]{1,0:T(8,128)(2,1)S(1)}, u32[]{:S(2)}, u32[]{:S(2)}) collective-permute-start(bf16[80,512]{1,0:T(8,128)(2,1)S(1)} %collective-permute-done.8.refs_1_), channel_id=1, source_target_pairs={{0,8},{1,9},{2,10},{3,11},{4,12},{5,13},{6,14},{7,15},{8,0},{9,1},... | collective-permute-start | bytes 245768 | tf_op jit(solution)/shard_map/ppermute | solution.py:218
  24.5 6.3 %copy-start.1 = (bf16[6912,256]{1,0:T(8,128)(2,1)S(1)}, bf16[6912,256]{1,0:T(8,128)(2,1)}, u32[]{:S(2)}) copy-start(bf16[6912,256]{1,0:T(8,128)(2,1)} %w2.1) | copy-start | bytes 10616836
  25.9 10.2 %collective-permute-start.15 = (bf16[216,256]{1,0:T(8,128)(2,1)S(1)}, bf16[216,256]{1,0:T(8,128)(2,1)S(1)}, u32[]{:S(2)}, u32[]{:S(2)}) collective-permute-start(bf16[216,256]{1,0:T(8,128)(2,1)S(1)} %get-tuple-element.22), channel_id=1, source_target_pairs={{0,2},{1,3},{2,4},{3,5},{4,6},{5,7},{6,0},{7,1},{8,10},{9,11},{10,... | collective-permute-start | bytes 331784 | tf_op jit(solution)/shard_map/ppermute | solution.py:250
  26.4 11.9 %collective-permute-start.16 = (bf16[216,256]{1,0:T(8,128)(2,1)S(1)}, bf16[216,256]{1,0:T(8,128)(2,1)S(1)}, u32[]{:S(2)}, u32[]{:S(2)}) collective-permute-start(bf16[216,256]{1,0:T(8,128)(2,1)S(1)} %get-tuple-element.23), channel_id=1, source_target_pairs={{0,4},{1,5},{2,6},{3,7},{4,0},{5,1},{6,2},{7,3},{8,12},{9,13},{10,... | collective-permute-start | bytes 331784 | tf_op jit(solution)/shard_map/ppermute | solution.py:250
  30.7 7.6 %collective-permute-start.17 = (bf16[216,256]{1,0:T(8,128)(2,1)S(1)}, bf16[216,256]{1,0:T(8,128)(2,1)S(1)}, u32[]{:S(2)}, u32[]{:S(2)}) collective-permute-start(bf16[216,256]{1,0:T(8,128)(2,1)S(1)} %get-tuple-element.24), channel_id=1, source_target_pairs={{0,6},{1,7},{2,0},{3,1},{4,2},{5,3},{6,4},{7,5},{8,14},{9,15},{10,... | collective-permute-start | bytes 331784 | tf_op jit(solution)/shard_map/ppermute | solution.py:250

commit v3 on v2

v3 whole, which is shorter than its diff:
```python
import functools

import jax
import jax.numpy as jnp
from jax import lax
from jax.experimental import pallas as pl
from jax.experimental.pallas import tpu as pltpu
from jax.sharding import PartitionSpec as P

AX = ("gx", "gy")
F32 = jnp.float32
BF16 = jnp.bfloat16
CH = 256
ROWS = 27 * CH


def permutation(n_gx, n_gy, move):
    pairs = []
    for i in range(n_gx):
        for j in range(n_gy):
            x, c, z, y = move(i // 2, i % 2, j // 2, j % 2)
            x, z = x % (n_gx // 2), z % (n_gy // 2)
            pairs.append((i * n_gy + j, (x * 2 + c) * n_gy + z * 2 + y))
    return pairs


def dot(a, b):
    return lax.dot_general(a, b, (((1,), (0,)), ((), ())), preferred_element_type=F32)


def dot_t(a, b):
    return lax.dot_general(a, b, (((1,), (1,)), ((), ())), preferred_element_type=F32)


def shifted(v, by):
    if by == 0:
        return v
    axis, n = v.ndim - 2, v.shape[-2]
    if by > 0:
        parts = [lax.slice_in_dim(v, by, n, axis=axis), lax.slice_in_dim(v, 0, by, axis=axis)]
    else:
        parts = [lax.slice_in_dim(v, n + by, n, axis=axis), lax.slice_in_dim(v, 0, n + by, axis=axis)]
    return jnp.concatenate(parts, axis=axis)


def window(v, core):
    n = v.shape[-2]
    first = jnp.concatenate([v[..., n - 4 :, :], v[..., :12, :]], axis=-2)
    return jnp.where(core == 0, first, v[..., 4:20, :])


def ring(n_x, core, mine, theirs, rows):
    parts = []
    for dx in range(n_x):
        a, b = (ref[first : first + 16, :].astype(F32).reshape(2, 8, 512) for ref, first in (rows(mine, dx), rows(theirs, dx)))
        parts += [jnp.where(core == 0, a, b), jnp.where(core == 0, b, a)]
    return jnp.concatenate(parts, axis=1)


def assemble(n_x, which, pieces, put):
    _, core, _, side = place()
    n = 2 * n_x
    for dy in range(2):
        slot = side if dy == 0 else 1 - side
        for pair in range(4):
            rows = lambda refs, dx: (refs[dx * 2 + dy], which * 64 + pair * 16)
            put(which, 8 * slot + 2 * pair, ring(n_x, core, pieces[:n], pieces[n:], rows))


def putter(vol, cot):
    def put(which, row, line):
        for s in range(3):
            (vol, cot)[which][s, pl.ds(row, 2)] = shifted(line, (s - 1, 1 - s)[which]).astype(BF16)

    return put


def both(w):
    return jnp.concatenate([w[CH:], w[: 2 * CH]], axis=1)


def place():
    gx, gy = lax.axis_index("gx"), lax.axis_index("gy")
    return gx, lax.rem(gx, 2), lax.div(gy, 2), lax.rem(gy, 2)


def edge_kernel(n_x, *refs):
    *pieces, first = refs
    side = place()[3]
    for dx in range(n_x):
        for which in range(2):
            a, b = pieces[dx * 2], pieces[dx * 2 + 1]
            out = slice(dx * 32 + which * 16, dx * 32 + which * 16 + 16)
            rows = slice(which * 64, which * 64 + 16)
            first[out, :] = jnp.where(side == 0, a[rows, :], b[rows, :])


def later_kernel(lines, _, out):
    out[...] = lines[...]


def inner_kernel(n_x, *refs):
    *pieces, w_ref, pre, vol, cot = refs
    full = 16 * n_x
    put = putter(vol, cot)
    assemble(n_x, 0, pieces, put)
    for k in range(9):
        left = vol[k // 3, k % 3 : k % 3 + 14].reshape(14 * full, 512)
        term = dot(left, both(w_ref[k * 768 : k * 768 + 768, :]))
        pre[...] = term if k == 0 else pre[...] + term
    assemble(n_x, 1, pieces, put)


def gradient_kernel(n_x, n_z, groups, strip, block, scale, *refs):
    beyond_a, beyond_b, w_ref, pre, _, _, vol, cot, own_out, *sends, hid, grad, flat = refs
    gx, core, z, side = place()
    full = 16 * n_x
    put = putter(vol, cot)
    for which in range(2):
        put(which, 16, ring(n_x, core, beyond_a, beyond_b, lambda ref, dx: (ref, dx * 32 + which * 16)))
    outer = None
    for k in range(9):
        left = vol[k // 3, 14 + k % 3 : 16 + k % 3].reshape(2 * full, 512)
        term = dot(left, both(w_ref[k * 768 : k * 768 + 768, :]))
        outer = term if k == 0 else outer + term
    inner = jnp.concatenate([pre[...], outer], axis=0)
    hid[...] = (inner * jax.nn.sigmoid(inner)).T.astype(BF16)
    first = lax.div(gx * strip, 3 * CH)
    for k in range(groups):
        ab = jnp.minimum(first + k, 8)
        right = cot[lax.div(ab, 3), pl.ds(2 - lax.rem(ab, 3), 16)].reshape(16 * full, 512)
        product = dot(hid[...], right) * scale
        at = k * 3 * CH
        grad[at : at + CH, :] = product[:CH, CH:]
        grad[at + CH : at + 2 * CH, :] = product[:CH, :CH] + product[CH:, CH:]
        grad[at + 2 * CH : at + 3 * CH, :] = product[CH:, :CH]

    for k in range(n_z):
        start = gx * strip + (2 * lax.rem(z + k, n_z) + side) * block - first * 3 * CH
        if block % 8 == 0:
            value = grad[pl.ds(pl.multiple_of(start, 8), block), :]
        else:
            over = lax.rem(start, 8)
            rows = (block + 7 + 7) // 8 * 8
            value = grad[pl.ds(pl.multiple_of(start - over, 8), rows), :]
            value = pltpu.roll(value, lax.rem(rows - over, rows), 0)[:block]
        for half in range(2):
            flat[pl.ds(half, block, stride=2), :] = value[:, half * 128 : half * 128 + 128]
        if k == 0:
            own_out[...] = flat[...]
        else:
            sends[k - 1][...] = flat[...].astype(BF16)


def last_kernel(n_x, *refs):
    *pieces, out = refs
    _, core, _, side = place()
    n = 2 * n_x
    for which in range(2):
        low, high = (
            ring(n_x, core, pieces[:n], pieces[n:], lambda refs, dx: (refs[dx * 2 + dy], which * 64 + 48)) for dy in range(2)
        )
        lines = window(jnp.where(side == 0, high, low), core)
        out[which * 32 : which * 32 + 32, :] = lines.reshape(32, 512).astype(BF16)


def local_kernel(vol_ref, cot_ref, before_ref, w1, w2, out_ref, vgrad_ref, vol, hid, cot, thr, acc):
    _, core, _, side = place()

    def cut(which, ref):
        lines = window(ref[1, pl.ds(side * 8, 10)].astype(F32), core)
        before = before_ref[which * 32 : which * 32 + 32, :].astype(F32).reshape(2, 16, 512)
        before = jnp.where(side == 0, before, window(ref[1, 6:8].astype(F32), core))
        return jnp.concatenate([before, lines], axis=0)

    v, c = cut(0, vol_ref), cut(1, cot_ref)
    for s in range(3):
        vol[s] = shifted(v, s - 1).astype(BF16)
        cot[s] = shifted(c, s - 1).astype(BF16)

    for k in range(9):
        left = vol[k // 3, k % 3 : k % 3 + 10].reshape(160, 512)
        term = dot(left, both(w1[k * 768 : k * 768 + 768, :]))
        acc[...] = term if k == 0 else acc[...] + term
    pre = acc[...].reshape(10, 16, 512)
    sig = jax.nn.sigmoid(pre)
    for s in range(3):
        hid[s] = shifted(pre * sig, s - 1).astype(BF16)
    slope = sig * (1.0 + pre * (1.0 - sig))

    for k in range(9):
        left = cot[k // 3, k % 3 : k % 3 + 10].reshape(160, 512)
        term = dot_t(left, both(w2[(8 - k) * 768 : (8 - k) * 768 + 768, :]))
        acc[...] = term if k == 0 else acc[...] + term
    through = acc[...].reshape(10, 16, 512) * slope
    for s in range(3):
        thr[s] = shifted(through, s - 1).astype(BF16)

    for k in range(9):
        left = hid[k // 3, k % 3 : k % 3 + 8].reshape(128, 512)
        term = dot(left, both(w2[k * 768 : k * 768 + 768, :]))
        acc[:128] = term if k == 0 else acc[:128] + term
    out_ref[...] = acc[:128].reshape(8, 16, 512)[:, 4:12].astype(BF16)

    for k in range(9):
        left = thr[k // 3, k % 3 : k % 3 + 8].reshape(128, 512)
        term = dot_t(left, both(w1[(8 - k) * 768 : (8 - k) * 768 + 768, :]))
        acc[:128] = term if k == 0 else acc[:128] + term
    vgrad_ref[...] = acc[:128].reshape(8, 16, 512)[:, 4:12].astype(BF16)


def params(mib):
    return pltpu.CompilerParams(vmem_limit_bytes=mib * 1024 * 1024)


def cost(us):
    return pl.CostEstimate(flops=us * 10**9, bytes_accessed=us * 3 * 10**6, transcendentals=0)


def body(volume, first_weight, second_weight, cotangent):
    sx, sy, sz, chans = volume.shape
    n_gx, n_gy = lax.axis_size("gx"), lax.axis_size("gy")
    n_x, n_z = n_gx // 2, n_gy // 2
    scale = 1.0 / float(sx * n_gx * sy * n_gy * sz) ** 0.5
    strip = ROWS // n_gx
    block = strip // n_gy
    groups = max(-(-(i + 1) * strip // (3 * CH)) - i * strip // (3 * CH) for i in range(n_gx))
    full = sx * n_gx
    perm = functools.partial(permutation, n_gx, n_gy)
    vmem = pl.BlockSpec(memory_space=pltpu.VMEM)

    def lines(v):
        return jnp.transpose(v, (1, 0, 2, 3)).reshape(-1, sz * chans)

    def across(v):
        return lax.ppermute(v, AX, perm(lambda x, c, z, y: (x, 1 - c, z, y)))

    own = jnp.concatenate([lines(volume), lines(cotangent)])
    pieces = [own]
    for dx in range(n_x):
        for dy in range(2):
            if dx or dy:
                pieces.append(lax.ppermute(own, AX, perm(lambda x, c, z, y, dx=dx, dy=dy: (x - dx, c, z, y ^ dy))))
    first = pl.pallas_call(
        functools.partial(edge_kernel, n_x),
        out_shape=jax.ShapeDtypeStruct((n_x * 32, 512), BF16),
        in_specs=[vmem] * (2 * n_x),
        out_specs=vmem,
        compiler_params=params(4),
        cost_estimate=cost(4),
        name="edges",
    )(*pieces)
    pieces += [across(v) for v in pieces]
    beyond = lax.ppermute(first, AX, perm(lambda x, c, z, y: (x, c, z - 1, y)))

    last = pl.pallas_call(
        functools.partial(last_kernel, n_x),
        out_shape=jax.ShapeDtypeStruct((64, 512), BF16),
        in_specs=[vmem] * (4 * n_x),
        out_specs=vmem,
        compiler_params=params(4),
        cost_estimate=cost(0),
        name="last_lines",
    )(*pieces)
    before = lax.ppermute(last, AX, perm(lambda x, c, z, y: (x, c, z + 1, y)))

    plane = jax.ShapeDtypeStruct((3, 18, full, 512), BF16)
    pre, vol, cot = pl.pallas_call(
        functools.partial(inner_kernel, n_x),
        out_shape=[jax.ShapeDtypeStruct((14 * full, 512), F32), plane, plane],
        in_specs=[vmem] * (4 * n_x + 1),
        out_specs=[vmem] * 3,
        compiler_params=params(24),
        cost_estimate=cost(5),
        name="plane_inner",
    )(*pieces, first_weight)
    beyond = pl.pallas_call(
        later_kernel,
        out_shape=jax.ShapeDtypeStruct(beyond.shape, BF16),
        in_specs=[vmem] * 2,
        out_specs=vmem,
        compiler_params=params(4),
        cost_estimate=cost(0),
        name="later",
    )(beyond, pre)
    vol, cot, mine, *sends = pl.pallas_call(
        functools.partial(gradient_kernel, n_x, n_z, groups, strip, block, scale),
        out_shape=[plane, plane, jax.ShapeDtypeStruct((2 * block, 128), F32)]
        + [jax.ShapeDtypeStruct((2 * block, 128), BF16)] * (n_z - 1),
        in_specs=[vmem] * 6,
        out_specs=[vmem] * (2 + n_z),
        input_output_aliases={4: 0, 5: 1},
        scratch_shapes=[
            pltpu.VMEM((512, 16 * full), BF16),
            pltpu.VMEM((groups * 3 * CH + (0 if block % 8 == 0 else 16), CH), F32),
            pltpu.VMEM((2 * block, 128), F32),
        ],
        compiler_params=params(24),
        cost_estimate=cost(0),
        name="plane_gradient",
    )(beyond, across(beyond), first_weight, pre, vol, cot)

    received = [
        lax.ppermute(sends[k - 1], AX, perm(lambda x, c, z, y, k=k: (x, c, z + k, y)))
        for k in sorted(range(1, n_z), key=lambda k: k != n_z // 2)
    ]

    output, volume_grad = pl.pallas_call(
        local_kernel,
        out_shape=[jax.ShapeDtypeStruct((sy, sx, 512), BF16)] * 2,
        in_specs=[vmem] * 5,
        out_specs=[vmem] * 2,
        scratch_shapes=[
            pltpu.VMEM((3, 12, 16, 512), BF16),
            pltpu.VMEM((3, 10, 16, 512), BF16),
            pltpu.VMEM((3, 12, 16, 512), BF16),
            pltpu.VMEM((3, 10, 16, 512), BF16),
            pltpu.VMEM((160, 512), F32),
        ],
        compiler_params=params(24),
        cost_estimate=cost(0),
        name="local_convolutions",
    )(vol, cot, before, first_weight, second_weight)

    def cells(v):
        return jnp.transpose(v.reshape(sy, sx, sz, chans), (1, 0, 2, 3))

    total = mine
    for v in received:
        total = total + v.astype(F32)
    return cells(output), cells(volume_grad), total.reshape(-1)


def solution(mesh):
    in_specs = (P("gx", "gy", None, None), P(), P(), P("gx", "gy", None, None))
    out_specs = (P("gx", "gy", None, None), P("gx", "gy", None, None), P(("gx", "gy")))
    return jax.shard_map(body, mesh=mesh, in_specs=in_specs, out_specs=out_specs, check_vma=False)
```

time: 39.4 us -> 36.7 us (0.931)
  starting transfers between devices: 18.1 us -> 15.5 us
  local copies, waits for them, and re-layouts: 4.68 us -> 2.49 us
  Pallas kernels: 8.59 us -> 9.52 us
  other arithmetic: 0.07 us -> 0.75 us
  waiting for transfers between devices: 6.95 us -> 7.49 us
    ppermute x18 -> x13, starting transfers between devices: 18.1 us -> 15.5 us  [the longest x3 6.59 us: body(): lax.ppermute(sends[k - 1], AX, perm(lambda x, c, z, y, k=k: (x, c, z + k,...]
    reshape x2 -> x0, local copies, waits for them, and re-layouts: 1.36 us -> none  [cells(): return jnp.transpose(v.reshape(sy, sx, sz, chans), (1, 0, 2, 3))]
    unnamed x5 -> x4, local copies, waits for them, and re-layouts: 0.81 us -> 0.01 us
    pallas_call x1, Pallas kernels: 3.92 us -> 4.72 us  [body(): pl.pallas_call(local_kernel, out_shape=[jax.ShapeDtypeStruct((sy, sx, 512...]
    transpose x5 -> x2, local copies, waits for them, and re-layouts: 2.51 us -> 1.73 us  [lines(): return jnp.transpose(v, (1, 0, 2, 3)).reshape(-1, sz * chans)]
    transpose x0 -> x1, local copies, waits for them, and re-layouts: none -> 0.75 us  [cells(): return jnp.transpose(v.reshape(sy, sx, sz, chans), (1, 0, 2, 3))]
    reshape x0 -> x1, other arithmetic: none -> 0.74 us  [body(): return (cells(output), cells(volume_grad), total.reshape(-1))]
    pallas_call x1, Pallas kernels: 1.39 us -> 1.97 us  [body(): pl.pallas_call(functools.partial(gradient_kernel, n_x, n_z, groups, strip...]
  transfers between devices with their start and end apart: 18 -> 13, of which waited for: 7 -> 4; matrix products, arithmetic and copies ran while one was open for 8% -> 2% of each run, Pallas kernels for 18% -> 26%
where the time goes in v3:
time: 36.7 us; the launch traced here: 36.5 us
  starting transfers between devices  15.5 us (42%)
  Pallas kernels  9.52 us (26%)
  waiting for transfers between devices  7.49 us (20%)
  local copies, waits for them, and re-layouts  2.49 us (7%)
  other arithmetic  0.75 us (2%)
  between operations  0.74 us (2%)
    ppermute x3, starting transfers between devices, body(): lax.ppermute(sends[k - 1], AX, perm(lambda x, c, z, y, k=k: (x, c, z + k,...  6.59 us
    ppermute x3, waiting for transfers between devices, body(): lax.ppermute(own, AX, perm(lambda x, c, z, y, dx=dx, dy=dy: (x - dx, c, z...  5.91 us
    pallas_call x1, Pallas kernels, body(): pl.pallas_call(local_kernel, out_shape=[jax.ShapeDtypeStruct((sy, sx, 512...  4.72 us
    ppermute x3, starting transfers between devices, body(): lax.ppermute(own, AX, perm(lambda x, c, z, y, dx=dx, dy=dy: (x - dx, c, z...  4.6 us
    ppermute x1, starting transfers between devices, body(): beyond = lax.ppermute(first, AX, perm(lambda x, c, z, y: (x, c, z - 1, y)))  3.65 us
    pallas_call x1, Pallas kernels, body(): pl.pallas_call(functools.partial(inner_kernel, n_x), out_shape=[jax.Shape...  2.72 us
    pallas_call x1, Pallas kernels, body(): pl.pallas_call(functools.partial(gradient_kernel, n_x, n_z, groups, strip...  1.97 us
    transpose x2, local copies, waits for them, and re-layouts, lines(): return jnp.transpose(v, (1, 0, 2, 3)).reshape(-1, sz * chans)  1.73 us
  transfers between devices with their start and end apart: 13, of which 4 were waited for; matrix products, arithmetic and copies ran while one was open for 2% of the time, Pallas kernels for 26%

profile of v3, /device:TPU:0, one launch (start us, length us, event | category | flops | bytes accessed | tf_op | source)
XLA Modules:
  0.0 36.5 jit_solution(17151769345302418793)
XLA Ops:
  0.6 0.9 %copy.9 = bf16[8,8,2,256]{3,1,2,0:T(8,128)(2,1)S(1)} copy(bf16[8,8,2,256]{3,2,0,1:T(2,128)(2,1)} %bitcast.16) | data formatting | bytes 131072 | tf_op jit(solution)/shard_map/transpose | solution.py:233
  1.5 0.9 %copy.10 = bf16[8,8,2,256]{3,1,2,0:T(8,128)(2,1)S(1)} copy(bf16[8,8,2,256]{3,2,0,1:T(2,128)(2,1)} %bitcast.17) | data formatting | bytes 131072 | tf_op jit(solution)/shard_map/transpose | solution.py:233
  2.4 0.0 copy-start
  2.4 4.0 %collective-permute-start.2 = (bf16[128,512]{1,0:T(8,128)(2,1)S(1)}, bf16[128,512]{1,0:T(8,128)(2,1)S(1)}, u32[]{:S(2)}, u32[]{:S(2)}) collective-permute-start(bf16[128,512]{1,0:T(8,128)(2,1)S(1)} %pad_maximum_fusion.refs_0_), channel_id=1, source_target_pairs={{0,17},{1,16},{2,19},{3,18},{4,21},{5,20},{6,23},{7,22},{8,25},{9,... | collective-permute-start | bytes 393224 | tf_op jit(solution)/shard_map/ppermute | solution.py:243
  6.4 0.5 %collective-permute-start.1 = (bf16[128,512]{1,0:T(8,128)(2,1)S(1)}, bf16[128,512]{1,0:T(8,128)(2,1)S(1)}, u32[]{:S(2)}, u32[]{:S(2)}) collective-permute-start(bf16[128,512]{1,0:T(8,128)(2,1)S(1)} %pad_maximum_fusion.refs_0_), channel_id=1, source_target_pairs={{0,16},{1,17},{2,18},{3,19},{4,20},{5,21},{6,22},{7,23},{8,24},{9,... | collective-permute-start | bytes 393224 | tf_op jit(solution)/shard_map/ppermute | solution.py:243
  6.9 0.1 collective-permute-start
  7.0 0.0 collective-permute-start.4
  7.0 3.7 %collective-permute-done.2.refs_3_ = bf16[128,512]{1,0:T(8,128)(2,1)S(1)} collective-permute-done((bf16[128,512]{1,0:T(8,128)(2,1)S(1)}, bf16[128,512]{1,0:T(8,128)(2,1)S(1)}, u32[]{:S(2)}, u32[]{:S(2)}) %collective-permute-start.2) | collective-permute-done | bytes 131104 | tf_op jit(solution)/shard_map/ppermute | solution.py:243
  10.7 0.0 collective-permute-start.7
  10.7 2.2 %collective-permute-done.1.refs_2_ = bf16[128,512]{1,0:T(8,128)(2,1)S(1)} collective-permute-done((bf16[128,512]{1,0:T(8,128)(2,1)S(1)}, bf16[128,512]{1,0:T(8,128)(2,1)S(1)}, u32[]{:S(2)}, u32[]{:S(2)}) %collective-permute-start.1) | collective-permute-done | bytes 131104 | tf_op jit(solution)/shard_map/ppermute | solution.py:243
  12.9 0.0 collective-permute-start.6
  12.9 0.0 collective-permute-done.refs_1_
  12.9 0.5 %collective-permute-start.5 = (bf16[128,512]{1,0:T(8,128)(2,1)S(1)}, bf16[128,512]{1,0:T(8,128)(2,1)S(1)}, u32[]{:S(2)}, u32[]{:S(2)}) collective-permute-start(bf16[128,512]{1,0:T(8,128)(2,1)S(1)} %collective-permute-done.refs_1_), channel_id=1, source_target_pairs={{0,8},{1,9},{2,10},{3,11},{4,12},{5,13},{6,14},{7,15},{8,0},{9,1},... | collective-permute-start | bytes 393224 | tf_op jit(solution)/shard_map/ppermute | solution.py:236
  13.4 3.7 %collective-permute-start.3 = (bf16[64,512]{1,0:T(8,128)(2,1)S(1)}, bf16[64,512]{1,0:T(8,128)(2,1)S(1)}, u32[]{:S(2)}, u32[]{:S(2)}) collective-permute-start(bf16[64,512]{1,0:T(8,128)(2,1)S(1)} %edges.1), channel_id=1, source_target_pairs={{0,6},{1,7},{2,0},{3,1},{4,2},{5,3},{6,4},{7,5},{8,14},{9,15},{10,... | collective-permute-start | bytes 196616 | tf_op jit(solution)/shard_map/ppermute | solution.py:254
  17.1 0.0 collective-permute-done.7.refs_7_
  17.1 0.0 collective-permute-done.6.refs_6_
  17.1 2.7 %plane_inner.1 = (f32[448,512]{1,0:T(8,128)S(1)}, bf16[3,18,32,512]{3,2,1,0:T(8,128)(2,1)S(1)}, bf16[3,18,32,512]{3,2,1,0:T(8,128)(2,1)S(1)}) custom-call(bf16[128,512]{1,0:T(8,128)(2,1)S(1)} %pad_maximum_fusion.refs_0_, bf16[128,512]{1,0:T(8,128)(2,1)S(1)} %collective-permute-done.refs_1_, bf16[128,512]{1,0:T(8,128)(2,1)S(1)} %collective-permute-done.1.refs_2_, ...), custom_call_target="tpu_custom_call" | custom-call | flops 5000000000 | bytes 15000000 | tf_op jit(solution)/shard_map/plane_inner/pallas_call | solution.py:268
  19.9 0.1 collective-permute-start.8
  20.0 0.1 last_lines.1
  20.1 0.1 collective-permute-start.9
  20.1 1.1 %collective-permute-done.8.refs_1_ = bf16[64,512]{1,0:T(8,128)(2,1)S(1)} collective-permute-done((bf16[64,512]{1,0:T(8,128)(2,1)S(1)}, bf16[64,512]{1,0:T(8,128)(2,1)S(1)}, u32[]{:S(2)}, u32[]{:S(2)}) %collective-permute-start.8) | collective-permute-done | bytes 65568 | tf_op jit(solution)/shard_map/ppermute | solution.py:236
  21.2 2.0 %plane_gradient.1 = (bf16[3,18,32,512]{3,2,1,0:T(8,128)(2,1)S(1)}, bf16[3,18,32,512]{3,2,1,0:T(8,128)(2,1)S(1)}, f32[432,128]{1,0:T(8,128)S(1)}, bf16[432,128]{1...) custom-call(bf16[64,512]{1,0:T(8,128)(2,1)S(1)} %later.1.refs_0_, ...), custom_call_target="tpu_custom_call", output_to_operand_aliasing={{0}: (4, {}), {1}: (5, {})} | custom-call | tf_op jit(solution)/shard_map/plane_gradient/pallas_call | solution.py:286
  23.2 2.8 %collective-permute-start.10 = (bf16[432,128]{1,0:T(8,128)(2,1)S(1)}, bf16[432,128]{1,0:T(8,128)(2,1)S(1)}, u32[]{:S(2)}, u32[]{:S(2)}) collective-permute-start(bf16[432,128]{1,0:T(8,128)(2,1)S(1)} %get-tuple-element.22), channel_id=1, source_target_pairs={{0,4},{1,5},{2,6},{3,7},{4,0},{5,1},{6,2},{7,3},{8,12},{9,13},{10,... | collective-permute-start | bytes 331784 | tf_op jit(solution)/shard_map/ppermute | solution.py:304
  25.9 1.1 %collective-permute-start.11 = (bf16[432,128]{1,0:T(8,128)(2,1)S(1)}, bf16[432,128]{1,0:T(8,128)(2,1)S(1)}, u32[]{:S(2)}, u32[]{:S(2)}) collective-permute-start(bf16[432,128]{1,0:T(8,128)(2,1)S(1)} %get-tuple-element.23), channel_id=1, source_target_pairs={{0,2},{1,3},{2,4},{3,5},{4,6},{5,7},{6,0},{7,1},{8,10},{9,11},{10,... | collective-permute-start | bytes 331784 | tf_op jit(solution)/shard_map/ppermute | solution.py:304
  27.0 2.7 %collective-permute-start.12 = (bf16[432,128]{1,0:T(8,128)(2,1)S(1)}, bf16[432,128]{1,0:T(8,128)(2,1)S(1)}, u32[]{:S(2)}, u32[]{:S(2)}) collective-permute-start(bf16[432,128]{1,0:T(8,128)(2,1)S(1)} %get-tuple-element.24), channel_id=1, source_target_pairs={{0,6},{1,7},{2,0},{3,1},{4,2},{5,3},{6,4},{7,5},{8,14},{9,15},{10,... | collective-permute-start | bytes 331784 | tf_op jit(solution)/shard_map/ppermute | solution.py:304
  29.8 0.0 collective-permute-done.9.before_ref
  29.8 4.7 %local_convolutions.1 = (bf16[8,8,512]{2,1,0:T(8,128)(2,1)S(1)}, bf16[8,8,512]{2,1,0:T(8,128)(2,1)S(1)}) custom-call(bf16[3,18,32,512]{3,2,1,0:T(8,128)(2,1)S(1)} %get-tuple-element.17.vol_ref, bf16[3,18,32,512]{3,2,1,0:T(8,128)(2,1)S(1)} %get-tuple-element.18.cot_ref, bf16[64,512]{1,0:T(8,128)(2,1)S(1)} %collective-permute-done.9.before_ref, ...), custom_call_target="tpu_custom_call" | custom-call | tf_op jit(solution)/shard_map/local_convolutions/pallas_call | solution.py:308
  34.5 0.8 %copy_bitcast_fusion = (bf16[8,8,2,256]{3,2,1,0:T(2,128)(2,1)}, bf16[8,8,2,256]{3,2,1,0:T(2,128)(2,1)}) fusion(bf16[8,8,2,256]{3,1,2,0:T(8,128)(2,1)S(1)} %bitcast.13, bf16[8,8,2,256]{3,1,2,0:T(8,128)(2,1)S(1)} %bitcast.12), kind=kLoop, calls=%fused_computation.2 | loop fusion | bytes 262144 | tf_op jit(solution)/shard_map/transpose | solution.py:326
  35.3 0.0 collective-permute-done.10
  35.3 0.0 collective-permute-done.11
  35.3 0.5 %collective-permute-done.12 = bf16[432,128]{1,0:T(8,128)(2,1)S(1)} collective-permute-done((bf16[432,128]{1,0:T(8,128)(2,1)S(1)}, bf16[432,128]{1,0:T(8,128)(2,1)S(1)}, u32[]{:S(2)}, u32[]{:S(2)}) %collective-permute-start.12) | collective-permute-done | bytes 110624 | tf_op jit(solution)/shard_map/ppermute | solution.py:304
  35.8 0.7 %add_bitcast_fusion = f32[55296]{0:T(1024)} fusion(bf16[432,128]{1,0:T(8,128)(2,1)S(1)} %collective-permute-done.12, bf16[432,128]{1,0:T(8,128)(2,1)S(1)} %collective-permute-done.11, f32[432,128]{1,0:T(8,128)S(1)} %get-tuple-element.21, bf16[432,128]{1,0:T(8,128)(2,1)S(1)} %collective-permute-done.10), kind=kLoop, calls=%fused_computation | loop fusion | flops 331776 | bytes 774144 | tf_op jit(solution)/shard_map/reshape | solution.py:331
  (9 shorter events, 0.0 us)
Async XLA Ops:
  2.4 14.7 %copy-start = (bf16[6912,256]{1,0:T(8,128)(2,1)S(1)}, bf16[6912,256]{1,0:T(8,128)(2,1)}, u32[]{:S(2)}) copy-start(bf16[6912,256]{1,0:T(8,128)(2,1)} %w1.1) | copy-start | bytes 10616836
  2.4 8.3 %collective-permute-start.2 = (bf16[128,512]{1,0:T(8,128)(2,1)S(1)}, bf16[128,512]{1,0:T(8,128)(2,1)S(1)}, u32[]{:S(2)}, u32[]{:S(2)}) collective-permute-start(bf16[128,512]{1,0:T(8,128)(2,1)S(1)} %pad_maximum_fusion.refs_0_), channel_id=1, source_target_pairs={{0,17},{1,16},{2,19},{3,18},{4,21},{5,20},{6,23},{7,22},{8,25},{9,... | collective-permute-start | bytes 393224 | tf_op jit(solution)/shard_map/ppermute | solution.py:243
  6.4 6.6 %collective-permute-start.1 = (bf16[128,512]{1,0:T(8,128)(2,1)S(1)}, bf16[128,512]{1,0:T(8,128)(2,1)S(1)}, u32[]{:S(2)}, u32[]{:S(2)}) collective-permute-start(bf16[128,512]{1,0:T(8,128)(2,1)S(1)} %pad_maximum_fusion.refs_0_), channel_id=1, source_target_pairs={{0,16},{1,17},{2,18},{3,19},{4,20},{5,21},{6,22},{7,23},{8,24},{9,... | collective-permute-start | bytes 393224 | tf_op jit(solution)/shard_map/ppermute | solution.py:243
  6.9 6.0 %collective-permute-start = (bf16[128,512]{1,0:T(8,128)(2,1)S(1)}, bf16[128,512]{1,0:T(8,128)(2,1)S(1)}, u32[]{:S(2)}, u32[]{:S(2)}) collective-permute-start(bf16[128,512]{1,0:T(8,128)(2,1)S(1)} %pad_maximum_fusion.refs_0_), channel_id=1, source_target_pairs={{0,1},{1,0},{2,3},{3,2},{4,5},{5,4},{6,7},{7,6},{8,9},{9,8},{10,11... | collective-permute-start | bytes 393224 | tf_op jit(solution)/shard_map/ppermute | solution.py:243
  7.0 10.1 %collective-permute-start.4 = (bf16[128,512]{1,0:T(8,128)(2,1)S(1)}, bf16[128,512]{1,0:T(8,128)(2,1)S(1)}, u32[]{:S(2)}, u32[]{:S(2)}) collective-permute-start(bf16[128,512]{1,0:T(8,128)(2,1)S(1)} %pad_maximum_fusion.refs_0_), channel_id=1, source_target_pairs={{0,8},{1,9},{2,10},{3,11},{4,12},{5,13},{6,14},{7,15},{8,0},{9,1},... | collective-permute-start | bytes 393224 | tf_op jit(solution)/shard_map/ppermute | solution.py:236
  10.7 6.4 %collective-permute-start.7 = (bf16[128,512]{1,0:T(8,128)(2,1)S(1)}, bf16[128,512]{1,0:T(8,128)(2,1)S(1)}, u32[]{:S(2)}, u32[]{:S(2)}) collective-permute-start(bf16[128,512]{1,0:T(8,128)(2,1)S(1)} %collective-permute-done.2.refs_3_), channel_id=1, source_target_pairs={{0,8},{1,9},{2,10},{3,11},{4,12},{5,13},{6,14},{7,15},{8,0},{9,1},... | collective-permute-start | bytes 393224 | tf_op jit(solution)/shard_map/ppermute | solution.py:236
  12.9 4.2 %collective-permute-start.6 = (bf16[128,512]{1,0:T(8,128)(2,1)S(1)}, bf16[128,512]{1,0:T(8,128)(2,1)S(1)}, u32[]{:S(2)}, u32[]{:S(2)}) collective-permute-start(bf16[128,512]{1,0:T(8,128)(2,1)S(1)} %collective-permute-done.1.refs_2_), channel_id=1, source_target_pairs={{0,8},{1,9},{2,10},{3,11},{4,12},{5,13},{6,14},{7,15},{8,0},{9,1},... | collective-permute-start | bytes 393224 | tf_op jit(solution)/shard_map/ppermute | solution.py:236
  12.9 4.2 %collective-permute-start.5 = (bf16[128,512]{1,0:T(8,128)(2,1)S(1)}, bf16[128,512]{1,0:T(8,128)(2,1)S(1)}, u32[]{:S(2)}, u32[]{:S(2)}) collective-permute-start(bf16[128,512]{1,0:T(8,128)(2,1)S(1)} %collective-permute-done.refs_1_), channel_id=1, source_target_pairs={{0,8},{1,9},{2,10},{3,11},{4,12},{5,13},{6,14},{7,15},{8,0},{9,1},... | collective-permute-start | bytes 393224 | tf_op jit(solution)/shard_map/ppermute | solution.py:236
  13.4 6.4 %collective-permute-start.3 = (bf16[64,512]{1,0:T(8,128)(2,1)S(1)}, bf16[64,512]{1,0:T(8,128)(2,1)S(1)}, u32[]{:S(2)}, u32[]{:S(2)}) collective-permute-start(bf16[64,512]{1,0:T(8,128)(2,1)S(1)} %edges.1), channel_id=1, source_target_pairs={{0,6},{1,7},{2,0},{3,1},{4,2},{5,3},{6,4},{7,5},{8,14},{9,15},{10,... | collective-permute-start | bytes 196616 | tf_op jit(solution)/shard_map/ppermute | solution.py:254
  19.9 1.3 %collective-permute-start.8 = (bf16[64,512]{1,0:T(8,128)(2,1)S(1)}, bf16[64,512]{1,0:T(8,128)(2,1)S(1)}, u32[]{:S(2)}, u32[]{:S(2)}) collective-permute-start(bf16[64,512]{1,0:T(8,128)(2,1)S(1)} %later.1.refs_0_), channel_id=1, source_target_pairs={{0,8},{1,9},{2,10},{3,11},{4,12},{5,13},{6,14},{7,15},{8,0},{9,1},... | collective-permute-start | bytes 196616 | tf_op jit(solution)/shard_map/ppermute | solution.py:236
  20.1 9.7 %collective-permute-start.9 = (bf16[64,512]{1,0:T(8,128)(2,1)S(1)}, bf16[64,512]{1,0:T(8,128)(2,1)S(1)}, u32[]{:S(2)}, u32[]{:S(2)}) collective-permute-start(bf16[64,512]{1,0:T(8,128)(2,1)S(1)} %last_lines.1), channel_id=1, source_target_pairs={{0,2},{1,3},{2,4},{3,5},{4,6},{5,7},{6,0},{7,1},{8,10},{9,11},{10,... | collective-permute-start | bytes 196616 | tf_op jit(solution)/shard_map/ppermute | solution.py:265
  21.2 8.6 %copy-start.1 = (bf16[6912,256]{1,0:T(8,128)(2,1)S(1)}, bf16[6912,256]{1,0:T(8,128)(2,1)}, u32[]{:S(2)}) copy-start(bf16[6912,256]{1,0:T(8,128)(2,1)} %w2.1) | copy-start | bytes 10616836
  23.2 12.1 %collective-permute-start.10 = (bf16[432,128]{1,0:T(8,128)(2,1)S(1)}, bf16[432,128]{1,0:T(8,128)(2,1)S(1)}, u32[]{:S(2)}, u32[]{:S(2)}) collective-permute-start(bf16[432,128]{1,0:T(8,128)(2,1)S(1)} %get-tuple-element.22), channel_id=1, source_target_pairs={{0,4},{1,5},{2,6},{3,7},{4,0},{5,1},{6,2},{7,3},{8,12},{9,13},{10,... | collective-permute-start | bytes 331784 | tf_op jit(solution)/shard_map/ppermute | solution.py:304
  25.9 9.3 %collective-permute-start.11 = (bf16[432,128]{1,0:T(8,128)(2,1)S(1)}, bf16[432,128]{1,0:T(8,128)(2,1)S(1)}, u32[]{:S(2)}, u32[]{:S(2)}) collective-permute-start(bf16[432,128]{1,0:T(8,128)(2,1)S(1)} %get-tuple-element.23), channel_id=1, source_target_pairs={{0,2},{1,3},{2,4},{3,5},{4,6},{5,7},{6,0},{7,1},{8,10},{9,11},{10,... | collective-permute-start | bytes 331784 | tf_op jit(solution)/shard_map/ppermute | solution.py:304
  27.0 8.7 %collective-permute-start.12 = (bf16[432,128]{1,0:T(8,128)(2,1)S(1)}, bf16[432,128]{1,0:T(8,128)(2,1)S(1)}, u32[]{:S(2)}, u32[]{:S(2)}) collective-permute-start(bf16[432,128]{1,0:T(8,128)(2,1)S(1)} %get-tuple-element.24), channel_id=1, source_target_pairs={{0,6},{1,7},{2,0},{3,1},{4,2},{5,3},{6,4},{7,5},{8,14},{9,15},{10,... | collective-permute-start | bytes 331784 | tf_op jit(solution)/shard_map/ppermute | solution.py:304

commit v4 on v3

--- a/solution.py
+++ b/solution.py
@@ -64,7 +64,7 @@
         slot = side if dy == 0 else 1 - side
         for pair in range(4):
             rows = lambda refs, dx: (refs[dx * 2 + dy], which * 64 + pair * 16)
-            put(which, 8 * slot + 2 * pair, ring(n_x, core, pieces[:n], pieces[n:], rows))
+            put(which, 2 + 8 * slot + 2 * pair, ring(n_x, core, pieces[:n], pieces[n:], rows))
 
 
 def putter(vol, cot):
@@ -85,14 +85,24 @@
 
 
 def edge_kernel(n_x, *refs):
-    *pieces, first = refs
+    *pieces, last = refs
     side = place()[3]
     for dx in range(n_x):
         for which in range(2):
             a, b = pieces[dx * 2], pieces[dx * 2 + 1]
             out = slice(dx * 32 + which * 16, dx * 32 + which * 16 + 16)
-            rows = slice(which * 64, which * 64 + 16)
-            first[out, :] = jnp.where(side == 0, a[rows, :], b[rows, :])
+            rows = slice(which * 64 + 48, which * 64 + 64)
+            last[out, :] = jnp.where(side == 0, b[rows, :], a[rows, :])
+
+
+def lines_kernel(fields, out, rows):
+    sy, sx = rows.shape[:2]
+    for k in range(2):
+        for x in range(sx):
+            block = fields[k, x].astype(F32)
+            rows[:, x, :CH] = block[:, 0, :]
+            rows[:, x, CH:] = block[:, 1, :]
+        out[k * sy * sx : (k + 1) * sy * sx, :] = rows[...].reshape(sy * sx, 2 * CH).astype(BF16)
 
 
 def later_kernel(lines, _, out):
@@ -105,7 +115,7 @@
     put = putter(vol, cot)
     assemble(n_x, 0, pieces, put)
     for k in range(9):
-        left = vol[k // 3, k % 3 : k % 3 + 14].reshape(14 * full, 512)
+        left = vol[k // 3, 2 + k % 3 : k % 3 + 16].reshape(14 * full, 512)
         term = dot(left, both(w_ref[k * 768 : k * 768 + 768, :]))
         pre[...] = term if k == 0 else pre[...] + term
     assemble(n_x, 1, pieces, put)
@@ -117,13 +127,13 @@
     full = 16 * n_x
     put = putter(vol, cot)
     for which in range(2):
-        put(which, 16, ring(n_x, core, beyond_a, beyond_b, lambda ref, dx: (ref, dx * 32 + which * 16)))
+        put(which, 0, ring(n_x, core, beyond_a, beyond_b, lambda ref, dx: (ref, dx * 32 + which * 16)))
     outer = None
     for k in range(9):
-        left = vol[k // 3, 14 + k % 3 : 16 + k % 3].reshape(2 * full, 512)
+        left = vol[k // 3, k % 3 : k % 3 + 2].reshape(2 * full, 512)
         term = dot(left, both(w_ref[k * 768 : k * 768 + 768, :]))
         outer = term if k == 0 else outer + term
-    inner = jnp.concatenate([pre[...], outer], axis=0)
+    inner = jnp.concatenate([outer, pre[...]], axis=0)
     hid[...] = (inner * jax.nn.sigmoid(inner)).T.astype(BF16)
     first = lax.div(gx * strip, 3 * CH)
     for k in range(groups):
@@ -152,26 +162,26 @@
             sends[k - 1][...] = flat[...].astype(BF16)
 
 
-def last_kernel(n_x, *refs):
+def first_kernel(n_x, *refs):
     *pieces, out = refs
     _, core, _, side = place()
     n = 2 * n_x
     for which in range(2):
         low, high = (
-            ring(n_x, core, pieces[:n], pieces[n:], lambda refs, dx: (refs[dx * 2 + dy], which * 64 + 48)) for dy in range(2)
+            ring(n_x, core, pieces[:n], pieces[n:], lambda refs, dx: (refs[dx * 2 + dy], which * 64)) for dy in range(2)
         )
-        lines = window(jnp.where(side == 0, high, low), core)
+        lines = window(jnp.where(side == 0, low, high), core)
         out[which * 32 : which * 32 + 32, :] = lines.reshape(32, 512).astype(BF16)
 
 
-def local_kernel(vol_ref, cot_ref, before_ref, w1, w2, out_ref, vgrad_ref, vol, hid, cot, thr, acc):
+def local_kernel(vol_ref, cot_ref, after_ref, w1, w2, out_ref, vgrad_ref, vol, hid, cot, thr, acc):
     _, core, _, side = place()
 
     def cut(which, ref):
         lines = window(ref[1, pl.ds(side * 8, 10)].astype(F32), core)
-        before = before_ref[which * 32 : which * 32 + 32, :].astype(F32).reshape(2, 16, 512)
-        before = jnp.where(side == 0, before, window(ref[1, 6:8].astype(F32), core))
-        return jnp.concatenate([before, lines], axis=0)
+        after = after_ref[which * 32 : which * 32 + 32, :].astype(F32).reshape(2, 16, 512)
+        after = jnp.where(side == 0, window(ref[1, 10:12].astype(F32), core), after)
+        return jnp.concatenate([lines, after], axis=0)
 
     v, c = cut(0, vol_ref), cut(1, cot_ref)
     for s in range(3):
@@ -229,19 +239,25 @@
     perm = functools.partial(permutation, n_gx, n_gy)
     vmem = pl.BlockSpec(memory_space=pltpu.VMEM)
 
-    def lines(v):
-        return jnp.transpose(v, (1, 0, 2, 3)).reshape(-1, sz * chans)
-
     def across(v):
         return lax.ppermute(v, AX, perm(lambda x, c, z, y: (x, 1 - c, z, y)))
 
-    own = jnp.concatenate([lines(volume), lines(cotangent)])
+    own = pl.pallas_call(
+        lines_kernel,
+        out_shape=jax.ShapeDtypeStruct((2 * sy * sx, sz * chans), BF16),
+        in_specs=[vmem],
+        out_specs=vmem,
+        scratch_shapes=[pltpu.VMEM((sy, sx, sz * chans), F32)],
+        compiler_params=params(4),
+        cost_estimate=cost(1),
+        name="lines",
+    )(jnp.stack([volume, cotangent]))
     pieces = [own]
     for dx in range(n_x):
         for dy in range(2):
             if dx or dy:
                 pieces.append(lax.ppermute(own, AX, perm(lambda x, c, z, y, dx=dx, dy=dy: (x - dx, c, z, y ^ dy))))
-    first = pl.pallas_call(
+    last = pl.pallas_call(
         functools.partial(edge_kernel, n_x),
         out_shape=jax.ShapeDtypeStruct((n_x * 32, 512), BF16),
         in_specs=[vmem] * (2 * n_x),
@@ -251,18 +267,18 @@
         name="edges",
     )(*pieces)
     pieces += [across(v) for v in pieces]
-    beyond = lax.ppermute(first, AX, perm(lambda x, c, z, y: (x, c, z - 1, y)))
-
-    last = pl.pallas_call(
-        functools.partial(last_kernel, n_x),
+    beyond = lax.ppermute(last, AX, perm(lambda x, c, z, y: (x, c, z + 1, y)))
+
+    first = pl.pallas_call(
+        functools.partial(first_kernel, n_x),
         out_shape=jax.ShapeDtypeStruct((64, 512), BF16),
         in_specs=[vmem] * (4 * n_x),
         out_specs=vmem,
         compiler_params=params(4),
         cost_estimate=cost(0),
-        name="last_lines",
+        name="first_lines",
     )(*pieces)
-    before = lax.ppermute(last, AX, perm(lambda x, c, z, y: (x, c, z + 1, y)))
+    after = lax.ppermute(first, AX, perm(lambda x, c, z, y: (x, c, z - 1, y)))
 
     plane = jax.ShapeDtypeStruct((3, 18, full, 512), BF16)
     pre, vol, cot = pl.pallas_call(
@@ -302,7 +318,7 @@
 
     received = [
         lax.ppermute(sends[k - 1], AX, perm(lambda x, c, z, y, k=k: (x, c, z + k, y)))
-        for k in sorted(range(1, n_z), key=lambda k: k != n_z // 2)
+        for k in sorted(range(n_z - 1, 0, -1), key=lambda k: k != n_z // 2)
     ]
 
     output, volume_grad = pl.pallas_call(
@@ -320,7 +336,7 @@
         compiler_params=params(24),
         cost_estimate=cost(0),
         name="local_convolutions",
-    )(vol, cot, before, first_weight, second_weight)
+    )(vol, cot, after, first_weight, second_weight)
 
     def cells(v):
         return jnp.transpose(v.reshape(sy, sx, sz, chans), (1, 0, 2, 3))

time: 36.7 us -> 34.6 us (0.943)
  starting transfers between devices: 15.5 us -> 11.3 us
  waiting for transfers between devices: 7.49 us -> 10.2 us
  local copies, waits for them, and re-layouts: 2.49 us -> 0.76 us
  other arithmetic: 0.75 us -> 1.81 us
    ppermute x3, starting transfers between devices: 6.59 us -> 2.65 us  [body(): lax.ppermute(sends[k - 1], AX, perm(lambda x, c, z, y, k=k: (x, c, z + k,...]
    ppermute x3, waiting for transfers between devices: 0.5 us -> 2.53 us  [body(): lax.ppermute(sends[k - 1], AX, perm(lambda x, c, z, y, k=k: (x, c, z + k,...]
    ppermute x2, waiting for transfers between devices: 0.01 us -> 1.73 us  [the longest x1 1.73 us: body(): beyond = lax.ppermute(last, AX, perm(lambda x, c, z, y: (x, c, z + 1, y)))]
    transpose x2 -> x0, local copies, waits for them, and re-layouts: 1.73 us -> none  [lines(): return jnp.transpose(v, (1, 0, 2, 3)).reshape(-1, sz * chans)]
    ppermute x5, waiting for transfers between devices: 1.08 us -> 0.01 us  [across(): return lax.ppermute(v, AX, perm(lambda x, c, z, y: (x, 1 - c, z, y)))]
    another operation x0 -> x1, other arithmetic: none -> 1.06 us  [body(): jnp.stack([volume, cotangent])]
  transfers between devices with their start and end apart: 13 -> 13, of which waited for: 4 -> 5; matrix products, arithmetic and copies ran while one was open for 2% -> 2% of each run, Pallas kernels for 26% -> 28%
where the time goes in v4:
time: 34.6 us; the launch traced here: 34.5 us
  starting transfers between devices  11.3 us (33%)
  waiting for transfers between devices  10.2 us (29%)
  Pallas kernels  9.73 us (28%)
  other arithmetic  1.81 us (5%)
  local copies, waits for them, and re-layouts  0.76 us (2%)
  between operations  0.72 us (2%)
    ppermute x3, waiting for transfers between devices, body(): lax.ppermute(own, AX, perm(lambda x, c, z, y, dx=dx, dy=dy: (x - dx, c, z...  5.91 us
    pallas_call x1, Pallas kernels, body(): pl.pallas_call(local_kernel, out_shape=[jax.ShapeDtypeStruct((sy, sx, 512...  4.7 us
    ppermute x3, starting transfers between devices, body(): lax.ppermute(own, AX, perm(lambda x, c, z, y, dx=dx, dy=dy: (x - dx, c, z...  4.6 us
    pallas_call x1, Pallas kernels, body(): pl.pallas_call(functools.partial(inner_kernel, n_x), out_shape=[jax.Shape...  2.72 us
    ppermute x3, starting transfers between devices, body(): lax.ppermute(sends[k - 1], AX, perm(lambda x, c, z, y, k=k: (x, c, z + k,...  2.65 us
    ppermute x3, waiting for transfers between devices, body(): lax.ppermute(sends[k - 1], AX, perm(lambda x, c, z, y, k=k: (x, c, z + k,...  2.53 us
    pallas_call x1, Pallas kernels, body(): pl.pallas_call(functools.partial(gradient_kernel, n_x, n_z, groups, strip...  2.08 us
    ppermute x1, starting transfers between devices, body(): after = lax.ppermute(first, AX, perm(lambda x, c, z, y: (x, c, z - 1, y)))  1.86 us
  transfers between devices with their start and end apart: 13, of which 5 were waited for; matrix products, arithmetic and copies ran while one was open for 2% of the time, Pallas kernels for 28%

profile of v4, /device:TPU:0, one launch (start us, length us, event | category | flops | bytes accessed | tf_op | source)
XLA Modules:
  0.0 34.5 jit_solution(11012730235640299132)
XLA Ops:
  0.6 1.1 %pad_maximum_fusion.fields = bf16[2,8,8,2,256]{4,3,2,1,0:T(2,128)(2,1)S(1)} fusion(bf16[1,8,8,2,256]{4,3,2,1,0:T(2,128)(2,1)} %bitcast.12, bf16[1,8,8,2,256]{4,3,2,1,0:T(2,128)(2,1)} %bitcast.13), kind=kLoop, calls=%fused_computation.1 | loop fusion | flops 65536 | bytes 262144 | tf_op jit(solution)/shard_map/stack | solution.py:254
  1.7 0.1 lines.1.refs_0_
  1.8 0.0 copy-start
  1.8 4.0 %collective-permute-start.2 = (bf16[128,512]{1,0:T(8,128)(2,1)S(1)}, bf16[128,512]{1,0:T(8,128)(2,1)S(1)}, u32[]{:S(2)}, u32[]{:S(2)}) collective-permute-start(bf16[128,512]{1,0:T(8,128)(2,1)S(1)} %lines.1.refs_0_), channel_id=1, source_target_pairs={{0,17},{1,16},{2,19},{3,18},{4,21},{5,20},{6,23},{7,22},{8,25},{9,... | collective-permute-start | bytes 393224 | tf_op jit(solution)/shard_map/ppermute | solution.py:259
  5.8 0.5 %collective-permute-start.1 = (bf16[128,512]{1,0:T(8,128)(2,1)S(1)}, bf16[128,512]{1,0:T(8,128)(2,1)S(1)}, u32[]{:S(2)}, u32[]{:S(2)}) collective-permute-start(bf16[128,512]{1,0:T(8,128)(2,1)S(1)} %lines.1.refs_0_), channel_id=1, source_target_pairs={{0,16},{1,17},{2,18},{3,19},{4,20},{5,21},{6,22},{7,23},{8,24},{9,... | collective-permute-start | bytes 393224 | tf_op jit(solution)/shard_map/ppermute | solution.py:259
  6.3 0.1 collective-permute-start
  6.4 3.7 %collective-permute-done.2.refs_3_ = bf16[128,512]{1,0:T(8,128)(2,1)S(1)} collective-permute-done((bf16[128,512]{1,0:T(8,128)(2,1)S(1)}, bf16[128,512]{1,0:T(8,128)(2,1)S(1)}, u32[]{:S(2)}, u32[]{:S(2)}) %collective-permute-start.2) | collective-permute-done | bytes 131104 | tf_op jit(solution)/shard_map/ppermute | solution.py:259
  10.1 0.0 collective-permute-start.7
  10.1 2.2 %collective-permute-done.1.refs_2_ = bf16[128,512]{1,0:T(8,128)(2,1)S(1)} collective-permute-done((bf16[128,512]{1,0:T(8,128)(2,1)S(1)}, bf16[128,512]{1,0:T(8,128)(2,1)S(1)}, u32[]{:S(2)}, u32[]{:S(2)}) %collective-permute-start.1) | collective-permute-done | bytes 131104 | tf_op jit(solution)/shard_map/ppermute | solution.py:259
  12.3 0.0 collective-permute-start.6
  12.4 0.0 collective-permute-done.refs_1_
  12.4 0.5 %collective-permute-start.5 = (bf16[128,512]{1,0:T(8,128)(2,1)S(1)}, bf16[128,512]{1,0:T(8,128)(2,1)S(1)}, u32[]{:S(2)}, u32[]{:S(2)}) collective-permute-start(bf16[128,512]{1,0:T(8,128)(2,1)S(1)} %collective-permute-done.refs_1_), channel_id=1, source_target_pairs={{0,8},{1,9},{2,10},{3,11},{4,12},{5,13},{6,14},{7,15},{8,0},{9,1},... | collective-permute-start | bytes 393224 | tf_op jit(solution)/shard_map/ppermute | solution.py:243
  12.9 1.6 %collective-permute-start.3 = (bf16[64,512]{1,0:T(8,128)(2,1)S(1)}, bf16[64,512]{1,0:T(8,128)(2,1)S(1)}, u32[]{:S(2)}, u32[]{:S(2)}) collective-permute-start(bf16[64,512]{1,0:T(8,128)(2,1)S(1)} %edges.1), channel_id=1, source_target_pairs={{0,2},{1,3},{2,4},{3,5},{4,6},{5,7},{6,0},{7,1},{8,10},{9,11},{10,... | collective-permute-start | bytes 196616 | tf_op jit(solution)/shard_map/ppermute | solution.py:270
  14.5 0.0 collective-permute-done.4.refs_4_
  14.5 0.0 collective-permute-done.7.refs_7_
  14.5 0.0 collective-permute-done.6.refs_6_
  14.5 2.7 %plane_inner.1 = (f32[448,512]{1,0:T(8,128)S(1)}, bf16[3,18,32,512]{3,2,1,0:T(8,128)(2,1)S(1)}, bf16[3,18,32,512]{3,2,1,0:T(8,128)(2,1)S(1)}) custom-call(bf16[128,512]{1,0:T(8,128)(2,1)S(1)} %lines.1.refs_0_, bf16[128,512]{1,0:T(8,128)(2,1)S(1)} %collective-permute-done.refs_1_, bf16[128,512]{1,0:T(8,128)(2,1)S(1)} %collective-permute-done.1.refs_2_, ...), custom_call_target="tpu_custom_call" | custom-call | flops 5000000000 | bytes 15000000 | tf_op jit(solution)/shard_map/plane_inner/pallas_call | solution.py:284
  17.3 1.7 %collective-permute-done.3.lines = bf16[64,512]{1,0:T(8,128)(2,1)S(1)} collective-permute-done((bf16[64,512]{1,0:T(8,128)(2,1)S(1)}, bf16[64,512]{1,0:T(8,128)(2,1)S(1)}, u32[]{:S(2)}, u32[]{:S(2)}) %collective-permute-start.3) | collective-permute-done | bytes 65568 | tf_op jit(solution)/shard_map/ppermute | solution.py:270
  19.0 0.0 collective-permute-start.8
  19.0 0.1 first_lines.1
  19.1 1.9 %collective-permute-start.9 = (bf16[64,512]{1,0:T(8,128)(2,1)S(1)}, bf16[64,512]{1,0:T(8,128)(2,1)S(1)}, u32[]{:S(2)}, u32[]{:S(2)}) collective-permute-start(bf16[64,512]{1,0:T(8,128)(2,1)S(1)} %first_lines.1), channel_id=1, source_target_pairs={{0,6},{1,7},{2,0},{3,1},{4,2},{5,3},{6,4},{7,5},{8,14},{9,15},{10,... | collective-permute-start | bytes 196616 | tf_op jit(solution)/shard_map/ppermute | solution.py:281
  21.0 0.0 collective-permute-done.8.refs_1_
  21.0 2.1 %plane_gradient.1 = (bf16[3,18,32,512]{3,2,1,0:T(8,128)(2,1)S(1)}, bf16[3,18,32,512]{3,2,1,0:T(8,128)(2,1)S(1)}, f32[432,128]{1,0:T(8,128)S(1)}, bf16[432,128]{1...) custom-call(bf16[64,512]{1,0:T(8,128)(2,1)S(1)} %later.1.refs_0_, ...), custom_call_target="tpu_custom_call", output_to_operand_aliasing={{0}: (4, {}), {1}: (5, {})} | custom-call | tf_op jit(solution)/shard_map/plane_gradient/pallas_call | solution.py:302
  23.1 0.3 collective-permute-start.10
  23.4 2.3 %collective-permute-start.11 = (bf16[432,128]{1,0:T(8,128)(2,1)S(1)}, bf16[432,128]{1,0:T(8,128)(2,1)S(1)}, u32[]{:S(2)}, u32[]{:S(2)}) collective-permute-start(bf16[432,128]{1,0:T(8,128)(2,1)S(1)} %get-tuple-element.23), channel_id=1, source_target_pairs={{0,6},{1,7},{2,0},{3,1},{4,2},{5,3},{6,4},{7,5},{8,14},{9,15},{10,... | collective-permute-start | bytes 331784 | tf_op jit(solution)/shard_map/ppermute | solution.py:320
  25.7 0.0 collective-permute-done.9.after_ref
  25.7 4.7 %local_convolutions.1 = (bf16[8,8,512]{2,1,0:T(8,128)(2,1)S(1)}, bf16[8,8,512]{2,1,0:T(8,128)(2,1)S(1)}) custom-call(bf16[3,18,32,512]{3,2,1,0:T(8,128)(2,1)S(1)} %get-tuple-element.17.vol_ref, bf16[3,18,32,512]{3,2,1,0:T(8,128)(2,1)S(1)} %get-tuple-element.18.cot_ref, bf16[64,512]{1,0:T(8,128)(2,1)S(1)} %collective-permute-done.9.after_ref, ...), custom_call_target="tpu_custom_call" | custom-call | tf_op jit(solution)/shard_map/local_convolutions/pallas_call | solution.py:324
  30.4 0.8 %copy_bitcast_fusion = (bf16[8,8,2,256]{3,2,1,0:T(2,128)(2,1)}, bf16[8,8,2,256]{3,2,1,0:T(2,128)(2,1)}) fusion(bf16[8,8,2,256]{3,1,2,0:T(8,128)(2,1)S(1)} %bitcast.11, bf16[8,8,2,256]{3,1,2,0:T(8,128)(2,1)S(1)} %bitcast.10), kind=kLoop, calls=%fused_computation.2 | loop fusion | bytes 262144 | tf_op jit(solution)/shard_map/transpose | solution.py:342
  31.2 0.8 %collective-permute-done.10 = bf16[432,128]{1,0:T(8,128)(2,1)S(1)} collective-permute-done((bf16[432,128]{1,0:T(8,128)(2,1)S(1)}, bf16[432,128]{1,0:T(8,128)(2,1)S(1)}, u32[]{:S(2)}, u32[]{:S(2)}) %collective-permute-start.10) | collective-permute-done | bytes 110624 | tf_op jit(solution)/shard_map/ppermute | solution.py:320
  32.0 0.0 collective-permute-done.11
  32.0 1.7 %collective-permute-done.12 = bf16[432,128]{1,0:T(8,128)(2,1)S(1)} collective-permute-done((bf16[432,128]{1,0:T(8,128)(2,1)S(1)}, bf16[432,128]{1,0:T(8,128)(2,1)S(1)}, u32[]{:S(2)}, u32[]{:S(2)}) %collective-permute-start.12) | collective-permute-done | bytes 110624 | tf_op jit(solution)/shard_map/ppermute | solution.py:320
  33.7 0.7 %add_bitcast_fusion = f32[55296]{0:T(1024)} fusion(bf16[432,128]{1,0:T(8,128)(2,1)S(1)} %collective-permute-done.12, bf16[432,128]{1,0:T(8,128)(2,1)S(1)} %collective-permute-done.11, f32[432,128]{1,0:T(8,128)S(1)} %get-tuple-element.21, bf16[432,128]{1,0:T(8,128)(2,1)S(1)} %collective-permute-done.10), kind=kLoop, calls=%fused_computation | loop fusion | flops 331776 | bytes 774144 | tf_op jit(solution)/shard_map/reshape | solution.py:347
  (8 shorter events, 0.0 us)
Async XLA Ops:
  1.8 12.7 %copy-start = (bf16[6912,256]{1,0:T(8,128)(2,1)S(1)}, bf16[6912,256]{1,0:T(8,128)(2,1)}, u32[]{:S(2)}) copy-start(bf16[6912,256]{1,0:T(8,128)(2,1)} %w1.1) | copy-start | bytes 10616836
  1.8 8.3 %collective-permute-start.2 = (bf16[128,512]{1,0:T(8,128)(2,1)S(1)}, bf16[128,512]{1,0:T(8,128)(2,1)S(1)}, u32[]{:S(2)}, u32[]{:S(2)}) collective-permute-start(bf16[128,512]{1,0:T(8,128)(2,1)S(1)} %lines.1.refs_0_), channel_id=1, source_target_pairs={{0,17},{1,16},{2,19},{3,18},{4,21},{5,20},{6,23},{7,22},{8,25},{9,... | collective-permute-start | bytes 393224 | tf_op jit(solution)/shard_map/ppermute | solution.py:259
  5.8 6.6 %collective-permute-start.1 = (bf16[128,512]{1,0:T(8,128)(2,1)S(1)}, bf16[128,512]{1,0:T(8,128)(2,1)S(1)}, u32[]{:S(2)}, u32[]{:S(2)}) collective-permute-start(bf16[128,512]{1,0:T(8,128)(2,1)S(1)} %lines.1.refs_0_), channel_id=1, source_target_pairs={{0,16},{1,17},{2,18},{3,19},{4,20},{5,21},{6,22},{7,23},{8,24},{9,... | collective-permute-start | bytes 393224 | tf_op jit(solution)/shard_map/ppermute | solution.py:259
  6.3 6.0 %collective-permute-start = (bf16[128,512]{1,0:T(8,128)(2,1)S(1)}, bf16[128,512]{1,0:T(8,128)(2,1)S(1)}, u32[]{:S(2)}, u32[]{:S(2)}) collective-permute-start(bf16[128,512]{1,0:T(8,128)(2,1)S(1)} %lines.1.refs_0_), channel_id=1, source_target_pairs={{0,1},{1,0},{2,3},{3,2},{4,5},{5,4},{6,7},{7,6},{8,9},{9,8},{10,11... | collective-permute-start | bytes 393224 | tf_op jit(solution)/shard_map/ppermute | solution.py:259
  6.4 8.1 %collective-permute-start.4 = (bf16[128,512]{1,0:T(8,128)(2,1)S(1)}, bf16[128,512]{1,0:T(8,128)(2,1)S(1)}, u32[]{:S(2)}, u32[]{:S(2)}) collective-permute-start(bf16[128,512]{1,0:T(8,128)(2,1)S(1)} %lines.1.refs_0_), channel_id=1, source_target_pairs={{0,8},{1,9},{2,10},{3,11},{4,12},{5,13},{6,14},{7,15},{8,0},{9,1},... | collective-permute-start | bytes 393224 | tf_op jit(solution)/shard_map/ppermute | solution.py:243
  10.1 4.4 %collective-permute-start.7 = (bf16[128,512]{1,0:T(8,128)(2,1)S(1)}, bf16[128,512]{1,0:T(8,128)(2,1)S(1)}, u32[]{:S(2)}, u32[]{:S(2)}) collective-permute-start(bf16[128,512]{1,0:T(8,128)(2,1)S(1)} %collective-permute-done.2.refs_3_), channel_id=1, source_target_pairs={{0,8},{1,9},{2,10},{3,11},{4,12},{5,13},{6,14},{7,15},{8,0},{9,1},... | collective-permute-start | bytes 393224 | tf_op jit(solution)/shard_map/ppermute | solution.py:243
  12.3 2.2 %collective-permute-start.6 = (bf16[128,512]{1,0:T(8,128)(2,1)S(1)}, bf16[128,512]{1,0:T(8,128)(2,1)S(1)}, u32[]{:S(2)}, u32[]{:S(2)}) collective-permute-start(bf16[128,512]{1,0:T(8,128)(2,1)S(1)} %collective-permute-done.1.refs_2_), channel_id=1, source_target_pairs={{0,8},{1,9},{2,10},{3,11},{4,12},{5,13},{6,14},{7,15},{8,0},{9,1},... | collective-permute-start | bytes 393224 | tf_op jit(solution)/shard_map/ppermute | solution.py:243
  12.4 2.2 %collective-permute-start.5 = (bf16[128,512]{1,0:T(8,128)(2,1)S(1)}, bf16[128,512]{1,0:T(8,128)(2,1)S(1)}, u32[]{:S(2)}, u32[]{:S(2)}) collective-permute-start(bf16[128,512]{1,0:T(8,128)(2,1)S(1)} %collective-permute-done.refs_1_), channel_id=1, source_target_pairs={{0,8},{1,9},{2,10},{3,11},{4,12},{5,13},{6,14},{7,15},{8,0},{9,1},... | collective-permute-start | bytes 393224 | tf_op jit(solution)/shard_map/ppermute | solution.py:243
  12.9 6.1 %collective-permute-start.3 = (bf16[64,512]{1,0:T(8,128)(2,1)S(1)}, bf16[64,512]{1,0:T(8,128)(2,1)S(1)}, u32[]{:S(2)}, u32[]{:S(2)}) collective-permute-start(bf16[64,512]{1,0:T(8,128)(2,1)S(1)} %edges.1), channel_id=1, source_target_pairs={{0,2},{1,3},{2,4},{3,5},{4,6},{5,7},{6,0},{7,1},{8,10},{9,11},{10,... | collective-permute-start | bytes 196616 | tf_op jit(solution)/shard_map/ppermute | solution.py:270
  19.0 2.0 %collective-permute-start.8 = (bf16[64,512]{1,0:T(8,128)(2,1)S(1)}, bf16[64,512]{1,0:T(8,128)(2,1)S(1)}, u32[]{:S(2)}, u32[]{:S(2)}) collective-permute-start(bf16[64,512]{1,0:T(8,128)(2,1)S(1)} %later.1.refs_0_), channel_id=1, source_target_pairs={{0,8},{1,9},{2,10},{3,11},{4,12},{5,13},{6,14},{7,15},{8,0},{9,1},... | collective-permute-start | bytes 196616 | tf_op jit(solution)/shard_map/ppermute | solution.py:243
  19.1 6.6 %collective-permute-start.9 = (bf16[64,512]{1,0:T(8,128)(2,1)S(1)}, bf16[64,512]{1,0:T(8,128)(2,1)S(1)}, u32[]{:S(2)}, u32[]{:S(2)}) collective-permute-start(bf16[64,512]{1,0:T(8,128)(2,1)S(1)} %first_lines.1), channel_id=1, source_target_pairs={{0,6},{1,7},{2,0},{3,1},{4,2},{5,3},{6,4},{7,5},{8,14},{9,15},{10,... | collective-permute-start | bytes 196616 | tf_op jit(solution)/shard_map/ppermute | solution.py:281
  21.0 4.7 %copy-start.1 = (bf16[6912,256]{1,0:T(8,128)(2,1)S(1)}, bf16[6912,256]{1,0:T(8,128)(2,1)}, u32[]{:S(2)}) copy-start(bf16[6912,256]{1,0:T(8,128)(2,1)} %w2.1) | copy-start | bytes 10616836
  23.1 9.0 %collective-permute-start.10 = (bf16[432,128]{1,0:T(8,128)(2,1)S(1)}, bf16[432,128]{1,0:T(8,128)(2,1)S(1)}, u32[]{:S(2)}, u32[]{:S(2)}) collective-permute-start(bf16[432,128]{1,0:T(8,128)(2,1)S(1)} %get-tuple-element.22), channel_id=1, source_target_pairs={{0,4},{1,5},{2,6},{3,7},{4,0},{5,1},{6,2},{7,3},{8,12},{9,13},{10,... | collective-permute-start | bytes 331784 | tf_op jit(solution)/shard_map/ppermute | solution.py:320
  23.4 8.7 %collective-permute-start.11 = (bf16[432,128]{1,0:T(8,128)(2,1)S(1)}, bf16[432,128]{1,0:T(8,128)(2,1)S(1)}, u32[]{:S(2)}, u32[]{:S(2)}) collective-permute-start(bf16[432,128]{1,0:T(8,128)(2,1)S(1)} %get-tuple-element.23), channel_id=1, source_target_pairs={{0,6},{1,7},{2,0},{3,1},{4,2},{5,3},{6,4},{7,5},{8,14},{9,15},{10,... | collective-permute-start | bytes 331784 | tf_op jit(solution)/shard_map/ppermute | solution.py:320
  25.7 8.0 %collective-permute-start.12 = (bf16[432,128]{1,0:T(8,128)(2,1)S(1)}, bf16[432,128]{1,0:T(8,128)(2,1)S(1)}, u32[]{:S(2)}, u32[]{:S(2)}) collective-permute-start(bf16[432,128]{1,0:T(8,128)(2,1)S(1)} %get-tuple-element.24), channel_id=1, source_target_pairs={{0,2},{1,3},{2,4},{3,5},{4,6},{5,7},{6,0},{7,1},{8,10},{9,11},{10,... | collective-permute-start | bytes 331784 | tf_op jit(solution)/shard_map/ppermute | solution.py:320

commit v5 on v4

--- a/solution.py
+++ b/solution.py
@@ -109,36 +109,46 @@
     out[...] = lines[...]
 
 
+def silu_t(pre):
+    return (pre * jax.nn.sigmoid(pre)).T.astype(BF16)
+
+
 def inner_kernel(n_x, *refs):
-    *pieces, w_ref, pre, vol, cot = refs
+    *pieces, w_ref, outer, hid, vol, cot, pre = refs
     full = 16 * n_x
     put = putter(vol, cot)
+    vol[:, :2] = jnp.zeros_like(vol[:, :2])
     assemble(n_x, 0, pieces, put)
     for k in range(9):
-        left = vol[k // 3, 2 + k % 3 : k % 3 + 16].reshape(14 * full, 512)
+        left = vol[k // 3, k % 3 : k % 3 + 16].reshape(16 * full, 512)
         term = dot(left, both(w_ref[k * 768 : k * 768 + 768, :]))
         pre[...] = term if k == 0 else pre[...] + term
+    outer[...] = pre[: 2 * full, :]
+    hid[:, : 14 * full] = silu_t(pre[2 * full :, :])
     assemble(n_x, 1, pieces, put)
 
 
 def gradient_kernel(n_x, n_z, groups, strip, block, scale, *refs):
-    beyond_a, beyond_b, w_ref, pre, _, _, vol, cot, own_out, *sends, hid, grad, flat = refs
+    beyond_a, beyond_b, w_ref, outer, _, _, _, vol, cot, hid, own_out, *sends, grad, flat = refs
     gx, core, z, side = place()
     full = 16 * n_x
     put = putter(vol, cot)
     for which in range(2):
         put(which, 0, ring(n_x, core, beyond_a, beyond_b, lambda ref, dx: (ref, dx * 32 + which * 16)))
-    outer = None
-    for k in range(9):
-        left = vol[k // 3, k % 3 : k % 3 + 2].reshape(2 * full, 512)
-        term = dot(left, both(w_ref[k * 768 : k * 768 + 768, :]))
-        outer = term if k == 0 else outer + term
-    inner = jnp.concatenate([outer, pre[...]], axis=0)
-    hid[...] = (inner * jax.nn.sigmoid(inner)).T.astype(BF16)
+    pre, first_line = outer[...], None
+    for a in range(3):
+        left = vol[a, 0:2].reshape(2 * full, 512)
+        w = w_ref[a * 2304 : a * 2304 + 1536, :]
+        pre = pre + dot(left, both(w[:768]))
+        term = dot(left[full:], both(w[768:]))
+        first_line = term if a == 0 else first_line + term
+    pre = jnp.concatenate([pre[:full] + first_line, pre[full:]], axis=0)
+    hid[:, 14 * full :] = silu_t(pre)
     first = lax.div(gx * strip, 3 * CH)
     for k in range(groups):
         ab = jnp.minimum(first + k, 8)
-        right = cot[lax.div(ab, 3), pl.ds(2 - lax.rem(ab, 3), 16)].reshape(16 * full, 512)
+        shift, row = lax.div(ab, 3), 2 - lax.rem(ab, 3)
+        right = jnp.concatenate([cot[shift, pl.ds(row + 2, 14)], cot[shift, pl.ds(row, 2)]], axis=0).reshape(16 * full, 512)
         product = dot(hid[...], right) * scale
         at = k * 3 * CH
         grad[at : at + CH, :] = product[:CH, CH:]
@@ -281,11 +291,13 @@
     after = lax.ppermute(first, AX, perm(lambda x, c, z, y: (x, c, z - 1, y)))
 
     plane = jax.ShapeDtypeStruct((3, 18, full, 512), BF16)
-    pre, vol, cot = pl.pallas_call(
+    columns = jax.ShapeDtypeStruct((512, 16 * full), BF16)
+    outer, hid, vol, cot = pl.pallas_call(
         functools.partial(inner_kernel, n_x),
-        out_shape=[jax.ShapeDtypeStruct((14 * full, 512), F32), plane, plane],
+        out_shape=[jax.ShapeDtypeStruct((2 * full, 512), F32), columns, plane, plane],
         in_specs=[vmem] * (4 * n_x + 1),
-        out_specs=[vmem] * 3,
+        out_specs=[vmem] * 4,
+        scratch_shapes=[pltpu.VMEM((16 * full, 512), F32)],
         compiler_params=params(24),
         cost_estimate=cost(5),
         name="plane_inner",
@@ -298,23 +310,22 @@
         compiler_params=params(4),
         cost_estimate=cost(0),
         name="later",
-    )(beyond, pre)
-    vol, cot, mine, *sends = pl.pallas_call(
+    )(beyond, outer)
+    vol, cot, _, mine, *sends = pl.pallas_call(
         functools.partial(gradient_kernel, n_x, n_z, groups, strip, block, scale),
-        out_shape=[plane, plane, jax.ShapeDtypeStruct((2 * block, 128), F32)]
+        out_shape=[plane, plane, columns, jax.ShapeDtypeStruct((2 * block, 128), F32)]
         + [jax.ShapeDtypeStruct((2 * block, 128), BF16)] * (n_z - 1),
-        in_specs=[vmem] * 6,
-        out_specs=[vmem] * (2 + n_z),
-        input_output_aliases={4: 0, 5: 1},
+        in_specs=[vmem] * 7,
+        out_specs=[vmem] * (3 + n_z),
+        input_output_aliases={4: 0, 5: 1, 6: 2},
         scratch_shapes=[
-            pltpu.VMEM((512, 16 * full), BF16),
             pltpu.VMEM((groups * 3 * CH + (0 if block % 8 == 0 else 16), CH), F32),
             pltpu.VMEM((2 * block, 128), F32),
         ],
         compiler_params=params(24),
         cost_estimate=cost(0),
         name="plane_gradient",
-    )(beyond, across(beyond), first_weight, pre, vol, cot)
+    )(beyond, across(beyond), first_weight, outer, vol, cot, hid)
 
     received = [
         lax.ppermute(sends[k - 1], AX, perm(lambda x, c, z, y, k=k: (x, c, z + k, y)))

time: 34.6 us -> 34.5 us (level)
  waiting for transfers between devices: 10.2 us -> 9.69 us
    ppermute x1, waiting for transfers between devices: 1.73 us -> 1.31 us  [body(): beyond = lax.ppermute(last, AX, perm(lambda x, c, z, y: (x, c, z + 1, y)))]
    pallas_call x1, Pallas kernels: 2.72 us -> 3.13 us  [body(): pl.pallas_call(functools.partial(inner_kernel, n_x), out_shape=[jax.Shape...]
  transfers between devices with their start and end apart: 13 -> 13, of which waited for: 5 -> 5; matrix products, arithmetic and copies ran while one was open for 2% -> 2% of each run, Pallas kernels for 28% -> 29%
where the time goes in v5:
time: 34.5 us; the launch traced here: 34.3 us
  starting transfers between devices  11.3 us (33%)
  Pallas kernels  9.96 us (29%)
  waiting for transfers between devices  9.69 us (28%)
  other arithmetic  1.81 us (5%)
  local copies, waits for them, and re-layouts  0.76 us (2%)
  between operations  0.72 us (2%)
    ppermute x3, waiting for transfers between devices, body(): lax.ppermute(own, AX, perm(lambda x, c, z, y, dx=dx, dy=dy: (x - dx, c, z...  5.91 us
    pallas_call x1, Pallas kernels, body(): pl.pallas_call(local_kernel, out_shape=[jax.ShapeDtypeStruct((sy, sx, 512...  4.69 us
    ppermute x3, starting transfers between devices, body(): lax.ppermute(own, AX, perm(lambda x, c, z, y, dx=dx, dy=dy: (x - dx, c, z...  4.6 us
    pallas_call x1, Pallas kernels, body(): pl.pallas_call(functools.partial(inner_kernel, n_x), out_shape=[jax.Shape...  3.13 us
    ppermute x3, starting transfers between devices, body(): lax.ppermute(sends[k - 1], AX, perm(lambda x, c, z, y, k=k: (x, c, z + k,...  2.52 us
    ppermute x3, waiting for transfers between devices, body(): lax.ppermute(sends[k - 1], AX, perm(lambda x, c, z, y, k=k: (x, c, z + k,...  2.46 us
    ppermute x1, starting transfers between devices, body(): after = lax.ppermute(first, AX, perm(lambda x, c, z, y: (x, c, z - 1, y)))  2.08 us
    pallas_call x1, Pallas kernels, body(): pl.pallas_call(functools.partial(gradient_kernel, n_x, n_z, groups, strip...  1.9 us
  transfers between devices with their start and end apart: 13, of which 5 were waited for; matrix products, arithmetic and copies ran while one was open for 2% of the time, Pallas kernels for 29%

profile of v5, /device:TPU:0, one launch (start us, length us, event | category | flops | bytes accessed | tf_op | source)
XLA Modules:
  0.0 34.3 jit_solution(2728011268906501343)
XLA Ops:
  0.6 1.1 %pad_maximum_fusion.fields = bf16[2,8,8,2,256]{4,3,2,1,0:T(2,128)(2,1)S(1)} fusion(bf16[1,8,8,2,256]{4,3,2,1,0:T(2,128)(2,1)} %bitcast.12, bf16[1,8,8,2,256]{4,3,2,1,0:T(2,128)(2,1)} %bitcast.13), kind=kLoop, calls=%fused_computation.1 | loop fusion | flops 65536 | bytes 262144 | tf_op jit(solution)/shard_map/stack | solution.py:264
  1.7 0.1 lines.1.refs_0_
  1.8 0.0 copy-start
  1.8 4.0 %collective-permute-start.2 = (bf16[128,512]{1,0:T(8,128)(2,1)S(1)}, bf16[128,512]{1,0:T(8,128)(2,1)S(1)}, u32[]{:S(2)}, u32[]{:S(2)}) collective-permute-start(bf16[128,512]{1,0:T(8,128)(2,1)S(1)} %lines.1.refs_0_), channel_id=1, source_target_pairs={{0,17},{1,16},{2,19},{3,18},{4,21},{5,20},{6,23},{7,22},{8,25},{9,... | collective-permute-start | bytes 393224 | tf_op jit(solution)/shard_map/ppermute | solution.py:269
  5.8 0.5 %collective-permute-start.1 = (bf16[128,512]{1,0:T(8,128)(2,1)S(1)}, bf16[128,512]{1,0:T(8,128)(2,1)S(1)}, u32[]{:S(2)}, u32[]{:S(2)}) collective-permute-start(bf16[128,512]{1,0:T(8,128)(2,1)S(1)} %lines.1.refs_0_), channel_id=1, source_target_pairs={{0,16},{1,17},{2,18},{3,19},{4,20},{5,21},{6,22},{7,23},{8,24},{9,... | collective-permute-start | bytes 393224 | tf_op jit(solution)/shard_map/ppermute | solution.py:269
  6.3 0.1 collective-permute-start
  6.4 3.7 %collective-permute-done.2.refs_3_ = bf16[128,512]{1,0:T(8,128)(2,1)S(1)} collective-permute-done((bf16[128,512]{1,0:T(8,128)(2,1)S(1)}, bf16[128,512]{1,0:T(8,128)(2,1)S(1)}, u32[]{:S(2)}, u32[]{:S(2)}) %collective-permute-start.2) | collective-permute-done | bytes 131104 | tf_op jit(solution)/shard_map/ppermute | solution.py:269
  10.1 0.0 collective-permute-start.7
  10.1 2.2 %collective-permute-done.1.refs_2_ = bf16[128,512]{1,0:T(8,128)(2,1)S(1)} collective-permute-done((bf16[128,512]{1,0:T(8,128)(2,1)S(1)}, bf16[128,512]{1,0:T(8,128)(2,1)S(1)}, u32[]{:S(2)}, u32[]{:S(2)}) %collective-permute-start.1) | collective-permute-done | bytes 131104 | tf_op jit(solution)/shard_map/ppermute | solution.py:269
  12.3 0.0 collective-permute-start.6
  12.4 0.0 collective-permute-done.refs_1_
  12.4 0.5 %collective-permute-start.5 = (bf16[128,512]{1,0:T(8,128)(2,1)S(1)}, bf16[128,512]{1,0:T(8,128)(2,1)S(1)}, u32[]{:S(2)}, u32[]{:S(2)}) collective-permute-start(bf16[128,512]{1,0:T(8,128)(2,1)S(1)} %collective-permute-done.refs_1_), channel_id=1, source_target_pairs={{0,8},{1,9},{2,10},{3,11},{4,12},{5,13},{6,14},{7,15},{8,0},{9,1},... | collective-permute-start | bytes 393224 | tf_op jit(solution)/shard_map/ppermute | solution.py:253
  12.9 1.6 %collective-permute-start.3 = (bf16[64,512]{1,0:T(8,128)(2,1)S(1)}, bf16[64,512]{1,0:T(8,128)(2,1)S(1)}, u32[]{:S(2)}, u32[]{:S(2)}) collective-permute-start(bf16[64,512]{1,0:T(8,128)(2,1)S(1)} %edges.1), channel_id=1, source_target_pairs={{0,2},{1,3},{2,4},{3,5},{4,6},{5,7},{6,0},{7,1},{8,10},{9,11},{10,... | collective-permute-start | bytes 196616 | tf_op jit(solution)/shard_map/ppermute | solution.py:280
  14.5 0.0 collective-permute-done.4.refs_4_
  14.5 0.0 collective-permute-done.7.refs_7_
  14.5 0.0 collective-permute-done.6.refs_6_
  14.5 0.0 collective-permute-done.5.refs_5_
  14.5 3.1 %plane_inner.1 = (f32[64,512]{1,0:T(8,128)S(1)}, bf16[512,512]{1,0:T(8,128)(2,1)S(1)}, bf16[3,18,32,512]{3,2,1,0:T(8,128)(2,1)S(1)}, bf16[3,18,32,512]{3,2,1,0:T(8,128)(2,1)S(1)}) custom-call(bf16[128,512]{1,0:T(8,128)(2,1)S(1)} %lines.1.refs_0_, bf16[128,512]{1,0:T(8,128)(2,1)S(1)} %collective-permute-done.refs_1_, ...), custom_call_target="tpu_custom_call" | custom-call | flops 5000000000 | bytes 15000000 | tf_op jit(solution)/shard_map/plane_inner/pallas_call | solution.py:295
  17.7 1.3 %collective-permute-done.3.lines = bf16[64,512]{1,0:T(8,128)(2,1)S(1)} collective-permute-done((bf16[64,512]{1,0:T(8,128)(2,1)S(1)}, bf16[64,512]{1,0:T(8,128)(2,1)S(1)}, u32[]{:S(2)}, u32[]{:S(2)}) %collective-permute-start.3) | collective-permute-done | bytes 65568 | tf_op jit(solution)/shard_map/ppermute | solution.py:280
  19.0 0.0 collective-permute-start.8
  19.0 0.1 first_lines.1
  19.1 2.1 %collective-permute-start.9 = (bf16[64,512]{1,0:T(8,128)(2,1)S(1)}, bf16[64,512]{1,0:T(8,128)(2,1)S(1)}, u32[]{:S(2)}, u32[]{:S(2)}) collective-permute-start(bf16[64,512]{1,0:T(8,128)(2,1)S(1)} %first_lines.1), channel_id=1, source_target_pairs={{0,6},{1,7},{2,0},{3,1},{4,2},{5,3},{6,4},{7,5},{8,14},{9,15},{10,... | collective-permute-start | bytes 196616 | tf_op jit(solution)/shard_map/ppermute | solution.py:291
  21.2 0.0 collective-permute-done.8.refs_1_
  21.2 1.9 %plane_gradient.1 = (bf16[3,18,32,512]{3,2,1,0:T(8,128)(2,1)S(1)}, bf16[3,18,32,512]{3,2,1,0:T(8,128)(2,1)S(1)}, bf16[512,512]{1,0:T(8,128)(2,1)S(1)}, f32[432,1...) custom-call(bf16[64,512]{1,0:T(8,128)(2,1)S(1)} %later.1.refs_0_, ...), custom_call_target="tpu_custom_call", output_to_operand_aliasing={{0}: (4, {}), {1}: (5, {}), {2}: (6, {})} | custom-call | tf_op jit(solution)/shard_map/plane_gradient/pallas_call | solution.py:314
  23.1 0.5 %collective-permute-start.10 = (bf16[432,128]{1,0:T(8,128)(2,1)S(1)}, bf16[432,128]{1,0:T(8,128)(2,1)S(1)}, u32[]{:S(2)}, u32[]{:S(2)}) collective-permute-start(bf16[432,128]{1,0:T(8,128)(2,1)S(1)} %get-tuple-element.24), channel_id=1, source_target_pairs={{0,4},{1,5},{2,6},{3,7},{4,0},{5,1},{6,2},{7,3},{8,12},{9,13},{10,... | collective-permute-start | bytes 331784 | tf_op jit(solution)/shard_map/ppermute | solution.py:331
  23.6 1.9 %collective-permute-start.11 = (bf16[432,128]{1,0:T(8,128)(2,1)S(1)}, bf16[432,128]{1,0:T(8,128)(2,1)S(1)}, u32[]{:S(2)}, u32[]{:S(2)}) collective-permute-start(bf16[432,128]{1,0:T(8,128)(2,1)S(1)} %get-tuple-element.25), channel_id=1, source_target_pairs={{0,6},{1,7},{2,0},{3,1},{4,2},{5,3},{6,4},{7,5},{8,14},{9,15},{10,... | collective-permute-start | bytes 331784 | tf_op jit(solution)/shard_map/ppermute | solution.py:331
  25.5 0.1 collective-permute-start.12
  25.6 4.7 %local_convolutions.1 = (bf16[8,8,512]{2,1,0:T(8,128)(2,1)S(1)}, bf16[8,8,512]{2,1,0:T(8,128)(2,1)S(1)}) custom-call(bf16[3,18,32,512]{3,2,1,0:T(8,128)(2,1)S(1)} %get-tuple-element.19.vol_ref, bf16[3,18,32,512]{3,2,1,0:T(8,128)(2,1)S(1)} %get-tuple-element.20.cot_ref, bf16[64,512]{1,0:T(8,128)(2,1)S(1)} %collective-permute-done.9.after_ref, ...), custom_call_target="tpu_custom_call" | custom-call | tf_op jit(solution)/shard_map/local_convolutions/pallas_call | solution.py:335
  30.3 0.8 %copy_bitcast_fusion = (bf16[8,8,2,256]{3,2,1,0:T(2,128)(2,1)}, bf16[8,8,2,256]{3,2,1,0:T(2,128)(2,1)}) fusion(bf16[8,8,2,256]{3,1,2,0:T(8,128)(2,1)S(1)} %bitcast.11, bf16[8,8,2,256]{3,1,2,0:T(8,128)(2,1)S(1)} %bitcast.10), kind=kLoop, calls=%fused_computation.2 | loop fusion | bytes 262144 | tf_op jit(solution)/shard_map/transpose | solution.py:353
  31.1 0.8 %collective-permute-done.10 = bf16[432,128]{1,0:T(8,128)(2,1)S(1)} collective-permute-done((bf16[432,128]{1,0:T(8,128)(2,1)S(1)}, bf16[432,128]{1,0:T(8,128)(2,1)S(1)}, u32[]{:S(2)}, u32[]{:S(2)}) %collective-permute-start.10) | collective-permute-done | bytes 110624 | tf_op jit(solution)/shard_map/ppermute | solution.py:331
  31.9 1.7 %collective-permute-done.12 = bf16[432,128]{1,0:T(8,128)(2,1)S(1)} collective-permute-done((bf16[432,128]{1,0:T(8,128)(2,1)S(1)}, bf16[432,128]{1,0:T(8,128)(2,1)S(1)}, u32[]{:S(2)}, u32[]{:S(2)}) %collective-permute-start.12) | collective-permute-done | bytes 110624 | tf_op jit(solution)/shard_map/ppermute | solution.py:331
  33.5 0.7 %add_bitcast_fusion = f32[55296]{0:T(1024)} fusion(bf16[432,128]{1,0:T(8,128)(2,1)S(1)} %collective-permute-done.12, bf16[432,128]{1,0:T(8,128)(2,1)S(1)} %collective-permute-done.11, f32[432,128]{1,0:T(8,128)S(1)} %get-tuple-element.23, bf16[432,128]{1,0:T(8,128)(2,1)S(1)} %collective-permute-done.10), kind=kLoop, calls=%fused_computation | loop fusion | flops 331776 | bytes 774144 | tf_op jit(solution)/shard_map/reshape | solution.py:358
  (8 shorter events, 0.0 us)
Async XLA Ops:
  1.8 12.7 %copy-start = (bf16[6912,256]{1,0:T(8,128)(2,1)S(1)}, bf16[6912,256]{1,0:T(8,128)(2,1)}, u32[]{:S(2)}) copy-start(bf16[6912,256]{1,0:T(8,128)(2,1)} %w1.1) | copy-start | bytes 10616836
  1.8 8.3 %collective-permute-start.2 = (bf16[128,512]{1,0:T(8,128)(2,1)S(1)}, bf16[128,512]{1,0:T(8,128)(2,1)S(1)}, u32[]{:S(2)}, u32[]{:S(2)}) collective-permute-start(bf16[128,512]{1,0:T(8,128)(2,1)S(1)} %lines.1.refs_0_), channel_id=1, source_target_pairs={{0,17},{1,16},{2,19},{3,18},{4,21},{5,20},{6,23},{7,22},{8,25},{9,... | collective-permute-start | bytes 393224 | tf_op jit(solution)/shard_map/ppermute | solution.py:269
  5.8 6.6 %collective-permute-start.1 = (bf16[128,512]{1,0:T(8,128)(2,1)S(1)}, bf16[128,512]{1,0:T(8,128)(2,1)S(1)}, u32[]{:S(2)}, u32[]{:S(2)}) collective-permute-start(bf16[128,512]{1,0:T(8,128)(2,1)S(1)} %lines.1.refs_0_), channel_id=1, source_target_pairs={{0,16},{1,17},{2,18},{3,19},{4,20},{5,21},{6,22},{7,23},{8,24},{9,... | collective-permute-start | bytes 393224 | tf_op jit(solution)/shard_map/ppermute | solution.py:269
  6.3 6.0 %collective-permute-start = (bf16[128,512]{1,0:T(8,128)(2,1)S(1)}, bf16[128,512]{1,0:T(8,128)(2,1)S(1)}, u32[]{:S(2)}, u32[]{:S(2)}) collective-permute-start(bf16[128,512]{1,0:T(8,128)(2,1)S(1)} %lines.1.refs_0_), channel_id=1, source_target_pairs={{0,1},{1,0},{2,3},{3,2},{4,5},{5,4},{6,7},{7,6},{8,9},{9,8},{10,11... | collective-permute-start | bytes 393224 | tf_op jit(solution)/shard_map/ppermute | solution.py:269
  6.4 8.1 %collective-permute-start.4 = (bf16[128,512]{1,0:T(8,128)(2,1)S(1)}, bf16[128,512]{1,0:T(8,128)(2,1)S(1)}, u32[]{:S(2)}, u32[]{:S(2)}) collective-permute-start(bf16[128,512]{1,0:T(8,128)(2,1)S(1)} %lines.1.refs_0_), channel_id=1, source_target_pairs={{0,8},{1,9},{2,10},{3,11},{4,12},{5,13},{6,14},{7,15},{8,0},{9,1},... | collective-permute-start | bytes 393224 | tf_op jit(solution)/shard_map/ppermute | solution.py:253
  10.1 4.4 %collective-permute-start.7 = (bf16[128,512]{1,0:T(8,128)(2,1)S(1)}, bf16[128,512]{1,0:T(8,128)(2,1)S(1)}, u32[]{:S(2)}, u32[]{:S(2)}) collective-permute-start(bf16[128,512]{1,0:T(8,128)(2,1)S(1)} %collective-permute-done.2.refs_3_), channel_id=1, source_target_pairs={{0,8},{1,9},{2,10},{3,11},{4,12},{5,13},{6,14},{7,15},{8,0},{9,1},... | collective-permute-start | bytes 393224 | tf_op jit(solution)/shard_map/ppermute | solution.py:253
  12.3 2.2 %collective-permute-start.6 = (bf16[128,512]{1,0:T(8,128)(2,1)S(1)}, bf16[128,512]{1,0:T(8,128)(2,1)S(1)}, u32[]{:S(2)}, u32[]{:S(2)}) collective-permute-start(bf16[128,512]{1,0:T(8,128)(2,1)S(1)} %collective-permute-done.1.refs_2_), channel_id=1, source_target_pairs={{0,8},{1,9},{2,10},{3,11},{4,12},{5,13},{6,14},{7,15},{8,0},{9,1},... | collective-permute-start | bytes 393224 | tf_op jit(solution)/shard_map/ppermute | solution.py:253
  12.4 2.2 %collective-permute-start.5 = (bf16[128,512]{1,0:T(8,128)(2,1)S(1)}, bf16[128,512]{1,0:T(8,128)(2,1)S(1)}, u32[]{:S(2)}, u32[]{:S(2)}) collective-permute-start(bf16[128,512]{1,0:T(8,128)(2,1)S(1)} %collective-permute-done.refs_1_), channel_id=1, source_target_pairs={{0,8},{1,9},{2,10},{3,11},{4,12},{5,13},{6,14},{7,15},{8,0},{9,1},... | collective-permute-start | bytes 393224 | tf_op jit(solution)/shard_map/ppermute | solution.py:253
  12.9 6.1 %collective-permute-start.3 = (bf16[64,512]{1,0:T(8,128)(2,1)S(1)}, bf16[64,512]{1,0:T(8,128)(2,1)S(1)}, u32[]{:S(2)}, u32[]{:S(2)}) collective-permute-start(bf16[64,512]{1,0:T(8,128)(2,1)S(1)} %edges.1), channel_id=1, source_target_pairs={{0,2},{1,3},{2,4},{3,5},{4,6},{5,7},{6,0},{7,1},{8,10},{9,11},{10,... | collective-permute-start | bytes 196616 | tf_op jit(solution)/shard_map/ppermute | solution.py:280
  19.0 2.2 %collective-permute-start.8 = (bf16[64,512]{1,0:T(8,128)(2,1)S(1)}, bf16[64,512]{1,0:T(8,128)(2,1)S(1)}, u32[]{:S(2)}, u32[]{:S(2)}) collective-permute-start(bf16[64,512]{1,0:T(8,128)(2,1)S(1)} %later.1.refs_0_), channel_id=1, source_target_pairs={{0,8},{1,9},{2,10},{3,11},{4,12},{5,13},{6,14},{7,15},{8,0},{9,1},... | collective-permute-start | bytes 196616 | tf_op jit(solution)/shard_map/ppermute | solution.py:253
  19.1 6.5 %collective-permute-start.9 = (bf16[64,512]{1,0:T(8,128)(2,1)S(1)}, bf16[64,512]{1,0:T(8,128)(2,1)S(1)}, u32[]{:S(2)}, u32[]{:S(2)}) collective-permute-start(bf16[64,512]{1,0:T(8,128)(2,1)S(1)} %first_lines.1), channel_id=1, source_target_pairs={{0,6},{1,7},{2,0},{3,1},{4,2},{5,3},{6,4},{7,5},{8,14},{9,15},{10,... | collective-permute-start | bytes 196616 | tf_op jit(solution)/shard_map/ppermute | solution.py:291
  21.2 4.4 %copy-start.1 = (bf16[6912,256]{1,0:T(8,128)(2,1)S(1)}, bf16[6912,256]{1,0:T(8,128)(2,1)}, u32[]{:S(2)}) copy-start(bf16[6912,256]{1,0:T(8,128)(2,1)} %w2.1) | copy-start | bytes 10616836
  23.1 8.8 %collective-permute-start.10 = (bf16[432,128]{1,0:T(8,128)(2,1)S(1)}, bf16[432,128]{1,0:T(8,128)(2,1)S(1)}, u32[]{:S(2)}, u32[]{:S(2)}) collective-permute-start(bf16[432,128]{1,0:T(8,128)(2,1)S(1)} %get-tuple-element.24), channel_id=1, source_target_pairs={{0,4},{1,5},{2,6},{3,7},{4,0},{5,1},{6,2},{7,3},{8,12},{9,13},{10,... | collective-permute-start | bytes 331784 | tf_op jit(solution)/shard_map/ppermute | solution.py:331
  23.6 8.3 %collective-permute-start.11 = (bf16[432,128]{1,0:T(8,128)(2,1)S(1)}, bf16[432,128]{1,0:T(8,128)(2,1)S(1)}, u32[]{:S(2)}, u32[]{:S(2)}) collective-permute-start(bf16[432,128]{1,0:T(8,128)(2,1)S(1)} %get-tuple-element.25), channel_id=1, source_target_pairs={{0,6},{1,7},{2,0},{3,1},{4,2},{5,3},{6,4},{7,5},{8,14},{9,15},{10,... | collective-permute-start | bytes 331784 | tf_op jit(solution)/shard_map/ppermute | solution.py:331
  25.5 8.0 %collective-permute-start.12 = (bf16[432,128]{1,0:T(8,128)(2,1)S(1)}, bf16[432,128]{1,0:T(8,128)(2,1)S(1)}, u32[]{:S(2)}, u32[]{:S(2)}) collective-permute-start(bf16[432,128]{1,0:T(8,128)(2,1)S(1)} %get-tuple-element.26), channel_id=1, source_target_pairs={{0,2},{1,3},{2,4},{3,5},{4,6},{5,7},{6,0},{7,1},{8,10},{9,11},{10,... | collective-permute-start | bytes 331784 | tf_op jit(solution)/shard_map/ppermute | solution.py:331

commit v6 on v5

--- a/solution.py
+++ b/solution.py
@@ -129,26 +129,29 @@
 
 
 def gradient_kernel(n_x, n_z, groups, strip, block, scale, *refs):
-    beyond_a, beyond_b, w_ref, outer, _, _, _, vol, cot, hid, own_out, *sends, grad, flat = refs
+    beyond_a, beyond_b, w_ref, outer, cot, hid_ref, near_vol, near_cot, own_out, *sends, hid, ends, grad, flat = refs
     gx, core, z, side = place()
     full = 16 * n_x
-    put = putter(vol, cot)
+    put = putter(near_vol, near_cot)
     for which in range(2):
         put(which, 0, ring(n_x, core, beyond_a, beyond_b, lambda ref, dx: (ref, dx * 32 + which * 16)))
+    ends[:, :2] = near_cot[...]
+    ends[:, 2:] = cot[:, 2:4]
     pre, first_line = outer[...], None
     for a in range(3):
-        left = vol[a, 0:2].reshape(2 * full, 512)
+        left = near_vol[a].reshape(2 * full, 512)
         w = w_ref[a * 2304 : a * 2304 + 1536, :]
         pre = pre + dot(left, both(w[:768]))
         term = dot(left[full:], both(w[768:]))
         first_line = term if a == 0 else first_line + term
     pre = jnp.concatenate([pre[:full] + first_line, pre[full:]], axis=0)
+    hid[...] = hid_ref[...]
     hid[:, 14 * full :] = silu_t(pre)
     first = lax.div(gx * strip, 3 * CH)
     for k in range(groups):
         ab = jnp.minimum(first + k, 8)
         shift, row = lax.div(ab, 3), 2 - lax.rem(ab, 3)
-        right = jnp.concatenate([cot[shift, pl.ds(row + 2, 14)], cot[shift, pl.ds(row, 2)]], axis=0).reshape(16 * full, 512)
+        right = jnp.concatenate([cot[shift, pl.ds(row + 2, 14)], ends[shift, pl.ds(row, 2)]], axis=0).reshape(16 * full, 512)
         product = dot(hid[...], right) * scale
         at = k * 3 * CH
         grad[at : at + CH, :] = product[:CH, CH:]
@@ -184,16 +187,17 @@
         out[which * 32 : which * 32 + 32, :] = lines.reshape(32, 512).astype(BF16)
 
 
-def local_kernel(vol_ref, cot_ref, after_ref, w1, w2, out_ref, vgrad_ref, vol, hid, cot, thr, acc):
+def local_kernel(vol_ref, cot_ref, near_vol, near_cot, after_ref, w1, w2, out_ref, vgrad_ref, vol, hid, cot, thr, acc):
     _, core, _, side = place()
 
-    def cut(which, ref):
-        lines = window(ref[1, pl.ds(side * 8, 10)].astype(F32), core)
+    def cut(which, ref, near):
+        before = jnp.where(side == 0, near[1].astype(F32), ref[1, 8:10].astype(F32))
+        lines = [before, ref[1, pl.ds(2 + side * 8, 8)].astype(F32)]
         after = after_ref[which * 32 : which * 32 + 32, :].astype(F32).reshape(2, 16, 512)
         after = jnp.where(side == 0, window(ref[1, 10:12].astype(F32), core), after)
-        return jnp.concatenate([lines, after], axis=0)
-
-    v, c = cut(0, vol_ref), cut(1, cot_ref)
+        return jnp.concatenate([window(jnp.concatenate(lines, axis=0), core), after], axis=0)
+
+    v, c = cut(0, vol_ref, near_vol), cut(1, cot_ref, near_cot)
     for s in range(3):
         vol[s] = shifted(v, s - 1).astype(BF16)
         cot[s] = shifted(c, s - 1).astype(BF16)
@@ -311,21 +315,23 @@
         cost_estimate=cost(0),
         name="later",
     )(beyond, outer)
-    vol, cot, _, mine, *sends = pl.pallas_call(
+    near = jax.ShapeDtypeStruct((3, 2, full, 512), BF16)
+    near_vol, near_cot, mine, *sends = pl.pallas_call(
         functools.partial(gradient_kernel, n_x, n_z, groups, strip, block, scale),
-        out_shape=[plane, plane, columns, jax.ShapeDtypeStruct((2 * block, 128), F32)]
+        out_shape=[near, near, jax.ShapeDtypeStruct((2 * block, 128), F32)]
         + [jax.ShapeDtypeStruct((2 * block, 128), BF16)] * (n_z - 1),
-        in_specs=[vmem] * 7,
-        out_specs=[vmem] * (3 + n_z),
-        input_output_aliases={4: 0, 5: 1, 6: 2},
+        in_specs=[vmem] * 6,
+        out_specs=[vmem] * (2 + n_z),
         scratch_shapes=[
+            pltpu.VMEM((512, 16 * full), BF16),
+            pltpu.VMEM((3, 4, full, 512), BF16),
             pltpu.VMEM((groups * 3 * CH + (0 if block % 8 == 0 else 16), CH), F32),
             pltpu.VMEM((2 * block, 128), F32),
         ],
         compiler_params=params(24),
         cost_estimate=cost(0),
         name="plane_gradient",
-    )(beyond, across(beyond), first_weight, outer, vol, cot, hid)
+    )(beyond, across(beyond), first_weight, outer, cot, hid)
 
     received = [
         lax.ppermute(sends[k - 1], AX, perm(lambda x, c, z, y, k=k: (x, c, z + k, y)))
@@ -335,7 +341,7 @@
     output, volume_grad = pl.pallas_call(
         local_kernel,
         out_shape=[jax.ShapeDtypeStruct((sy, sx, 512), BF16)] * 2,
-        in_specs=[vmem] * 5,
+        in_specs=[vmem] * 7,
         out_specs=[vmem] * 2,
         scratch_shapes=[
             pltpu.VMEM((3, 12, 16, 512), BF16),
@@ -347,7 +353,7 @@
         compiler_params=params(24),
         cost_estimate=cost(0),
         name="local_convolutions",
-    )(vol, cot, after, first_weight, second_weight)
+    )(vol, cot, near_vol, near_cot, after, first_weight, second_weight)
 
     def cells(v):
         return jnp.transpose(v.reshape(sy, sx, sz, chans), (1, 0, 2, 3))

time: 34.5 us -> 34.5 us (level)
  no operation moved by 1% of the time
where the time goes in v6:
time: 34.5 us; the launch traced here: 34.4 us
  starting transfers between devices  11.3 us (33%)
  Pallas kernels  9.95 us (29%)
  waiting for transfers between devices  9.77 us (28%)
  other arithmetic  1.8 us (5%)
  local copies, waits for them, and re-layouts  0.76 us (2%)
  between operations  0.73 us (2%)
    ppermute x3, waiting for transfers between devices, body(): lax.ppermute(own, AX, perm(lambda x, c, z, y, dx=dx, dy=dy: (x - dx, c, z...  5.91 us
    pallas_call x1, Pallas kernels, body(): pl.pallas_call(local_kernel, out_shape=[jax.ShapeDtypeStruct((sy, sx, 512...  4.69 us
    ppermute x3, starting transfers between devices, body(): lax.ppermute(own, AX, perm(lambda x, c, z, y, dx=dx, dy=dy: (x - dx, c, z...  4.6 us
    pallas_call x1, Pallas kernels, body(): pl.pallas_call(functools.partial(inner_kernel, n_x), out_shape=[jax.Shape...  3.13 us
    ppermute x3, waiting for transfers between devices, body(): lax.ppermute(sends[k - 1], AX, perm(lambda x, c, z, y, k=k: (x, c, z + k,...  2.53 us
    ppermute x3, starting transfers between devices, body(): lax.ppermute(sends[k - 1], AX, perm(lambda x, c, z, y, k=k: (x, c, z + k,...  2.51 us
    ppermute x1, starting transfers between devices, body(): after = lax.ppermute(first, AX, perm(lambda x, c, z, y: (x, c, z - 1, y)))  2.02 us
    pallas_call x1, Pallas kernels, body(): pl.pallas_call(functools.partial(gradient_kernel, n_x, n_z, groups, strip...  1.89 us
  transfers between devices with their start and end apart: 13, of which 5 were waited for; matrix products, arithmetic and copies ran while one was open for 2% of the time, Pallas kernels for 29%

profile of v6, /device:TPU:0, one launch (start us, length us, event | category | flops | bytes accessed | tf_op | source)
XLA Modules:
  0.0 34.4 jit_solution(11672710418377033438)
XLA Ops:
  0.6 1.1 %pad_maximum_fusion.fields = bf16[2,8,8,2,256]{4,3,2,1,0:T(2,128)(2,1)S(1)} fusion(bf16[1,8,8,2,256]{4,3,2,1,0:T(2,128)(2,1)} %bitcast.12, bf16[1,8,8,2,256]{4,3,2,1,0:T(2,128)(2,1)} %bitcast.13), kind=kLoop, calls=%fused_computation.1 | loop fusion | flops 65536 | bytes 262144 | tf_op jit(solution)/shard_map/stack | solution.py:268
  1.7 0.1 lines.1.refs_0_
  1.8 0.0 copy-start
  1.8 4.0 %collective-permute-start.2 = (bf16[128,512]{1,0:T(8,128)(2,1)S(1)}, bf16[128,512]{1,0:T(8,128)(2,1)S(1)}, u32[]{:S(2)}, u32[]{:S(2)}) collective-permute-start(bf16[128,512]{1,0:T(8,128)(2,1)S(1)} %lines.1.refs_0_), channel_id=1, source_target_pairs={{0,17},{1,16},{2,19},{3,18},{4,21},{5,20},{6,23},{7,22},{8,25},{9,... | collective-permute-start | bytes 393224 | tf_op jit(solution)/shard_map/ppermute | solution.py:273
  5.8 0.5 %collective-permute-start.1 = (bf16[128,512]{1,0:T(8,128)(2,1)S(1)}, bf16[128,512]{1,0:T(8,128)(2,1)S(1)}, u32[]{:S(2)}, u32[]{:S(2)}) collective-permute-start(bf16[128,512]{1,0:T(8,128)(2,1)S(1)} %lines.1.refs_0_), channel_id=1, source_target_pairs={{0,16},{1,17},{2,18},{3,19},{4,20},{5,21},{6,22},{7,23},{8,24},{9,... | collective-permute-start | bytes 393224 | tf_op jit(solution)/shard_map/ppermute | solution.py:273
  6.3 0.1 collective-permute-start
  6.4 0.0 collective-permute-start.3
  6.4 3.7 %collective-permute-done.2.refs_3_ = bf16[128,512]{1,0:T(8,128)(2,1)S(1)} collective-permute-done((bf16[128,512]{1,0:T(8,128)(2,1)S(1)}, bf16[128,512]{1,0:T(8,128)(2,1)S(1)}, u32[]{:S(2)}, u32[]{:S(2)}) %collective-permute-start.2) | collective-permute-done | bytes 131104 | tf_op jit(solution)/shard_map/ppermute | solution.py:273
  10.1 0.0 collective-permute-start.6
  10.1 2.2 %collective-permute-done.1.refs_2_ = bf16[128,512]{1,0:T(8,128)(2,1)S(1)} collective-permute-done((bf16[128,512]{1,0:T(8,128)(2,1)S(1)}, bf16[128,512]{1,0:T(8,128)(2,1)S(1)}, u32[]{:S(2)}, u32[]{:S(2)}) %collective-permute-start.1) | collective-permute-done | bytes 131104 | tf_op jit(solution)/shard_map/ppermute | solution.py:273
  12.3 0.0 collective-permute-start.5
  12.4 0.0 collective-permute-done.refs_1_
  12.4 0.5 %collective-permute-start.4 = (bf16[128,512]{1,0:T(8,128)(2,1)S(1)}, bf16[128,512]{1,0:T(8,128)(2,1)S(1)}, u32[]{:S(2)}, u32[]{:S(2)}) collective-permute-start(bf16[128,512]{1,0:T(8,128)(2,1)S(1)} %collective-permute-done.refs_1_), channel_id=1, source_target_pairs={{0,8},{1,9},{2,10},{3,11},{4,12},{5,13},{6,14},{7,15},{8,0},{9,1},... | collective-permute-start | bytes 393224 | tf_op jit(solution)/shard_map/ppermute | solution.py:257
  12.9 1.6 %collective-permute-start.7 = (bf16[64,512]{1,0:T(8,128)(2,1)S(1)}, bf16[64,512]{1,0:T(8,128)(2,1)S(1)}, u32[]{:S(2)}, u32[]{:S(2)}) collective-permute-start(bf16[64,512]{1,0:T(8,128)(2,1)S(1)} %edges.1), channel_id=1, source_target_pairs={{0,2},{1,3},{2,4},{3,5},{4,6},{5,7},{6,0},{7,1},{8,10},{9,11},{10,... | collective-permute-start | bytes 196616 | tf_op jit(solution)/shard_map/ppermute | solution.py:284
  14.5 0.0 collective-permute-done.3.refs_4_
  14.5 0.0 collective-permute-done.6.refs_7_
  14.5 0.0 collective-permute-done.5.refs_6_
  14.5 0.0 collective-permute-done.4.refs_5_
  14.5 3.1 %plane_inner.1 = (f32[64,512]{1,0:T(8,128)S(1)}, bf16[512,512]{1,0:T(8,128)(2,1)S(1)}, bf16[3,18,32,512]{3,2,1,0:T(8,128)(2,1)S(1)}, bf16[3,18,32,512]{3,2,1,0:T(8,128)(2,1)S(1)}) custom-call(bf16[128,512]{1,0:T(8,128)(2,1)S(1)} %lines.1.refs_0_, bf16[128,512]{1,0:T(8,128)(2,1)S(1)} %collective-permute-done.refs_1_, ...), custom_call_target="tpu_custom_call" | custom-call | flops 5000000000 | bytes 15000000 | tf_op jit(solution)/shard_map/plane_inner/pallas_call | solution.py:299
  17.7 1.3 %collective-permute-done.7.lines = bf16[64,512]{1,0:T(8,128)(2,1)S(1)} collective-permute-done((bf16[64,512]{1,0:T(8,128)(2,1)S(1)}, bf16[64,512]{1,0:T(8,128)(2,1)S(1)}, u32[]{:S(2)}, u32[]{:S(2)}) %collective-permute-start.7) | collective-permute-done | bytes 65568 | tf_op jit(solution)/shard_map/ppermute | solution.py:284
  19.0 0.1 collective-permute-start.8
  19.1 0.1 first_lines.1
  19.2 2.0 %collective-permute-start.9 = (bf16[64,512]{1,0:T(8,128)(2,1)S(1)}, bf16[64,512]{1,0:T(8,128)(2,1)S(1)}, u32[]{:S(2)}, u32[]{:S(2)}) collective-permute-start(bf16[64,512]{1,0:T(8,128)(2,1)S(1)} %first_lines.1), channel_id=1, source_target_pairs={{0,6},{1,7},{2,0},{3,1},{4,2},{5,3},{6,4},{7,5},{8,14},{9,15},{10,... | collective-permute-start | bytes 196616 | tf_op jit(solution)/shard_map/ppermute | solution.py:295
  21.2 1.9 %plane_gradient.1 = (bf16[3,2,32,512]{3,2,1,0:T(8,128)(2,1)S(1)}, bf16[3,2,32,512]{3,2,1,0:T(8,128)(2,1)S(1)}, f32[432,128]{1,0:T(8,128)S(1)}, bf16[432,128]{1,0...) custom-call(bf16[64,512]{1,0:T(8,128)(2,1)S(1)} %later.1.refs_0_, ...), custom_call_target="tpu_custom_call" | custom-call | tf_op jit(solution)/shard_map/plane_gradient/pallas_call | solution.py:319
  23.1 0.5 %collective-permute-start.10 = (bf16[432,128]{1,0:T(8,128)(2,1)S(1)}, bf16[432,128]{1,0:T(8,128)(2,1)S(1)}, u32[]{:S(2)}, u32[]{:S(2)}) collective-permute-start(bf16[432,128]{1,0:T(8,128)(2,1)S(1)} %get-tuple-element.24), channel_id=1, source_target_pairs={{0,4},{1,5},{2,6},{3,7},{4,0},{5,1},{6,2},{7,3},{8,12},{9,13},{10,... | collective-permute-start | bytes 331784 | tf_op jit(solution)/shard_map/ppermute | solution.py:337
  23.6 2.0 %collective-permute-start.11 = (bf16[432,128]{1,0:T(8,128)(2,1)S(1)}, bf16[432,128]{1,0:T(8,128)(2,1)S(1)}, u32[]{:S(2)}, u32[]{:S(2)}) collective-permute-start(bf16[432,128]{1,0:T(8,128)(2,1)S(1)} %get-tuple-element.25), channel_id=1, source_target_pairs={{0,6},{1,7},{2,0},{3,1},{4,2},{5,3},{6,4},{7,5},{8,14},{9,15},{10,... | collective-permute-start | bytes 331784 | tf_op jit(solution)/shard_map/ppermute | solution.py:337
  25.6 0.0 collective-permute-start.12
  25.6 4.7 %local_convolutions.1 = (bf16[8,8,512]{2,1,0:T(8,128)(2,1)S(1)}, bf16[8,8,512]{2,1,0:T(8,128)(2,1)S(1)}) custom-call(bf16[3,18,32,512]{3,2,1,0:T(8,128)(2,1)S(1)} %get-tuple-element.15.vol_ref, bf16[3,18,32,512]{3,2,1,0:T(8,128)(2,1)S(1)} %get-tuple-element.16.refs_4_.cot_ref, bf16[3,2,32,512]{3,2,1,0:T(8,128)(2,1)S(1)} %get-tuple-element.19.near_vol, ...), custom_call_target="tpu_custom_call" | custom-call | tf_op jit(solution)/shard_map/local_convolutions/pallas_call | solution.py:341
  30.3 0.8 %copy_bitcast_fusion = (bf16[8,8,2,256]{3,2,1,0:T(2,128)(2,1)}, bf16[8,8,2,256]{3,2,1,0:T(2,128)(2,1)}) fusion(bf16[8,8,2,256]{3,1,2,0:T(8,128)(2,1)S(1)} %bitcast.11, bf16[8,8,2,256]{3,1,2,0:T(8,128)(2,1)S(1)} %bitcast.10), kind=kLoop, calls=%fused_computation.2 | loop fusion | bytes 262144 | tf_op jit(solution)/shard_map/transpose | solution.py:359
  31.1 0.8 %collective-permute-done.10 = bf16[432,128]{1,0:T(8,128)(2,1)S(1)} collective-permute-done((bf16[432,128]{1,0:T(8,128)(2,1)S(1)}, bf16[432,128]{1,0:T(8,128)(2,1)S(1)}, u32[]{:S(2)}, u32[]{:S(2)}) %collective-permute-start.10) | collective-permute-done | bytes 110624 | tf_op jit(solution)/shard_map/ppermute | solution.py:337
  31.9 1.7 %collective-permute-done.12 = bf16[432,128]{1,0:T(8,128)(2,1)S(1)} collective-permute-done((bf16[432,128]{1,0:T(8,128)(2,1)S(1)}, bf16[432,128]{1,0:T(8,128)(2,1)S(1)}, u32[]{:S(2)}, u32[]{:S(2)}) %collective-permute-start.12) | collective-permute-done | bytes 110624 | tf_op jit(solution)/shard_map/ppermute | solution.py:337
  33.6 0.7 %add_bitcast_fusion = f32[55296]{0:T(1024)} fusion(bf16[432,128]{1,0:T(8,128)(2,1)S(1)} %collective-permute-done.12, bf16[432,128]{1,0:T(8,128)(2,1)S(1)} %collective-permute-done.11, f32[432,128]{1,0:T(8,128)S(1)} %get-tuple-element.23, bf16[432,128]{1,0:T(8,128)(2,1)S(1)} %collective-permute-done.10), kind=kLoop, calls=%fused_computation | loop fusion | flops 331776 | bytes 774144 | tf_op jit(solution)/shard_map/reshape | solution.py:364
  (8 shorter events, 0.0 us)
Async XLA Ops:
  1.8 12.7 %copy-start = (bf16[6912,256]{1,0:T(8,128)(2,1)S(1)}, bf16[6912,256]{1,0:T(8,128)(2,1)}, u32[]{:S(2)}) copy-start(bf16[6912,256]{1,0:T(8,128)(2,1)} %w1.1) | copy-start | bytes 10616836
  1.8 8.3 %collective-permute-start.2 = (bf16[128,512]{1,0:T(8,128)(2,1)S(1)}, bf16[128,512]{1,0:T(8,128)(2,1)S(1)}, u32[]{:S(2)}, u32[]{:S(2)}) collective-permute-start(bf16[128,512]{1,0:T(8,128)(2,1)S(1)} %lines.1.refs_0_), channel_id=1, source_target_pairs={{0,17},{1,16},{2,19},{3,18},{4,21},{5,20},{6,23},{7,22},{8,25},{9,... | collective-permute-start | bytes 393224 | tf_op jit(solution)/shard_map/ppermute | solution.py:273
  5.8 6.6 %collective-permute-start.1 = (bf16[128,512]{1,0:T(8,128)(2,1)S(1)}, bf16[128,512]{1,0:T(8,128)(2,1)S(1)}, u32[]{:S(2)}, u32[]{:S(2)}) collective-permute-start(bf16[128,512]{1,0:T(8,128)(2,1)S(1)} %lines.1.refs_0_), channel_id=1, source_target_pairs={{0,16},{1,17},{2,18},{3,19},{4,20},{5,21},{6,22},{7,23},{8,24},{9,... | collective-permute-start | bytes 393224 | tf_op jit(solution)/shard_map/ppermute | solution.py:273
  6.3 6.0 %collective-permute-start = (bf16[128,512]{1,0:T(8,128)(2,1)S(1)}, bf16[128,512]{1,0:T(8,128)(2,1)S(1)}, u32[]{:S(2)}, u32[]{:S(2)}) collective-permute-start(bf16[128,512]{1,0:T(8,128)(2,1)S(1)} %lines.1.refs_0_), channel_id=1, source_target_pairs={{0,1},{1,0},{2,3},{3,2},{4,5},{5,4},{6,7},{7,6},{8,9},{9,8},{10,11... | collective-permute-start | bytes 393224 | tf_op jit(solution)/shard_map/ppermute | solution.py:273
  6.4 8.1 %collective-permute-start.3 = (bf16[128,512]{1,0:T(8,128)(2,1)S(1)}, bf16[128,512]{1,0:T(8,128)(2,1)S(1)}, u32[]{:S(2)}, u32[]{:S(2)}) collective-permute-start(bf16[128,512]{1,0:T(8,128)(2,1)S(1)} %lines.1.refs_0_), channel_id=1, source_target_pairs={{0,8},{1,9},{2,10},{3,11},{4,12},{5,13},{6,14},{7,15},{8,0},{9,1},... | collective-permute-start | bytes 393224 | tf_op jit(solution)/shard_map/ppermute | solution.py:257
  10.1 4.4 %collective-permute-start.6 = (bf16[128,512]{1,0:T(8,128)(2,1)S(1)}, bf16[128,512]{1,0:T(8,128)(2,1)S(1)}, u32[]{:S(2)}, u32[]{:S(2)}) collective-permute-start(bf16[128,512]{1,0:T(8,128)(2,1)S(1)} %collective-permute-done.2.refs_3_), channel_id=1, source_target_pairs={{0,8},{1,9},{2,10},{3,11},{4,12},{5,13},{6,14},{7,15},{8,0},{9,1},... | collective-permute-start | bytes 393224 | tf_op jit(solution)/shard_map/ppermute | solution.py:257
  12.3 2.2 %collective-permute-start.5 = (bf16[128,512]{1,0:T(8,128)(2,1)S(1)}, bf16[128,512]{1,0:T(8,128)(2,1)S(1)}, u32[]{:S(2)}, u32[]{:S(2)}) collective-permute-start(bf16[128,512]{1,0:T(8,128)(2,1)S(1)} %collective-permute-done.1.refs_2_), channel_id=1, source_target_pairs={{0,8},{1,9},{2,10},{3,11},{4,12},{5,13},{6,14},{7,15},{8,0},{9,1},... | collective-permute-start | bytes 393224 | tf_op jit(solution)/shard_map/ppermute | solution.py:257
  12.4 2.2 %collective-permute-start.4 = (bf16[128,512]{1,0:T(8,128)(2,1)S(1)}, bf16[128,512]{1,0:T(8,128)(2,1)S(1)}, u32[]{:S(2)}, u32[]{:S(2)}) collective-permute-start(bf16[128,512]{1,0:T(8,128)(2,1)S(1)} %collective-permute-done.refs_1_), channel_id=1, source_target_pairs={{0,8},{1,9},{2,10},{3,11},{4,12},{5,13},{6,14},{7,15},{8,0},{9,1},... | collective-permute-start | bytes 393224 | tf_op jit(solution)/shard_map/ppermute | solution.py:257
  12.9 6.1 %collective-permute-start.7 = (bf16[64,512]{1,0:T(8,128)(2,1)S(1)}, bf16[64,512]{1,0:T(8,128)(2,1)S(1)}, u32[]{:S(2)}, u32[]{:S(2)}) collective-permute-start(bf16[64,512]{1,0:T(8,128)(2,1)S(1)} %edges.1), channel_id=1, source_target_pairs={{0,2},{1,3},{2,4},{3,5},{4,6},{5,7},{6,0},{7,1},{8,10},{9,11},{10,... | collective-permute-start | bytes 196616 | tf_op jit(solution)/shard_map/ppermute | solution.py:284
  19.0 6.6 %copy-start.1 = (bf16[6912,256]{1,0:T(8,128)(2,1)S(1)}, bf16[6912,256]{1,0:T(8,128)(2,1)}, u32[]{:S(2)}) copy-start(bf16[6912,256]{1,0:T(8,128)(2,1)} %w2.1) | copy-start | bytes 10616836
  19.0 2.2 %collective-permute-start.8 = (bf16[64,512]{1,0:T(8,128)(2,1)S(1)}, bf16[64,512]{1,0:T(8,128)(2,1)S(1)}, u32[]{:S(2)}, u32[]{:S(2)}) collective-permute-start(bf16[64,512]{1,0:T(8,128)(2,1)S(1)} %later.1.refs_0_), channel_id=1, source_target_pairs={{0,8},{1,9},{2,10},{3,11},{4,12},{5,13},{6,14},{7,15},{8,0},{9,1},... | collective-permute-start | bytes 196616 | tf_op jit(solution)/shard_map/ppermute | solution.py:257
  19.2 6.4 %collective-permute-start.9 = (bf16[64,512]{1,0:T(8,128)(2,1)S(1)}, bf16[64,512]{1,0:T(8,128)(2,1)S(1)}, u32[]{:S(2)}, u32[]{:S(2)}) collective-permute-start(bf16[64,512]{1,0:T(8,128)(2,1)S(1)} %first_lines.1), channel_id=1, source_target_pairs={{0,6},{1,7},{2,0},{3,1},{4,2},{5,3},{6,4},{7,5},{8,14},{9,15},{10,... | collective-permute-start | bytes 196616 | tf_op jit(solution)/shard_map/ppermute | solution.py:295
  23.1 8.8 %collective-permute-start.10 = (bf16[432,128]{1,0:T(8,128)(2,1)S(1)}, bf16[432,128]{1,0:T(8,128)(2,1)S(1)}, u32[]{:S(2)}, u32[]{:S(2)}) collective-permute-start(bf16[432,128]{1,0:T(8,128)(2,1)S(1)} %get-tuple-element.24), channel_id=1, source_target_pairs={{0,4},{1,5},{2,6},{3,7},{4,0},{5,1},{6,2},{7,3},{8,12},{9,13},{10,... | collective-permute-start | bytes 331784 | tf_op jit(solution)/shard_map/ppermute | solution.py:337
  23.6 8.3 %collective-permute-start.11 = (bf16[432,128]{1,0:T(8,128)(2,1)S(1)}, bf16[432,128]{1,0:T(8,128)(2,1)S(1)}, u32[]{:S(2)}, u32[]{:S(2)}) collective-permute-start(bf16[432,128]{1,0:T(8,128)(2,1)S(1)} %get-tuple-element.25), channel_id=1, source_target_pairs={{0,6},{1,7},{2,0},{3,1},{4,2},{5,3},{6,4},{7,5},{8,14},{9,15},{10,... | collective-permute-start | bytes 331784 | tf_op jit(solution)/shard_map/ppermute | solution.py:337
  25.6 8.0 %collective-permute-start.12 = (bf16[432,128]{1,0:T(8,128)(2,1)S(1)}, bf16[432,128]{1,0:T(8,128)(2,1)S(1)}, u32[]{:S(2)}, u32[]{:S(2)}) collective-permute-start(bf16[432,128]{1,0:T(8,128)(2,1)S(1)} %get-tuple-element.26), channel_id=1, source_target_pairs={{0,2},{1,3},{2,4},{3,5},{4,6},{5,7},{6,0},{7,1},{8,10},{9,11},{10,... | collective-permute-start | bytes 331784 | tf_op jit(solution)/shard_map/ppermute | solution.py:337

commit v7 on v6

--- a/solution.py
+++ b/solution.py
@@ -105,7 +105,7 @@
         out[k * sy * sx : (k + 1) * sy * sx, :] = rows[...].reshape(sy * sx, 2 * CH).astype(BF16)
 
 
-def later_kernel(lines, _, out):
+def later_kernel(lines, _, __, out):
     out[...] = lines[...]
 
 
@@ -129,7 +129,7 @@
 
 
 def gradient_kernel(n_x, n_z, groups, strip, block, scale, *refs):
-    beyond_a, beyond_b, w_ref, outer, cot, hid_ref, near_vol, near_cot, own_out, *sends, hid, ends, grad, flat = refs
+    beyond_a, beyond_b, w_ref, outer, cot, hid_ref, near_vol, near_cot, own_out, *sends, ends, grad, flat = refs
     gx, core, z, side = place()
     full = 16 * n_x
     put = putter(near_vol, near_cot)
@@ -145,14 +145,13 @@
         term = dot(left[full:], both(w[768:]))
         first_line = term if a == 0 else first_line + term
     pre = jnp.concatenate([pre[:full] + first_line, pre[full:]], axis=0)
-    hid[...] = hid_ref[...]
-    hid[:, 14 * full :] = silu_t(pre)
+    hid = jnp.concatenate([hid_ref[:, : 14 * full], silu_t(pre)], axis=1)
     first = lax.div(gx * strip, 3 * CH)
     for k in range(groups):
         ab = jnp.minimum(first + k, 8)
         shift, row = lax.div(ab, 3), 2 - lax.rem(ab, 3)
         right = jnp.concatenate([cot[shift, pl.ds(row + 2, 14)], ends[shift, pl.ds(row, 2)]], axis=0).reshape(16 * full, 512)
-        product = dot(hid[...], right) * scale
+        product = dot(hid, right) * scale
         at = k * 3 * CH
         grad[at : at + CH, :] = product[:CH, CH:]
         grad[at + CH : at + 2 * CH, :] = product[:CH, :CH] + product[CH:, CH:]
@@ -309,12 +308,12 @@
     beyond = pl.pallas_call(
         later_kernel,
         out_shape=jax.ShapeDtypeStruct(beyond.shape, BF16),
-        in_specs=[vmem] * 2,
+        in_specs=[vmem] * 3,
         out_specs=vmem,
         compiler_params=params(4),
         cost_estimate=cost(0),
         name="later",
-    )(beyond, outer)
+    )(beyond, outer, first)
     near = jax.ShapeDtypeStruct((3, 2, full, 512), BF16)
     near_vol, near_cot, mine, *sends = pl.pallas_call(
         functools.partial(gradient_kernel, n_x, n_z, groups, strip, block, scale),
@@ -323,7 +322,6 @@
         in_specs=[vmem] * 6,
         out_specs=[vmem] * (2 + n_z),
         scratch_shapes=[
-            pltpu.VMEM((512, 16 * full), BF16),
             pltpu.VMEM((3, 4, full, 512), BF16),
             pltpu.VMEM((groups * 3 * CH + (0 if block % 8 == 0 else 16), CH), F32),
             pltpu.VMEM((2 * block, 128), F32),

time: 34.5 us -> 34.3 us (level)
  starting transfers between devices: 11.3 us -> 10.9 us
    ppermute x5, starting transfers between devices: 0.59 us -> 0.01 us  [across(): return lax.ppermute(v, AX, perm(lambda x, c, z, y: (x, 1 - c, z, y)))]
  transfers between devices with their start and end apart: 13 -> 13, of which waited for: 5 -> 6; matrix products, arithmetic and copies ran while one was open for 2% -> 2% of each run, Pallas kernels for 29% -> 29%
where the time goes in v7:
time: 34.3 us; the launch traced here: 34.2 us
  starting transfers between devices  10.9 us (32%)
  waiting for transfers between devices  9.98 us (29%)
  Pallas kernels  9.97 us (29%)
  other arithmetic  1.8 us (5%)
  local copies, waits for them, and re-layouts  0.77 us (2%)
  between operations  0.74 us (2%)
    ppermute x3, waiting for transfers between devices, body(): lax.ppermute(own, AX, perm(lambda x, c, z, y, dx=dx, dy=dy: (x - dx, c, z...  6.01 us
    pallas_call x1, Pallas kernels, body(): pl.pallas_call(local_kernel, out_shape=[jax.ShapeDtypeStruct((sy, sx, 512...  4.7 us
    ppermute x3, starting transfers between devices, body(): lax.ppermute(own, AX, perm(lambda x, c, z, y, dx=dx, dy=dy: (x - dx, c, z...  4.57 us
    pallas_call x1, Pallas kernels, body(): pl.pallas_call(functools.partial(inner_kernel, n_x), out_shape=[jax.Shape...  3.14 us
    ppermute x3, starting transfers between devices, body(): lax.ppermute(sends[k - 1], AX, perm(lambda x, c, z, y, k=k: (x, c, z + k,...  2.51 us
    ppermute x3, waiting for transfers between devices, body(): lax.ppermute(sends[k - 1], AX, perm(lambda x, c, z, y, k=k: (x, c, z + k,...  2.47 us
    ppermute x1, starting transfers between devices, body(): after = lax.ppermute(first, AX, perm(lambda x, c, z, y: (x, c, z - 1, y)))  2.01 us
    pallas_call x1, Pallas kernels, body(): pl.pallas_call(functools.partial(gradient_kernel, n_x, n_z, groups, strip...  1.9 us
  transfers between devices with their start and end apart: 13, of which 6 were waited for; matrix products, arithmetic and copies ran while one was open for 2% of the time, Pallas kernels for 29%

profile of v7, /device:TPU:0, one launch (start us, length us, event | category | flops | bytes accessed | tf_op | source)
XLA Modules:
  0.0 34.2 jit_solution(16144348833940925326)
XLA Ops:
  0.6 1.1 %pad_maximum_fusion.fields = bf16[2,8,8,2,256]{4,3,2,1,0:T(2,128)(2,1)S(1)} fusion(bf16[1,8,8,2,256]{4,3,2,1,0:T(2,128)(2,1)} %bitcast.12, bf16[1,8,8,2,256]{4,3,2,1,0:T(2,128)(2,1)} %bitcast.13), kind=kLoop, calls=%fused_computation.1 | loop fusion | flops 65536 | bytes 262144 | tf_op jit(solution)/shard_map/stack | solution.py:267
  1.7 0.1 lines.1.refs_0_
  1.8 0.0 copy-start
  1.8 3.0 %collective-permute-start = (bf16[128,512]{1,0:T(8,128)(2,1)S(1)}, bf16[128,512]{1,0:T(8,128)(2,1)S(1)}, u32[]{:S(2)}, u32[]{:S(2)}) collective-permute-start(bf16[128,512]{1,0:T(8,128)(2,1)S(1)} %lines.1.refs_0_), channel_id=1, source_target_pairs={{0,1},{1,0},{2,3},{3,2},{4,5},{5,4},{6,7},{7,6},{8,9},{9,8},{10,11... | collective-permute-start | bytes 393224 | tf_op jit(solution)/shard_map/ppermute | solution.py:272
  4.9 1.5 %collective-permute-start.1 = (bf16[128,512]{1,0:T(8,128)(2,1)S(1)}, bf16[128,512]{1,0:T(8,128)(2,1)S(1)}, u32[]{:S(2)}, u32[]{:S(2)}) collective-permute-start(bf16[128,512]{1,0:T(8,128)(2,1)S(1)} %lines.1.refs_0_), channel_id=1, source_target_pairs={{0,16},{1,17},{2,18},{3,19},{4,20},{5,21},{6,22},{7,23},{8,24},{9,... | collective-permute-start | bytes 393224 | tf_op jit(solution)/shard_map/ppermute | solution.py:272
  6.4 0.0 collective-permute-start.2
  6.4 0.0 collective-permute-start.3
  6.4 2.0 %collective-permute-done.refs_1_ = bf16[128,512]{1,0:T(8,128)(2,1)S(1)} collective-permute-done((bf16[128,512]{1,0:T(8,128)(2,1)S(1)}, bf16[128,512]{1,0:T(8,128)(2,1)S(1)}, u32[]{:S(2)}, u32[]{:S(2)}) %collective-permute-start) | collective-permute-done | bytes 131104 | tf_op jit(solution)/shard_map/ppermute | solution.py:272
  8.4 0.0 collective-permute-start.4
  8.4 2.9 %collective-permute-done.1.refs_2_ = bf16[128,512]{1,0:T(8,128)(2,1)S(1)} collective-permute-done((bf16[128,512]{1,0:T(8,128)(2,1)S(1)}, bf16[128,512]{1,0:T(8,128)(2,1)S(1)}, u32[]{:S(2)}, u32[]{:S(2)}) %collective-permute-start.1) | collective-permute-done | bytes 131104 | tf_op jit(solution)/shard_map/ppermute | solution.py:272
  11.2 1.2 %collective-permute-done.2.refs_3_ = bf16[128,512]{1,0:T(8,128)(2,1)S(1)} collective-permute-done((bf16[128,512]{1,0:T(8,128)(2,1)S(1)}, bf16[128,512]{1,0:T(8,128)(2,1)S(1)}, u32[]{:S(2)}, u32[]{:S(2)}) %collective-permute-start.2) | collective-permute-done | bytes 131104 | tf_op jit(solution)/shard_map/ppermute | solution.py:272
  12.4 0.0 collective-permute-start.6
  12.5 1.8 %collective-permute-start.7 = (bf16[64,512]{1,0:T(8,128)(2,1)S(1)}, bf16[64,512]{1,0:T(8,128)(2,1)S(1)}, u32[]{:S(2)}, u32[]{:S(2)}) collective-permute-start(bf16[64,512]{1,0:T(8,128)(2,1)S(1)} %edges.1), channel_id=1, source_target_pairs={{0,2},{1,3},{2,4},{3,5},{4,6},{5,7},{6,0},{7,1},{8,10},{9,11},{10,... | collective-permute-start | bytes 196616 | tf_op jit(solution)/shard_map/ppermute | solution.py:283
  14.3 0.0 collective-permute-done.6.refs_7_
  14.3 3.1 %plane_inner.1 = (f32[64,512]{1,0:T(8,128)S(1)}, bf16[512,512]{1,0:T(8,128)(2,1)S(1)}, bf16[3,18,32,512]{3,2,1,0:T(8,128)(2,1)S(1)}, bf16[3,18,32,512]{3,2,1,0:T(8,128)(2,1)S(1)}) custom-call(bf16[128,512]{1,0:T(8,128)(2,1)S(1)} %lines.1.refs_0_, bf16[128,512]{1,0:T(8,128)(2,1)S(1)} %collective-permute-done.refs_1_, ...), custom_call_target="tpu_custom_call" | custom-call | flops 5000000000 | bytes 15000000 | tf_op jit(solution)/shard_map/plane_inner/pallas_call | solution.py:298
  17.4 0.0 copy-start.1
  17.4 0.1 first_lines.1.__
  17.5 1.5 %collective-permute-done.7.lines = bf16[64,512]{1,0:T(8,128)(2,1)S(1)} collective-permute-done((bf16[64,512]{1,0:T(8,128)(2,1)S(1)}, bf16[64,512]{1,0:T(8,128)(2,1)S(1)}, u32[]{:S(2)}, u32[]{:S(2)}) %collective-permute-start.7) | collective-permute-done | bytes 65568 | tf_op jit(solution)/shard_map/ppermute | solution.py:283
  19.0 0.0 collective-permute-start.8
  19.0 2.0 %collective-permute-start.9 = (bf16[64,512]{1,0:T(8,128)(2,1)S(1)}, bf16[64,512]{1,0:T(8,128)(2,1)S(1)}, u32[]{:S(2)}, u32[]{:S(2)}) collective-permute-start(bf16[64,512]{1,0:T(8,128)(2,1)S(1)} %first_lines.1.__), channel_id=1, source_target_pairs={{0,6},{1,7},{2,0},{3,1},{4,2},{5,3},{6,4},{7,5},{8,14},{9,15},{10,... | collective-permute-start | bytes 196616 | tf_op jit(solution)/shard_map/ppermute | solution.py:294
  21.0 0.0 collective-permute-done.8.refs_1_
  21.1 1.9 %plane_gradient.1 = (bf16[3,2,32,512]{3,2,1,0:T(8,128)(2,1)S(1)}, bf16[3,2,32,512]{3,2,1,0:T(8,128)(2,1)S(1)}, f32[432,128]{1,0:T(8,128)S(1)}, bf16[432,128]{1,0...) custom-call(bf16[64,512]{1,0:T(8,128)(2,1)S(1)} %later.1.refs_0_, ...), custom_call_target="tpu_custom_call" | custom-call | tf_op jit(solution)/shard_map/plane_gradient/pallas_call | solution.py:318
  23.0 0.5 %collective-permute-start.10 = (bf16[432,128]{1,0:T(8,128)(2,1)S(1)}, bf16[432,128]{1,0:T(8,128)(2,1)S(1)}, u32[]{:S(2)}, u32[]{:S(2)}) collective-permute-start(bf16[432,128]{1,0:T(8,128)(2,1)S(1)} %get-tuple-element.24), channel_id=1, source_target_pairs={{0,4},{1,5},{2,6},{3,7},{4,0},{5,1},{6,2},{7,3},{8,12},{9,13},{10,... | collective-permute-start | bytes 331784 | tf_op jit(solution)/shard_map/ppermute | solution.py:335
  23.4 2.0 %collective-permute-start.11 = (bf16[432,128]{1,0:T(8,128)(2,1)S(1)}, bf16[432,128]{1,0:T(8,128)(2,1)S(1)}, u32[]{:S(2)}, u32[]{:S(2)}) collective-permute-start(bf16[432,128]{1,0:T(8,128)(2,1)S(1)} %get-tuple-element.25), channel_id=1, source_target_pairs={{0,6},{1,7},{2,0},{3,1},{4,2},{5,3},{6,4},{7,5},{8,14},{9,15},{10,... | collective-permute-start | bytes 331784 | tf_op jit(solution)/shard_map/ppermute | solution.py:335
  25.5 0.0 collective-permute-start.12
  25.5 0.0 collective-permute-done.9.after_ref
  25.5 4.7 %local_convolutions.1 = (bf16[8,8,512]{2,1,0:T(8,128)(2,1)S(1)}, bf16[8,8,512]{2,1,0:T(8,128)(2,1)S(1)}) custom-call(bf16[3,18,32,512]{3,2,1,0:T(8,128)(2,1)S(1)} %get-tuple-element.15.vol_ref, bf16[3,18,32,512]{3,2,1,0:T(8,128)(2,1)S(1)} %get-tuple-element.16.refs_4_.cot_ref, bf16[3,2,32,512]{3,2,1,0:T(8,128)(2,1)S(1)} %get-tuple-element.19.near_vol, ...), custom_call_target="tpu_custom_call" | custom-call | tf_op jit(solution)/shard_map/local_convolutions/pallas_call | solution.py:339
  30.2 0.8 %copy_bitcast_fusion = (bf16[8,8,2,256]{3,2,1,0:T(2,128)(2,1)}, bf16[8,8,2,256]{3,2,1,0:T(2,128)(2,1)}) fusion(bf16[8,8,2,256]{3,1,2,0:T(8,128)(2,1)S(1)} %bitcast.11, bf16[8,8,2,256]{3,1,2,0:T(8,128)(2,1)S(1)} %bitcast.10), kind=kLoop, calls=%fused_computation.2 | loop fusion | bytes 262144 | tf_op jit(solution)/shard_map/transpose | solution.py:357
  30.9 0.8 %collective-permute-done.10 = bf16[432,128]{1,0:T(8,128)(2,1)S(1)} collective-permute-done((bf16[432,128]{1,0:T(8,128)(2,1)S(1)}, bf16[432,128]{1,0:T(8,128)(2,1)S(1)}, u32[]{:S(2)}, u32[]{:S(2)}) %collective-permute-start.10) | collective-permute-done | bytes 110624 | tf_op jit(solution)/shard_map/ppermute | solution.py:335
  31.8 0.0 collective-permute-done.11
  31.8 1.6 %collective-permute-done.12 = bf16[432,128]{1,0:T(8,128)(2,1)S(1)} collective-permute-done((bf16[432,128]{1,0:T(8,128)(2,1)S(1)}, bf16[432,128]{1,0:T(8,128)(2,1)S(1)}, u32[]{:S(2)}, u32[]{:S(2)}) %collective-permute-start.12) | collective-permute-done | bytes 110624 | tf_op jit(solution)/shard_map/ppermute | solution.py:335
  33.4 0.7 %add_bitcast_fusion = f32[55296]{0:T(1024)} fusion(bf16[432,128]{1,0:T(8,128)(2,1)S(1)} %collective-permute-done.12, bf16[432,128]{1,0:T(8,128)(2,1)S(1)} %collective-permute-done.11, f32[432,128]{1,0:T(8,128)S(1)} %get-tuple-element.23, bf16[432,128]{1,0:T(8,128)(2,1)S(1)} %collective-permute-done.10), kind=kLoop, calls=%fused_computation | loop fusion | flops 331776 | bytes 774144 | tf_op jit(solution)/shard_map/reshape | solution.py:362
  (8 shorter events, 0.0 us)
Async XLA Ops:
  1.8 12.4 %copy-start = (bf16[6912,256]{1,0:T(8,128)(2,1)S(1)}, bf16[6912,256]{1,0:T(8,128)(2,1)}, u32[]{:S(2)}) copy-start(bf16[6912,256]{1,0:T(8,128)(2,1)} %w1.1) | copy-start | bytes 10616836
  1.8 6.5 %collective-permute-start = (bf16[128,512]{1,0:T(8,128)(2,1)S(1)}, bf16[128,512]{1,0:T(8,128)(2,1)S(1)}, u32[]{:S(2)}, u32[]{:S(2)}) collective-permute-start(bf16[128,512]{1,0:T(8,128)(2,1)S(1)} %lines.1.refs_0_), channel_id=1, source_target_pairs={{0,1},{1,0},{2,3},{3,2},{4,5},{5,4},{6,7},{7,6},{8,9},{9,8},{10,11... | collective-permute-start | bytes 393224 | tf_op jit(solution)/shard_map/ppermute | solution.py:272
  4.9 6.4 %collective-permute-start.1 = (bf16[128,512]{1,0:T(8,128)(2,1)S(1)}, bf16[128,512]{1,0:T(8,128)(2,1)S(1)}, u32[]{:S(2)}, u32[]{:S(2)}) collective-permute-start(bf16[128,512]{1,0:T(8,128)(2,1)S(1)} %lines.1.refs_0_), channel_id=1, source_target_pairs={{0,16},{1,17},{2,18},{3,19},{4,20},{5,21},{6,22},{7,23},{8,24},{9,... | collective-permute-start | bytes 393224 | tf_op jit(solution)/shard_map/ppermute | solution.py:272
  6.4 6.1 %collective-permute-start.2 = (bf16[128,512]{1,0:T(8,128)(2,1)S(1)}, bf16[128,512]{1,0:T(8,128)(2,1)S(1)}, u32[]{:S(2)}, u32[]{:S(2)}) collective-permute-start(bf16[128,512]{1,0:T(8,128)(2,1)S(1)} %lines.1.refs_0_), channel_id=1, source_target_pairs={{0,17},{1,16},{2,19},{3,18},{4,21},{5,20},{6,23},{7,22},{8,25},{9,... | collective-permute-start | bytes 393224 | tf_op jit(solution)/shard_map/ppermute | solution.py:272
  6.4 7.8 %collective-permute-start.3 = (bf16[128,512]{1,0:T(8,128)(2,1)S(1)}, bf16[128,512]{1,0:T(8,128)(2,1)S(1)}, u32[]{:S(2)}, u32[]{:S(2)}) collective-permute-start(bf16[128,512]{1,0:T(8,128)(2,1)S(1)} %lines.1.refs_0_), channel_id=1, source_target_pairs={{0,8},{1,9},{2,10},{3,11},{4,12},{5,13},{6,14},{7,15},{8,0},{9,1},... | collective-permute-start | bytes 393224 | tf_op jit(solution)/shard_map/ppermute | solution.py:256
  8.4 5.9 %collective-permute-start.4 = (bf16[128,512]{1,0:T(8,128)(2,1)S(1)}, bf16[128,512]{1,0:T(8,128)(2,1)S(1)}, u32[]{:S(2)}, u32[]{:S(2)}) collective-permute-start(bf16[128,512]{1,0:T(8,128)(2,1)S(1)} %collective-permute-done.refs_1_), channel_id=1, source_target_pairs={{0,8},{1,9},{2,10},{3,11},{4,12},{5,13},{6,14},{7,15},{8,0},{9,1},... | collective-permute-start | bytes 393224 | tf_op jit(solution)/shard_map/ppermute | solution.py:256
  11.2 3.0 %collective-permute-start.5 = (bf16[128,512]{1,0:T(8,128)(2,1)S(1)}, bf16[128,512]{1,0:T(8,128)(2,1)S(1)}, u32[]{:S(2)}, u32[]{:S(2)}) collective-permute-start(bf16[128,512]{1,0:T(8,128)(2,1)S(1)} %collective-permute-done.1.refs_2_), channel_id=1, source_target_pairs={{0,8},{1,9},{2,10},{3,11},{4,12},{5,13},{6,14},{7,15},{8,0},{9,1},... | collective-permute-start | bytes 393224 | tf_op jit(solution)/shard_map/ppermute | solution.py:256
  12.4 1.8 %collective-permute-start.6 = (bf16[128,512]{1,0:T(8,128)(2,1)S(1)}, bf16[128,512]{1,0:T(8,128)(2,1)S(1)}, u32[]{:S(2)}, u32[]{:S(2)}) collective-permute-start(bf16[128,512]{1,0:T(8,128)(2,1)S(1)} %collective-permute-done.2.refs_3_), channel_id=1, source_target_pairs={{0,8},{1,9},{2,10},{3,11},{4,12},{5,13},{6,14},{7,15},{8,0},{9,1},... | collective-permute-start | bytes 393224 | tf_op jit(solution)/shard_map/ppermute | solution.py:256
  12.5 6.6 %collective-permute-start.7 = (bf16[64,512]{1,0:T(8,128)(2,1)S(1)}, bf16[64,512]{1,0:T(8,128)(2,1)S(1)}, u32[]{:S(2)}, u32[]{:S(2)}) collective-permute-start(bf16[64,512]{1,0:T(8,128)(2,1)S(1)} %edges.1), channel_id=1, source_target_pairs={{0,2},{1,3},{2,4},{3,5},{4,6},{5,7},{6,0},{7,1},{8,10},{9,11},{10,... | collective-permute-start | bytes 196616 | tf_op jit(solution)/shard_map/ppermute | solution.py:283
  17.4 8.1 %copy-start.1 = (bf16[6912,256]{1,0:T(8,128)(2,1)S(1)}, bf16[6912,256]{1,0:T(8,128)(2,1)}, u32[]{:S(2)}) copy-start(bf16[6912,256]{1,0:T(8,128)(2,1)} %w2.1) | copy-start | bytes 10616836
  19.0 2.0 %collective-permute-start.8 = (bf16[64,512]{1,0:T(8,128)(2,1)S(1)}, bf16[64,512]{1,0:T(8,128)(2,1)S(1)}, u32[]{:S(2)}, u32[]{:S(2)}) collective-permute-start(bf16[64,512]{1,0:T(8,128)(2,1)S(1)} %later.1.refs_0_), channel_id=1, source_target_pairs={{0,8},{1,9},{2,10},{3,11},{4,12},{5,13},{6,14},{7,15},{8,0},{9,1},... | collective-permute-start | bytes 196616 | tf_op jit(solution)/shard_map/ppermute | solution.py:256
  19.0 6.4 %collective-permute-start.9 = (bf16[64,512]{1,0:T(8,128)(2,1)S(1)}, bf16[64,512]{1,0:T(8,128)(2,1)S(1)}, u32[]{:S(2)}, u32[]{:S(2)}) collective-permute-start(bf16[64,512]{1,0:T(8,128)(2,1)S(1)} %first_lines.1.__), channel_id=1, source_target_pairs={{0,6},{1,7},{2,0},{3,1},{4,2},{5,3},{6,4},{7,5},{8,14},{9,15},{10,... | collective-permute-start | bytes 196616 | tf_op jit(solution)/shard_map/ppermute | solution.py:294
  23.0 8.8 %collective-permute-start.10 = (bf16[432,128]{1,0:T(8,128)(2,1)S(1)}, bf16[432,128]{1,0:T(8,128)(2,1)S(1)}, u32[]{:S(2)}, u32[]{:S(2)}) collective-permute-start(bf16[432,128]{1,0:T(8,128)(2,1)S(1)} %get-tuple-element.24), channel_id=1, source_target_pairs={{0,4},{1,5},{2,6},{3,7},{4,0},{5,1},{6,2},{7,3},{8,12},{9,13},{10,... | collective-permute-start | bytes 331784 | tf_op jit(solution)/shard_map/ppermute | solution.py:335
  23.4 8.3 %collective-permute-start.11 = (bf16[432,128]{1,0:T(8,128)(2,1)S(1)}, bf16[432,128]{1,0:T(8,128)(2,1)S(1)}, u32[]{:S(2)}, u32[]{:S(2)}) collective-permute-start(bf16[432,128]{1,0:T(8,128)(2,1)S(1)} %get-tuple-element.25), channel_id=1, source_target_pairs={{0,6},{1,7},{2,0},{3,1},{4,2},{5,3},{6,4},{7,5},{8,14},{9,15},{10,... | collective-permute-start | bytes 331784 | tf_op jit(solution)/shard_map/ppermute | solution.py:335
  25.5 8.0 %collective-permute-start.12 = (bf16[432,128]{1,0:T(8,128)(2,1)S(1)}, bf16[432,128]{1,0:T(8,128)(2,1)S(1)}, u32[]{:S(2)}, u32[]{:S(2)}) collective-permute-start(bf16[432,128]{1,0:T(8,128)(2,1)S(1)} %get-tuple-element.26), channel_id=1, source_target_pairs={{0,2},{1,3},{2,4},{3,5},{4,6},{5,7},{6,0},{7,1},{8,10},{9,11},{10,... | collective-permute-start | bytes 331784 | tf_op jit(solution)/shard_map/ppermute | solution.py:335

commit v8 on v7

--- a/solution.py
+++ b/solution.py
@@ -129,7 +129,7 @@
 
 
 def gradient_kernel(n_x, n_z, groups, strip, block, scale, *refs):
-    beyond_a, beyond_b, w_ref, outer, cot, hid_ref, near_vol, near_cot, own_out, *sends, ends, grad, flat = refs
+    beyond_a, beyond_b, w_ref, outer, cot, hid_ref, near_vol, near_cot, own_out, *sends, ends, grad = refs
     gx, core, z, side = place()
     full = 16 * n_x
     put = putter(near_vol, near_cot)
@@ -152,26 +152,25 @@
         shift, row = lax.div(ab, 3), 2 - lax.rem(ab, 3)
         right = jnp.concatenate([cot[shift, pl.ds(row + 2, 14)], ends[shift, pl.ds(row, 2)]], axis=0).reshape(16 * full, 512)
         product = dot(hid, right) * scale
-        at = k * 3 * CH
-        grad[at : at + CH, :] = product[:CH, CH:]
-        grad[at + CH : at + 2 * CH, :] = product[:CH, :CH] + product[CH:, CH:]
-        grad[at + 2 * CH : at + 3 * CH, :] = product[CH:, :CH]
-
+        terms = (product[:CH, CH:], product[:CH, :CH] + product[CH:, CH:], product[CH:, :CH])
+        for e, term in enumerate(terms):
+            for half in range(2):
+                grad[pl.ds((k * 3 + e) * 2 * CH + half, CH, stride=2), :] = term[:, half * 128 : half * 128 + 128]
+
+    size = 2 * block
     for k in range(n_z):
-        start = gx * strip + (2 * lax.rem(z + k, n_z) + side) * block - first * 3 * CH
-        if block % 8 == 0:
-            value = grad[pl.ds(pl.multiple_of(start, 8), block), :]
+        start = 2 * (gx * strip + (2 * lax.rem(z + k, n_z) + side) * block - first * 3 * CH)
+        if size % 8 == 0:
+            value = grad[pl.ds(pl.multiple_of(start, 8), size), :]
         else:
             over = lax.rem(start, 8)
-            rows = (block + 7 + 7) // 8 * 8
+            rows = (size + 7 + 7) // 8 * 8
             value = grad[pl.ds(pl.multiple_of(start - over, 8), rows), :]
-            value = pltpu.roll(value, lax.rem(rows - over, rows), 0)[:block]
-        for half in range(2):
-            flat[pl.ds(half, block, stride=2), :] = value[:, half * 128 : half * 128 + 128]
+            value = pltpu.roll(value, lax.rem(rows - over, rows), 0)[:size]
         if k == 0:
-            own_out[...] = flat[...]
+            own_out[...] = value
         else:
-            sends[k - 1][...] = flat[...].astype(BF16)
+            sends[k - 1][...] = value.astype(BF16)
 
 
 def first_kernel(n_x, *refs):
@@ -323,8 +322,7 @@
         out_specs=[vmem] * (2 + n_z),
         scratch_shapes=[
             pltpu.VMEM((3, 4, full, 512), BF16),
-            pltpu.VMEM((groups * 3 * CH + (0 if block % 8 == 0 else 16), CH), F32),
-            pltpu.VMEM((2 * block, 128), F32),
+            pltpu.VMEM((groups * 6 * CH + (0 if 2 * block % 8 == 0 else 16), 128), F32),
         ],
         compiler_params=params(24),
         cost_estimate=cost(0),

time: 34.3 us -> 34.3 us (level)
  no operation moved by 1% of the time
where the time goes in v8:
time: 34.3 us; the launch traced here: 34.1 us
  starting transfers between devices  10.9 us (32%)
  waiting for transfers between devices  9.99 us (29%)
  Pallas kernels  9.91 us (29%)
  other arithmetic  1.8 us (5%)
  local copies, waits for them, and re-layouts  0.77 us (2%)
  between operations  0.74 us (2%)
    ppermute x3, waiting for transfers between devices, body(): lax.ppermute(own, AX, perm(lambda x, c, z, y, dx=dx, dy=dy: (x - dx, c, z...  6.01 us
    pallas_call x1, Pallas kernels, body(): pl.pallas_call(local_kernel, out_shape=[jax.ShapeDtypeStruct((sy, sx, 512...  4.69 us
    ppermute x3, starting transfers between devices, body(): lax.ppermute(own, AX, perm(lambda x, c, z, y, dx=dx, dy=dy: (x - dx, c, z...  4.57 us
    pallas_call x1, Pallas kernels, body(): pl.pallas_call(functools.partial(inner_kernel, n_x), out_shape=[jax.Shape...  3.14 us
    ppermute x3, starting transfers between devices, body(): lax.ppermute(sends[k - 1], AX, perm(lambda x, c, z, y, k=k: (x, c, z + k,...  2.51 us
    ppermute x3, waiting for transfers between devices, body(): lax.ppermute(sends[k - 1], AX, perm(lambda x, c, z, y, k=k: (x, c, z + k,...  2.48 us
    ppermute x1, starting transfers between devices, body(): after = lax.ppermute(first, AX, perm(lambda x, c, z, y: (x, c, z - 1, y)))  2.01 us
    pallas_call x1, Pallas kernels, body(): pl.pallas_call(functools.partial(gradient_kernel, n_x, n_z, groups, strip...  1.84 us
  transfers between devices with their start and end apart: 13, of which 6 were waited for; matrix products, arithmetic and copies ran while one was open for 2% of the time, Pallas kernels for 29%

profile of v8, /device:TPU:0, one launch (start us, length us, event | category | flops | bytes accessed | tf_op | source)
XLA Modules:
  0.0 34.1 jit_solution(15810061873371993267)
XLA Ops:
  0.6 1.1 %pad_maximum_fusion.fields = bf16[2,8,8,2,256]{4,3,2,1,0:T(2,128)(2,1)S(1)} fusion(bf16[1,8,8,2,256]{4,3,2,1,0:T(2,128)(2,1)} %bitcast.12, bf16[1,8,8,2,256]{4,3,2,1,0:T(2,128)(2,1)} %bitcast.13), kind=kLoop, calls=%fused_computation.1 | loop fusion | flops 65536 | bytes 262144 | tf_op jit(solution)/shard_map/stack | solution.py:266
  1.7 0.1 lines.1.refs_0_
  1.8 0.0 copy-start
  1.8 3.0 %collective-permute-start = (bf16[128,512]{1,0:T(8,128)(2,1)S(1)}, bf16[128,512]{1,0:T(8,128)(2,1)S(1)}, u32[]{:S(2)}, u32[]{:S(2)}) collective-permute-start(bf16[128,512]{1,0:T(8,128)(2,1)S(1)} %lines.1.refs_0_), channel_id=1, source_target_pairs={{0,1},{1,0},{2,3},{3,2},{4,5},{5,4},{6,7},{7,6},{8,9},{9,8},{10,11... | collective-permute-start | bytes 393224 | tf_op jit(solution)/shard_map/ppermute | solution.py:271
  4.9 1.5 %collective-permute-start.1 = (bf16[128,512]{1,0:T(8,128)(2,1)S(1)}, bf16[128,512]{1,0:T(8,128)(2,1)S(1)}, u32[]{:S(2)}, u32[]{:S(2)}) collective-permute-start(bf16[128,512]{1,0:T(8,128)(2,1)S(1)} %lines.1.refs_0_), channel_id=1, source_target_pairs={{0,16},{1,17},{2,18},{3,19},{4,20},{5,21},{6,22},{7,23},{8,24},{9,... | collective-permute-start | bytes 393224 | tf_op jit(solution)/shard_map/ppermute | solution.py:271
  6.4 0.0 collective-permute-start.2
  6.4 0.0 collective-permute-start.3
  6.4 2.0 %collective-permute-done.refs_1_ = bf16[128,512]{1,0:T(8,128)(2,1)S(1)} collective-permute-done((bf16[128,512]{1,0:T(8,128)(2,1)S(1)}, bf16[128,512]{1,0:T(8,128)(2,1)S(1)}, u32[]{:S(2)}, u32[]{:S(2)}) %collective-permute-start) | collective-permute-done | bytes 131104 | tf_op jit(solution)/shard_map/ppermute | solution.py:271
  8.4 0.0 collective-permute-start.4
  8.4 2.9 %collective-permute-done.1.refs_2_ = bf16[128,512]{1,0:T(8,128)(2,1)S(1)} collective-permute-done((bf16[128,512]{1,0:T(8,128)(2,1)S(1)}, bf16[128,512]{1,0:T(8,128)(2,1)S(1)}, u32[]{:S(2)}, u32[]{:S(2)}) %collective-permute-start.1) | collective-permute-done | bytes 131104 | tf_op jit(solution)/shard_map/ppermute | solution.py:271
  11.2 1.2 %collective-permute-done.2.refs_3_ = bf16[128,512]{1,0:T(8,128)(2,1)S(1)} collective-permute-done((bf16[128,512]{1,0:T(8,128)(2,1)S(1)}, bf16[128,512]{1,0:T(8,128)(2,1)S(1)}, u32[]{:S(2)}, u32[]{:S(2)}) %collective-permute-start.2) | collective-permute-done | bytes 131104 | tf_op jit(solution)/shard_map/ppermute | solution.py:271
  12.4 0.0 collective-permute-start.6
  12.5 1.8 %collective-permute-start.7 = (bf16[64,512]{1,0:T(8,128)(2,1)S(1)}, bf16[64,512]{1,0:T(8,128)(2,1)S(1)}, u32[]{:S(2)}, u32[]{:S(2)}) collective-permute-start(bf16[64,512]{1,0:T(8,128)(2,1)S(1)} %edges.1), channel_id=1, source_target_pairs={{0,2},{1,3},{2,4},{3,5},{4,6},{5,7},{6,0},{7,1},{8,10},{9,11},{10,... | collective-permute-start | bytes 196616 | tf_op jit(solution)/shard_map/ppermute | solution.py:282
  14.3 0.0 collective-permute-done.6.refs_7_
  14.3 3.1 %plane_inner.1 = (f32[64,512]{1,0:T(8,128)S(1)}, bf16[512,512]{1,0:T(8,128)(2,1)S(1)}, bf16[3,18,32,512]{3,2,1,0:T(8,128)(2,1)S(1)}, bf16[3,18,32,512]{3,2,1,0:T(8,128)(2,1)S(1)}) custom-call(bf16[128,512]{1,0:T(8,128)(2,1)S(1)} %lines.1.refs_0_, bf16[128,512]{1,0:T(8,128)(2,1)S(1)} %collective-permute-done.refs_1_, ...), custom_call_target="tpu_custom_call" | custom-call | flops 5000000000 | bytes 15000000 | tf_op jit(solution)/shard_map/plane_inner/pallas_call | solution.py:297
  17.4 0.0 copy-start.1
  17.4 0.1 first_lines.1.__
  17.5 1.5 %collective-permute-done.7.lines = bf16[64,512]{1,0:T(8,128)(2,1)S(1)} collective-permute-done((bf16[64,512]{1,0:T(8,128)(2,1)S(1)}, bf16[64,512]{1,0:T(8,128)(2,1)S(1)}, u32[]{:S(2)}, u32[]{:S(2)}) %collective-permute-start.7) | collective-permute-done | bytes 65568 | tf_op jit(solution)/shard_map/ppermute | solution.py:282
  19.0 0.0 collective-permute-start.8
  19.0 2.0 %collective-permute-start.9 = (bf16[64,512]{1,0:T(8,128)(2,1)S(1)}, bf16[64,512]{1,0:T(8,128)(2,1)S(1)}, u32[]{:S(2)}, u32[]{:S(2)}) collective-permute-start(bf16[64,512]{1,0:T(8,128)(2,1)S(1)} %first_lines.1.__), channel_id=1, source_target_pairs={{0,6},{1,7},{2,0},{3,1},{4,2},{5,3},{6,4},{7,5},{8,14},{9,15},{10,... | collective-permute-start | bytes 196616 | tf_op jit(solution)/shard_map/ppermute | solution.py:293
  21.0 0.0 collective-permute-done.8.refs_1_
  21.1 1.8 %plane_gradient.1 = (bf16[3,2,32,512]{3,2,1,0:T(8,128)(2,1)S(1)}, bf16[3,2,32,512]{3,2,1,0:T(8,128)(2,1)S(1)}, f32[432,128]{1,0:T(8,128)S(1)}, bf16[432,128]{1,0...) custom-call(bf16[64,512]{1,0:T(8,128)(2,1)S(1)} %later.1.refs_0_, ...), custom_call_target="tpu_custom_call" | custom-call | tf_op jit(solution)/shard_map/plane_gradient/pallas_call | solution.py:317
  22.9 0.5 %collective-permute-start.10 = (bf16[432,128]{1,0:T(8,128)(2,1)S(1)}, bf16[432,128]{1,0:T(8,128)(2,1)S(1)}, u32[]{:S(2)}, u32[]{:S(2)}) collective-permute-start(bf16[432,128]{1,0:T(8,128)(2,1)S(1)} %get-tuple-element.24), channel_id=1, source_target_pairs={{0,4},{1,5},{2,6},{3,7},{4,0},{5,1},{6,2},{7,3},{8,12},{9,13},{10,... | collective-permute-start | bytes 331784 | tf_op jit(solution)/shard_map/ppermute | solution.py:333
  23.4 2.0 %collective-permute-start.11 = (bf16[432,128]{1,0:T(8,128)(2,1)S(1)}, bf16[432,128]{1,0:T(8,128)(2,1)S(1)}, u32[]{:S(2)}, u32[]{:S(2)}) collective-permute-start(bf16[432,128]{1,0:T(8,128)(2,1)S(1)} %get-tuple-element.25), channel_id=1, source_target_pairs={{0,6},{1,7},{2,0},{3,1},{4,2},{5,3},{6,4},{7,5},{8,14},{9,15},{10,... | collective-permute-start | bytes 331784 | tf_op jit(solution)/shard_map/ppermute | solution.py:333
  25.4 0.0 collective-permute-start.12
  25.4 0.0 collective-permute-done.9.after_ref
  25.4 4.7 %local_convolutions.1 = (bf16[8,8,512]{2,1,0:T(8,128)(2,1)S(1)}, bf16[8,8,512]{2,1,0:T(8,128)(2,1)S(1)}) custom-call(bf16[3,18,32,512]{3,2,1,0:T(8,128)(2,1)S(1)} %get-tuple-element.15.vol_ref, bf16[3,18,32,512]{3,2,1,0:T(8,128)(2,1)S(1)} %get-tuple-element.16.refs_4_.cot_ref, bf16[3,2,32,512]{3,2,1,0:T(8,128)(2,1)S(1)} %get-tuple-element.19.near_vol, ...), custom_call_target="tpu_custom_call" | custom-call | tf_op jit(solution)/shard_map/local_convolutions/pallas_call | solution.py:337
  30.1 0.8 %copy_bitcast_fusion = (bf16[8,8,2,256]{3,2,1,0:T(2,128)(2,1)}, bf16[8,8,2,256]{3,2,1,0:T(2,128)(2,1)}) fusion(bf16[8,8,2,256]{3,1,2,0:T(8,128)(2,1)S(1)} %bitcast.11, bf16[8,8,2,256]{3,1,2,0:T(8,128)(2,1)S(1)} %bitcast.10), kind=kLoop, calls=%fused_computation.2 | loop fusion | bytes 262144 | tf_op jit(solution)/shard_map/transpose | solution.py:355
  30.9 0.9 %collective-permute-done.10 = bf16[432,128]{1,0:T(8,128)(2,1)S(1)} collective-permute-done((bf16[432,128]{1,0:T(8,128)(2,1)S(1)}, bf16[432,128]{1,0:T(8,128)(2,1)S(1)}, u32[]{:S(2)}, u32[]{:S(2)}) %collective-permute-start.10) | collective-permute-done | bytes 110624 | tf_op jit(solution)/shard_map/ppermute | solution.py:333
  31.7 0.0 collective-permute-done.11
  31.7 1.6 %collective-permute-done.12 = bf16[432,128]{1,0:T(8,128)(2,1)S(1)} collective-permute-done((bf16[432,128]{1,0:T(8,128)(2,1)S(1)}, bf16[432,128]{1,0:T(8,128)(2,1)S(1)}, u32[]{:S(2)}, u32[]{:S(2)}) %collective-permute-start.12) | collective-permute-done | bytes 110624 | tf_op jit(solution)/shard_map/ppermute | solution.py:333
  33.4 0.7 %add_bitcast_fusion = f32[55296]{0:T(1024)} fusion(bf16[432,128]{1,0:T(8,128)(2,1)S(1)} %collective-permute-done.12, bf16[432,128]{1,0:T(8,128)(2,1)S(1)} %collective-permute-done.11, f32[432,128]{1,0:T(8,128)S(1)} %get-tuple-element.23, bf16[432,128]{1,0:T(8,128)(2,1)S(1)} %collective-permute-done.10), kind=kLoop, calls=%fused_computation | loop fusion | flops 331776 | bytes 774144 | tf_op jit(solution)/shard_map/reshape | solution.py:360
  (8 shorter events, 0.0 us)
Async XLA Ops:
  1.8 12.4 %copy-start = (bf16[6912,256]{1,0:T(8,128)(2,1)S(1)}, bf16[6912,256]{1,0:T(8,128)(2,1)}, u32[]{:S(2)}) copy-start(bf16[6912,256]{1,0:T(8,128)(2,1)} %w1.1) | copy-start | bytes 10616836
  1.8 6.5 %collective-permute-start = (bf16[128,512]{1,0:T(8,128)(2,1)S(1)}, bf16[128,512]{1,0:T(8,128)(2,1)S(1)}, u32[]{:S(2)}, u32[]{:S(2)}) collective-permute-start(bf16[128,512]{1,0:T(8,128)(2,1)S(1)} %lines.1.refs_0_), channel_id=1, source_target_pairs={{0,1},{1,0},{2,3},{3,2},{4,5},{5,4},{6,7},{7,6},{8,9},{9,8},{10,11... | collective-permute-start | bytes 393224 | tf_op jit(solution)/shard_map/ppermute | solution.py:271
  4.9 6.4 %collective-permute-start.1 = (bf16[128,512]{1,0:T(8,128)(2,1)S(1)}, bf16[128,512]{1,0:T(8,128)(2,1)S(1)}, u32[]{:S(2)}, u32[]{:S(2)}) collective-permute-start(bf16[128,512]{1,0:T(8,128)(2,1)S(1)} %lines.1.refs_0_), channel_id=1, source_target_pairs={{0,16},{1,17},{2,18},{3,19},{4,20},{5,21},{6,22},{7,23},{8,24},{9,... | collective-permute-start | bytes 393224 | tf_op jit(solution)/shard_map/ppermute | solution.py:271
  6.4 6.1 %collective-permute-start.2 = (bf16[128,512]{1,0:T(8,128)(2,1)S(1)}, bf16[128,512]{1,0:T(8,128)(2,1)S(1)}, u32[]{:S(2)}, u32[]{:S(2)}) collective-permute-start(bf16[128,512]{1,0:T(8,128)(2,1)S(1)} %lines.1.refs_0_), channel_id=1, source_target_pairs={{0,17},{1,16},{2,19},{3,18},{4,21},{5,20},{6,23},{7,22},{8,25},{9,... | collective-permute-start | bytes 393224 | tf_op jit(solution)/shard_map/ppermute | solution.py:271
  6.4 7.8 %collective-permute-start.3 = (bf16[128,512]{1,0:T(8,128)(2,1)S(1)}, bf16[128,512]{1,0:T(8,128)(2,1)S(1)}, u32[]{:S(2)}, u32[]{:S(2)}) collective-permute-start(bf16[128,512]{1,0:T(8,128)(2,1)S(1)} %lines.1.refs_0_), channel_id=1, source_target_pairs={{0,8},{1,9},{2,10},{3,11},{4,12},{5,13},{6,14},{7,15},{8,0},{9,1},... | collective-permute-start | bytes 393224 | tf_op jit(solution)/shard_map/ppermute | solution.py:255
  8.4 5.9 %collective-permute-start.4 = (bf16[128,512]{1,0:T(8,128)(2,1)S(1)}, bf16[128,512]{1,0:T(8,128)(2,1)S(1)}, u32[]{:S(2)}, u32[]{:S(2)}) collective-permute-start(bf16[128,512]{1,0:T(8,128)(2,1)S(1)} %collective-permute-done.refs_1_), channel_id=1, source_target_pairs={{0,8},{1,9},{2,10},{3,11},{4,12},{5,13},{6,14},{7,15},{8,0},{9,1},... | collective-permute-start | bytes 393224 | tf_op jit(solution)/shard_map/ppermute | solution.py:255
  11.2 3.0 %collective-permute-start.5 = (bf16[128,512]{1,0:T(8,128)(2,1)S(1)}, bf16[128,512]{1,0:T(8,128)(2,1)S(1)}, u32[]{:S(2)}, u32[]{:S(2)}) collective-permute-start(bf16[128,512]{1,0:T(8,128)(2,1)S(1)} %collective-permute-done.1.refs_2_), channel_id=1, source_target_pairs={{0,8},{1,9},{2,10},{3,11},{4,12},{5,13},{6,14},{7,15},{8,0},{9,1},... | collective-permute-start | bytes 393224 | tf_op jit(solution)/shard_map/ppermute | solution.py:255
  12.4 1.8 %collective-permute-start.6 = (bf16[128,512]{1,0:T(8,128)(2,1)S(1)}, bf16[128,512]{1,0:T(8,128)(2,1)S(1)}, u32[]{:S(2)}, u32[]{:S(2)}) collective-permute-start(bf16[128,512]{1,0:T(8,128)(2,1)S(1)} %collective-permute-done.2.refs_3_), channel_id=1, source_target_pairs={{0,8},{1,9},{2,10},{3,11},{4,12},{5,13},{6,14},{7,15},{8,0},{9,1},... | collective-permute-start | bytes 393224 | tf_op jit(solution)/shard_map/ppermute | solution.py:255
  12.5 6.6 %collective-permute-start.7 = (bf16[64,512]{1,0:T(8,128)(2,1)S(1)}, bf16[64,512]{1,0:T(8,128)(2,1)S(1)}, u32[]{:S(2)}, u32[]{:S(2)}) collective-permute-start(bf16[64,512]{1,0:T(8,128)(2,1)S(1)} %edges.1), channel_id=1, source_target_pairs={{0,2},{1,3},{2,4},{3,5},{4,6},{5,7},{6,0},{7,1},{8,10},{9,11},{10,... | collective-permute-start | bytes 196616 | tf_op jit(solution)/shard_map/ppermute | solution.py:282
  17.4 8.0 %copy-start.1 = (bf16[6912,256]{1,0:T(8,128)(2,1)S(1)}, bf16[6912,256]{1,0:T(8,128)(2,1)}, u32[]{:S(2)}) copy-start(bf16[6912,256]{1,0:T(8,128)(2,1)} %w2.1) | copy-start | bytes 10616836
  19.0 2.0 %collective-permute-start.8 = (bf16[64,512]{1,0:T(8,128)(2,1)S(1)}, bf16[64,512]{1,0:T(8,128)(2,1)S(1)}, u32[]{:S(2)}, u32[]{:S(2)}) collective-permute-start(bf16[64,512]{1,0:T(8,128)(2,1)S(1)} %later.1.refs_0_), channel_id=1, source_target_pairs={{0,8},{1,9},{2,10},{3,11},{4,12},{5,13},{6,14},{7,15},{8,0},{9,1},... | collective-permute-start | bytes 196616 | tf_op jit(solution)/shard_map/ppermute | solution.py:255
  19.0 6.4 %collective-permute-start.9 = (bf16[64,512]{1,0:T(8,128)(2,1)S(1)}, bf16[64,512]{1,0:T(8,128)(2,1)S(1)}, u32[]{:S(2)}, u32[]{:S(2)}) collective-permute-start(bf16[64,512]{1,0:T(8,128)(2,1)S(1)} %first_lines.1.__), channel_id=1, source_target_pairs={{0,6},{1,7},{2,0},{3,1},{4,2},{5,3},{6,4},{7,5},{8,14},{9,15},{10,... | collective-permute-start | bytes 196616 | tf_op jit(solution)/shard_map/ppermute | solution.py:293
  22.9 8.8 %collective-permute-start.10 = (bf16[432,128]{1,0:T(8,128)(2,1)S(1)}, bf16[432,128]{1,0:T(8,128)(2,1)S(1)}, u32[]{:S(2)}, u32[]{:S(2)}) collective-permute-start(bf16[432,128]{1,0:T(8,128)(2,1)S(1)} %get-tuple-element.24), channel_id=1, source_target_pairs={{0,4},{1,5},{2,6},{3,7},{4,0},{5,1},{6,2},{7,3},{8,12},{9,13},{10,... | collective-permute-start | bytes 331784 | tf_op jit(solution)/shard_map/ppermute | solution.py:333
  23.4 8.3 %collective-permute-start.11 = (bf16[432,128]{1,0:T(8,128)(2,1)S(1)}, bf16[432,128]{1,0:T(8,128)(2,1)S(1)}, u32[]{:S(2)}, u32[]{:S(2)}) collective-permute-start(bf16[432,128]{1,0:T(8,128)(2,1)S(1)} %get-tuple-element.25), channel_id=1, source_target_pairs={{0,6},{1,7},{2,0},{3,1},{4,2},{5,3},{6,4},{7,5},{8,14},{9,15},{10,... | collective-permute-start | bytes 331784 | tf_op jit(solution)/shard_map/ppermute | solution.py:333
  25.4 8.0 %collective-permute-start.12 = (bf16[432,128]{1,0:T(8,128)(2,1)S(1)}, bf16[432,128]{1,0:T(8,128)(2,1)S(1)}, u32[]{:S(2)}, u32[]{:S(2)}) collective-permute-start(bf16[432,128]{1,0:T(8,128)(2,1)S(1)} %get-tuple-element.26), channel_id=1, source_target_pairs={{0,2},{1,3},{2,4},{3,5},{4,6},{5,7},{6,0},{7,1},{8,10},{9,11},{10,... | collective-permute-start | bytes 331784 | tf_op jit(solution)/shard_map/ppermute | solution.py:333
